TPU v7x, 32 devices: a whole 2x2x4 slice. The times are simulated.
32 devices in a mesh: tok: 4 (over y, x), cent: 8 (over z, core).
Axes of the slice: x: 2, y: 2, z: 4, core: 2. Of those that a mesh axis runs over, the one named last changes fastest.
Arguments:
- tokens: bfloat16 [8192, 128], P('tok'), may hold values from -80 to 80
- centroids: bfloat16 [262144, 128], P('cent'), may hold values from -0.6 to 0.6
Outputs:
- updated: float32 [262144, 128], P('cent')
- masses: float32 [262144], P('cent')
All inputs are finite; a program needn't handle non-finite values.
Results may differ from a plain program's by a relative error of at most 0.0028.
Values may be sent and summed in bfloat16 or wider, within the bound.
No kernel may reach another device: no remote copies, remote signals or barrier semaphores. Data moves between devices by JAX's collectives and lax.ppermute only.
A program may use at most 128 MiB of HBM per device.

v0:
```python
import functools

import jax
import jax.numpy as jnp
import numpy as np
from jax import lax
from jax.experimental import pallas as pl
from jax.experimental.pallas import tpu as pltpu
from jax.sharding import PartitionSpec as P

inverse_temp = 2.0
prior_weight = 0.05
safe_sum = 1e30
headroom = 60.0
code_scale = 2.0**24
slice_rows = 64
vmem_bytes = 56 * 1024 * 1024


def divisor(count, most):
    size = min(count, most)
    while count % size:
        size //= 2
    return size


def dot_nt(a, b):
    return lax.dot_general(a, b, (((1,), (1,)), ((), ())), preferred_element_type=jnp.float32)


def fold_rows(x, combine):
    parts = [x[k * 8 : (k + 1) * 8, :] for k in range(x.shape[0] // 8)]
    while len(parts) > 1:
        half = len(parts) // 2
        parts = [combine(parts[2 * k], parts[2 * k + 1]) for k in range(half)] + parts[2 * half :]
    return parts[0]


def split_exactly(x):
    high = x.astype(jnp.bfloat16).astype(jnp.float32)
    middle = (x - high).astype(jnp.bfloat16).astype(jnp.float32)
    return high, middle, x - high - middle


def stats_kernel(
    sub_rows, tok_cols, tok_ref, cent_ref, out_ref, flip_ref, base_ref, shift_ref, sums_ref, worst_ref
):
    step = pl.program_id(0)
    tok_count = tok_ref.shape[0]
    subs = cent_ref.shape[0] // sub_rows
    col_blocks = tok_count // tok_cols
    redo_cols = divisor(tok_cols, 256)
    redo_blocks = tok_count // redo_cols

    def columns(t, size=tok_cols):
        return pl.ds(pl.multiple_of(t * size, size), size)

    def dot(a, b):
        return jnp.dot(a, b, preferred_element_type=jnp.float32)

    width = tok_ref.shape[1]

    @pl.when(step == 0)
    def _():
        @pl.loop(0, col_blocks)
        def _(t):
            flipped = (tok_ref[columns(t), :] * jnp.bfloat16(inverse_temp)).T
            flip_ref[0:width, columns(t)] = flipped
            logits = dot(cent_ref[0:128, :], flipped)
            top = jnp.max(fold_rows(logits, jnp.maximum), axis=0, keepdims=True)
            base = top + headroom
            base_ref[:, columns(t)] = base
            row = lax.broadcasted_iota(jnp.int32, (width, tok_cols), 0)
            terms = jnp.zeros((width, tok_cols), jnp.float32)
            for k, term in enumerate(split_exactly(-base)):
                terms = jnp.where(row == k, term, terms)
            flip_ref[width:, columns(t)] = terms.astype(jnp.bfloat16)

    lane = lax.broadcasted_iota(jnp.int32, (sub_rows, width), 1)
    ones = jnp.where(lane < 3, 1.0, 0.0).astype(jnp.bfloat16)

    @pl.loop(0, col_blocks)
    def _(t):
        rhs = flip_ref[:, columns(t)]
        shift = base_ref[:, columns(t)]
        for sub in range(subs):
            total = jnp.zeros((8, tok_cols), jnp.float32)
            lhs = jnp.concatenate([cent_ref[pl.ds(sub * sub_rows, sub_rows), :], ones], axis=1)
            logits = dot(lhs, rhs)
            for first in range(0, sub_rows, slice_rows):
                scaled = jnp.exp(logits[first : first + slice_rows])
                total = total + fold_rows(scaled, jnp.add)
            sums_ref[step * subs + sub, :, columns(t)] = total
            shift_ref[step * subs + sub, :, columns(t)] = shift

    worst = jnp.float32(0.0)
    for sub in range(subs):
        for t in range(redo_blocks):
            block = jnp.max(sums_ref[step * subs + sub, :, t * redo_cols : (t + 1) * redo_cols])
            worst_ref[sub * redo_blocks + t] = block
            worst = jnp.maximum(worst, block)

    @pl.when(jnp.logical_not(worst < safe_sum))
    def _():
        @pl.loop(0, subs * redo_blocks)
        def _(k):
            @pl.when(jnp.logical_not(worst_ref[k] < safe_sum))
            def _():
                sub, t = k // redo_blocks, lax.rem(k, redo_blocks)
                first = pl.multiple_of(sub * sub_rows, sub_rows)
                rhs = flip_ref[0:width, columns(t, redo_cols)]
                logits = dot(cent_ref[pl.ds(first, sub_rows), :], rhs)
                top = jnp.max(fold_rows(logits, jnp.maximum), axis=0, keepdims=True)
                total = fold_rows(jnp.exp(logits - top), jnp.add)
                sums_ref[step * subs + sub, :, columns(t, redo_cols)] = total
                shift_ref[step * subs + sub, :, columns(t, redo_cols)] = top

    @pl.when(step == pl.num_programs(0) - 1)
    def _():
        @pl.loop(0, col_blocks)
        def _(t):
            shifts = shift_ref[:, :, columns(t)]
            top = jnp.max(shifts, axis=0)
            scale = jnp.exp(shifts - top[None])
            total = jnp.sum(sums_ref[:, :, columns(t)] * scale, axis=0)
            total = jnp.sum(total, axis=0, keepdims=True)
            out_ref[:, :, columns(t)] = jnp.broadcast_to(
                (top + jnp.log(total))[None], (out_ref.shape[0], 1, tok_cols)
            )


def local_lse(tokens, centroids, copies):
    tok_count, width = tokens.shape
    cent_count = centroids.shape[0]
    block_rows = divisor(cent_count, 4096)
    sub_rows = divisor(block_rows, 1024)
    tok_cols = divisor(tok_count, 512)
    blocks = cent_count // block_rows
    subs = cent_count // sub_rows
    flags = block_rows // sub_rows * (tok_count // divisor(tok_cols, 256))
    return pl.pallas_call(
        functools.partial(stats_kernel, sub_rows, tok_cols),
        grid=(blocks,),
        in_specs=[
            pl.BlockSpec((tok_count, width), lambda j: (0, 0)),
            pl.BlockSpec((block_rows, width), lambda j: (j, 0)),
        ],
        out_specs=pl.BlockSpec((copies, 1, tok_count), lambda j: (0, 0, 0)),
        out_shape=jax.ShapeDtypeStruct((copies, 1, tok_count), jnp.float32),
        scratch_shapes=[
            pltpu.VMEM((2 * width, tok_count), jnp.bfloat16),
            pltpu.VMEM((1, tok_count), jnp.float32),
            pltpu.VMEM((subs, 1, tok_count), jnp.float32),
            pltpu.VMEM((subs, 8, tok_count), jnp.float32),
            pltpu.SMEM((flags,), jnp.float32),
        ],
        compiler_params=pltpu.CompilerParams(vmem_limit_bytes=vmem_bytes),
        cost_estimate=pl.CostEstimate(
            flops=2 * tok_count * cent_count * width,
            bytes_accessed=(tok_count + cent_count) * width * 2,
            transcendentals=tok_count * cent_count,
        ),
        name="row_stats",
    )(tokens, centroids)


def encoded(x):
    x = x * code_scale
    return (x * jnp.abs(x) * (x * x)).astype(jnp.bfloat16)


def decoded(code):
    code = code.astype(jnp.float32)
    size = lax.rsqrt(lax.rsqrt(jnp.maximum(jnp.abs(code), 1e-37))) * (1.0 / code_scale)
    return jnp.where(code < 0, -size, jnp.where(code > 0, size, 0.0))


class Placing:
    def __init__(self, block_rows, table_ref, chunk, pieces, code_refs, outs, scratch):
        self.block_rows, self.table_ref, self.chunk = block_rows, table_ref, chunk
        self.pieces, self.code_refs = pieces, code_refs
        self.updated_ref, self.masses_ref = outs
        self.codes, self.values, self.masses, self.sems = scratch

    @staticmethod
    def scratch(sources, blocks, block_rows, width):
        return [
            pltpu.VMEM((sources, blocks * coded_rows(block_rows), width), jnp.bfloat16),
            pltpu.VMEM((sources, blocks * block_rows, width), jnp.float32),
            pltpu.VMEM((sources, blocks * block_rows // 128, 128), jnp.float32),
            pltpu.SemaphoreType.DMA((4, sources)),
        ]

    def copies_in(self):
        found, refs = [], list(self.code_refs)
        for s, count in enumerate(self.pieces):
            found.append([])
            first = 0
            for k in range(count):
                ref = refs.pop(0)
                target = self.codes.at[s, pl.ds(first, ref.shape[0]), :]
                found[s].append(pltpu.make_async_copy(ref, target, self.sems.at[3 * k, s]))
                first += ref.shape[0]
        return found

    def copies_out(self, s):
        rows, mass_rows = self.values.shape[1], self.masses.shape[1]
        start = self.table_ref[self.chunk, s]
        span = pl.ds(pl.multiple_of(start * self.block_rows, self.block_rows), rows)
        per_block = self.block_rows // 128
        mass_span = pl.ds(pl.multiple_of(start * per_block, per_block), mass_rows)
        return [
            pltpu.make_async_copy(self.values.at[s], self.updated_ref.at[span, :], self.sems.at[1, s]),
            pltpu.make_async_copy(self.masses.at[s], self.masses_ref.at[mass_span, :], self.sems.at[2, s]),
        ]

    def fetch(self):
        for copies in self.copies_in():
            for copy in copies:
                copy.start()

    def place(self):
        block_rows, per_block = self.block_rows, self.block_rows // 128
        full = coded_rows(block_rows)
        tile = divisor(block_rows, 256)
        for s, copies in enumerate(self.copies_in()):
            for copy in copies:
                copy.wait()

            @pl.loop(0, self.values.shape[1] // block_rows)
            def _(b):
                for k in range(block_rows // tile):
                    source = pl.ds(pl.multiple_of(b * full + k * tile, 32), tile)
                    target = pl.ds(pl.multiple_of(b * block_rows + k * tile, tile), tile)
                    self.values[s, target, :] = decoded(self.codes[s, source, :])
                last = pl.ds(pl.multiple_of(b * full + block_rows, 32), full - block_rows)
                terms = self.codes[s, last, :].astype(jnp.float32)
                mass = terms[:per_block] + terms[per_block : 2 * per_block]
                mass = mass + terms[2 * per_block : 3 * per_block]
                self.masses[s, pl.ds(pl.multiple_of(b * per_block, per_block), per_block), :] = mass

            for copy in self.copies_out(s):
                copy.start()

    def finish(self):
        for s in range(len(self.pieces)):
            for copy in self.copies_out(s):
                copy.wait()


def coded_rows(block_rows):
    return block_rows + block_rows // 32


def combine(groups, parts_ref, out_ref):
    per_group = parts_ref.shape[0] // groups
    count = parts_ref.shape[2]
    for t in range(groups):
        parts = [parts_ref[t * per_group + k] for k in range(per_group)]
        top = functools.reduce(jnp.maximum, parts)
        total = functools.reduce(jnp.add, [jnp.exp(part - top) for part in parts])
        out_ref[:, t * count : (t + 1) * count] = top + jnp.log(total)


def update_kernel(joins, unread, placed_chunk, pieces, block_rows, *refs):
    table_ref, tok_ref, lse_ref, cent_ref = refs[:4]
    refs = refs[4 + unread :]
    code_refs, refs = refs[: sum(pieces)], refs[sum(pieces) :]
    if pieces:
        code_ref, updated_ref, masses_ref = refs[2:5]
        scratch = refs[5:]
        outs = updated_ref, masses_ref
        placing = Placing(block_rows, table_ref, placed_chunk, pieces, code_refs, outs, scratch[3:])
    else:
        code_ref, scratch, placing = refs[0], refs[1:], None
    if joins:
        parts_ref, lse_ref, scratch = lse_ref, scratch[0], scratch[1:]
        pl.when(pl.program_id(0) == 0)(lambda: combine(joins, parts_ref, lse_ref))
    weights_ref, total_ref, mass_ref = scratch[:3]
    step, steps = pl.program_id(0), pl.num_programs(0)
    width = tok_ref.shape[1]
    _, tile, depth = weights_ref.shape
    piece = divisor(depth, 512)
    stages = tok_ref.shape[0] // depth
    tiles = block_rows // tile

    if placing:
        pl.when(step == 0)(placing.fetch)

    def weigh(first, stage):
        cents = cent_ref[pl.ds(first, tile), :] * jnp.bfloat16(inverse_temp)
        for k in range(depth // piece):
            span = pl.ds(stage * depth + k * piece, piece)
            logits = dot_nt(cents, tok_ref[span, :])
            lse = lse_ref[:, span]
            for r in range(0, tile, slice_rows):
                weights = jnp.exp(logits[r : r + slice_rows] - lse).astype(jnp.bfloat16)
                weights_ref[stage % 2, r : r + slice_rows, pl.ds(k * piece, piece)] = weights

    def gather_up(stage):
        toks = tok_ref[pl.ds(stage * depth, depth), :]
        rhs = jnp.concatenate([toks, jnp.ones_like(toks)], axis=1)
        part = jnp.dot(weights_ref[stage % 2], rhs, preferred_element_type=jnp.float32)
        if stage == 0:
            total_ref[...] = part
        else:
            total_ref[...] += part

    diagonal = lax.broadcasted_iota(jnp.int32, (128, 128), 0) == lax.broadcasted_iota(
        jnp.int32, (128, 128), 1
    )

    def run(r):
        first = pl.multiple_of(r * tile, tile)
        weigh(first, 0)
        for stage in range(1, stages):
            weigh(first, stage)
            gather_up(stage - 1)
        gather_up(stages - 1)
        mass = total_ref[:, width : 2 * width]
        prior = prior_weight * cent_ref[pl.ds(first, tile), :].astype(jnp.float32)
        new = (total_ref[:, 0:width] + prior) / (mass + prior_weight)
        code_ref[pl.ds(first, tile), :] = encoded(new)
        for k in range(tile // 128):
            square = jnp.where(diagonal, mass[k * 128 : (k + 1) * 128, :], 0.0)
            mass_ref[pl.ds(r * (tile // 128) + k, 1), :] = jnp.sum(square, axis=0, keepdims=True)

    pl.loop(0, tiles // 2)(run)
    if placing:
        pl.when(step == 0)(placing.place)
    pl.loop(tiles // 2, tiles)(run)

    terms = split_exactly(mass_ref[...])
    terms = jnp.concatenate([*terms, jnp.zeros_like(terms[0])], axis=0)
    code_ref[block_rows : block_rows + terms.shape[0], :] = terms.astype(jnp.bfloat16)
    if placing:
        pl.when(step == steps - 1)(placing.finish)


def updated_chunk(
    table, chunk, toks, lse, centroids, blocks, block_rows, after=(), received=None, joins=0
):
    all_count, width = toks.shape
    depth = divisor(all_count, 2048)
    tile = divisor(block_rows, 1024)
    rows = blocks * block_rows
    full = coded_rows(block_rows)
    anywhere = pl.BlockSpec(memory_space=pl.ANY)
    whole = lambda j, place: (0, 0)
    operands = [
        toks,
        lse,
        pltpu.with_memory_space_constraint(centroids, pltpu.HBM),
        *after,
    ]
    in_specs = [
        pl.BlockSpec((all_count, width), whole),
        pl.BlockSpec(lse.shape, (lambda j, place: (0, 0, 0)) if joins else whole),
        pl.BlockSpec((block_rows, width), lambda j, table: (table[chunk, 0] + j, 0)),
    ] + [anywhere] * len(after)
    out_specs = [pl.BlockSpec((full, width), lambda j, place: (j, 0))]
    out_shape = [jax.ShapeDtypeStruct((blocks * full, width), jnp.bfloat16)]
    scratch_shapes = [
        pltpu.VMEM((2, tile, depth), jnp.bfloat16),
        pltpu.VMEM((tile, 2 * width), jnp.float32),
        pltpu.VMEM((block_rows // 128, 128), jnp.float32),
    ]
    aliases, pieces, placed_chunk = {}, [], None
    if joins:
        out_specs.append(pl.BlockSpec((1, all_count), whole))
        out_shape.append(jax.ShapeDtypeStruct((1, all_count), jnp.float32))
    if received:
        placed_chunk, codes, outs = received
        pieces = [len(parts) for parts in codes]
        operands += [*sum(codes, []), *outs]
        in_specs += [anywhere] * (sum(pieces) + 2)
        out_specs += [anywhere] * 2
        out_shape += [jax.ShapeDtypeStruct(out.shape, out.dtype) for out in outs]
        aliases = {len(operands) - 1: 1, len(operands): 2}
        scratch_shapes += Placing.scratch(len(codes), codes[0][0].shape[0] // full, block_rows, width)
    return pl.pallas_call(
        functools.partial(update_kernel, joins, len(after), placed_chunk, pieces, block_rows),
        grid_spec=pltpu.PrefetchScalarGridSpec(
            num_scalar_prefetch=1,
            grid=(blocks,),
            in_specs=in_specs,
            out_specs=out_specs,
            scratch_shapes=scratch_shapes,
        ),
        out_shape=out_shape,
        input_output_aliases=aliases,
        compiler_params=pltpu.CompilerParams(vmem_limit_bytes=vmem_bytes * 3 // 4),
        cost_estimate=pl.CostEstimate(
            flops=6 * all_count * rows * width // 8,
            bytes_accessed=(2 * all_count + 4 * rows) * width // 8,
            transcendentals=all_count * rows // 8,
        ),
        name="new_rows",
    )(table, *operands)


def place_kernel(chunks, block_rows, table_ref, *refs):
    count = sum(sum(pieces) for _, pieces in chunks)
    code_refs, outs, scratch = refs[:count], refs[count + 2 : count + 4], refs[count + 4 :]
    placings = []
    for chunk, pieces in chunks:
        used = code_refs[: sum(pieces)]
        placings.append(Placing(block_rows, table_ref, chunk, pieces, used, outs, scratch[:4]))
        code_refs, scratch = code_refs[sum(pieces) :], scratch[4:]
    for placing in placings:
        placing.fetch()
    for placing in placings:
        placing.place()
    for placing in placings:
        placing.finish()


def placed(table, received, outs, block_rows):
    operands, chunks, scratch_shapes = [], [], []
    for chunk, codes in received:
        chunks.append((chunk, [len(parts) for parts in codes]))
        operands += sum(codes, [])
        rows, width = codes[0][0].shape
        blocks = rows // coded_rows(block_rows)
        scratch_shapes += Placing.scratch(len(codes), blocks, block_rows, width)
    anywhere = pl.BlockSpec(memory_space=pl.ANY)
    return pl.pallas_call(
        functools.partial(place_kernel, chunks, block_rows),
        grid_spec=pltpu.PrefetchScalarGridSpec(
            num_scalar_prefetch=1,
            grid=(1,),
            in_specs=[anywhere] * (len(operands) + 2),
            out_specs=[anywhere] * 2,
            scratch_shapes=scratch_shapes,
        ),
        out_shape=[jax.ShapeDtypeStruct(out.shape, out.dtype) for out in outs],
        input_output_aliases={1 + len(operands): 0, 2 + len(operands): 1},
        compiler_params=pltpu.CompilerParams(vmem_limit_bytes=vmem_bytes // 2),
        name="placed_rows",
    )(table, *operands, *outs)


def blank(shape):
    return pl.pallas_call(
        lambda out_ref: None,
        out_specs=pl.BlockSpec(memory_space=pl.ANY),
        out_shape=jax.ShapeDtypeStruct(shape, jnp.float32),
        name="blank",
    )()


def from_others(value, axis):
    size = lax.axis_size(axis)
    found = [value]
    for s in range(1, size):
        pairs = [(partner(k, s, size), k) for k in range(size)]
        found.append(lax.ppermute(value, axis, pairs))
    return found


def partner(me, s, size):
    return me ^ s if size & (size - 1) == 0 else (me - s) % size


def chunk_plan(blocks):
    plan = []
    while blocks > 2:
        plan.append(2)
        blocks -= 2
    return plan + [1] * blocks


def local(tokens, centroids):
    tok_size, cent_size = lax.axis_size("tok"), lax.axis_size("cent")
    me = lax.axis_index("tok")
    cent_count, width = centroids.shape
    share_rows = cent_count // tok_size

    toks = lax.all_gather(tokens, "tok", axis=0, tiled=True)
    own_lse = local_lse(tokens, centroids, tok_size * cent_size)
    parts = lax.all_to_all(own_lse, ("tok", "cent"), 0, 0, tiled=True)

    block_rows = divisor(share_rows, 1024)
    plan = chunk_plan(share_rows // block_rows)
    sources = jnp.stack([partner(me, s, tok_size) for s in range(tok_size)])[None, :]
    starts = np.cumsum([0] + plan[:-1])[:, None] * tok_size
    table = (starts + sources * np.array(plan)[:, None]).astype(jnp.int32)
    outs = blank((cent_count, width)), blank((cent_count // 128, 128))
    waiting = []
    for k, blocks in enumerate(plan):
        arrived, received = [], None
        if len(waiting) > 1:
            arrived = sum(waiting[-2][1][1:], [])
            if blocks == 1:
                received = (*waiting.pop(0), outs)
                arrived = arrived[:1] if k + 1 == len(plan) else arrived
        operands = toks, lse if k else parts, centroids, blocks, block_rows, arrived, received
        codes, *rest = updated_chunk(table, k, *operands, joins=0 if k else tok_size)
        if not k:
            (lse,) = rest
        elif received:
            outs = rest
        waiting.append((k, [[part] for part in from_others(codes, "tok")]))
    if len(waiting) > 1:
        outs = placed(table, waiting[:-1], outs, block_rows)
    outs = placed(table, waiting[-1:], outs, block_rows)
    return outs[0], outs[1].reshape(cent_count)


def solution(mesh):
    placed_as = (P("tok", None), P("cent", None))
    return jax.shard_map(
        local, mesh=mesh, in_specs=placed_as, out_specs=(P("cent", None), P("cent")), check_vma=False
    )
```

profile of v0, /device:TPU:0, one launch (start us, length us, event | category | flops | bytes accessed | tf_op | source)
XLA Modules:
  0.0 200.7 jit_solution(18150705563213150687)
XLA Ops:
  7.2 0.7 all-gather.2.cloned.1.call-update
  7.9 49.5 %row_stats.1 = f32[32,1,2048]{2,1,0:T(1,128)} custom-call(bf16[2048,128]{1,0:T(8,128)(2,1)} %tok_ref.1, bf16[32768,128]{1,0:T(8,128)(2,1)} %refs_3_.9), custom_call_target="tpu_custom_call" | custom-call | flops 17179869184 | bytes 8912896 | tf_op jit(solution)/shard_map/row_stats/pallas_call | solution.py:141
  57.4 3.9 %all-to-all-start = ((f32[32,1,2048]{2,1,0:T(1,128)}), f32[32,1,2048]{2,1,0:T(1,128)S(1)}, u32[]{:S(2)}, u32[]{:S(2)}) async-start(f32[32,1,2048]{2,1,0:T(1,128)} %row_stats.1), calls=%async_computation | async-start | bytes 524288 | tf_op jit(solution)/shard_map/all_to_all | solution.py:481
  61.5 10.2 %all-to-all-done.refs_2_ = f32[32,1,2048]{2,1,0:T(1,128)S(1)} async-done(((f32[32,1,2048]{2,1,0:T(1,128)}), f32[32,1,2048]{2,1,0:T(1,128)S(1)}, u32[]{:S(2)}, u32[]{:S(2)}) %all-to-all-start) | async-done | bytes 262176 | tf_op jit(solution)/shard_map/all_to_all | solution.py:481
  71.8 1.6 copy-done
  73.3 19.8 %new_rows.5 = (bf16[2112,128]{1,0:T(8,128)(2,1)S(1)}, f32[1,8192]{1,0:T(1,128)S(1)}) custom-call(s32[5,4]{1,0:T(8,128)S(1)} %multiply_add_fusion.refs_0_.table_ref, bf16[8192,128]{1,0:T(8,128)(2,1)S(1)} %copy-done, f32[32,1,2048]{2,1,0:T(1,128)S(1)} %all-to-all-done.refs_2_, bf16[32768,128]{1,0:T(8,128)(2,1)} %refs_3_.9), custom_call_target="tpu_custom_call" | custom-call | flops 1610612736 | bytes 393216 | tf_op jit(solution)/shard_map/new_rows/pallas_call | solution.py:381
  93.2 0.6 collective-permute-start
  93.7 0.8 collective-permute-start.1
  94.6 2.2 %collective-permute-start.2 = (bf16[2112,128]{1,0:T(8,128)(2,1)S(1)}, bf16[2112,128]{1,0:T(8,128)(2,1)S(1)}, u32[]{:S(2)}, u32[]{:S(2)}) collective-permute-start(bf16[2112,128]{1,0:T(8,128)(2,1)S(1)} %get-tuple-element.15.refs_7_), channel_id=1, source_target_pairs={{24,0},{16,8},{8,16},{0,24},{25,1},{17,9},{9,17},{1,25},{26,2},{18... | collective-permute-start | bytes 1622024 | tf_op jit(solution)/shard_map/ppermute | solution.py:457
  96.7 21.0 %new_rows.7.refs_5_ = bf16[2112,128]{1,0:T(8,128)(2,1)} custom-call(s32[5,4]{1,0:T(8,128)S(1)} %multiply_add_fusion.refs_0_.table_ref, bf16[8192,128]{1,0:T(8,128)(2,1)S(1)} %copy-done, f32[1,8192]{1,0:T(1,128)S(1)} %get-tuple-element.14.refs_2_, bf16[32768,128]{1,0:T(8,128)(2,1)} %refs_3_.9), custom_call_target="tpu_custom_call" | custom-call | flops 1610612736 | bytes 393216 | tf_op jit(solution)/shard_map/new_rows/pallas_call | solution.py:381
  117.7 0.5 collective-permute-start.4
  118.2 0.8 collective-permute-start.5
  119.1 2.2 %collective-permute-start.6 = (bf16[2112,128]{1,0:T(8,128)(2,1)}, bf16[2112,128]{1,0:T(8,128)(2,1)}, u32[]{:S(2)}, u32[]{:S(2)}) collective-permute-start(bf16[2112,128]{1,0:T(8,128)(2,1)} %new_rows.7.refs_5_), channel_id=1, source_target_pairs={{24,0},{16,8},{8,16},{0,24},{25,1},{17,9},{9,17},{1,25},{26,2},{18... | collective-permute-start | bytes 1622024 | tf_op jit(solution)/shard_map/ppermute | solution.py:457
  121.2 19.9 %new_rows.6.refs_0_ = bf16[2112,128]{1,0:T(8,128)(2,1)S(1)} custom-call(s32[5,4]{1,0:T(8,128)S(1)} %multiply_add_fusion.refs_0_.table_ref, bf16[8192,128]{1,0:T(8,128)(2,1)S(1)} %copy-done, f32[1,8192]{1,0:T(1,128)S(1)} %get-tuple-element.14.refs_2_, bf16[32768,128]{1,0:T(8,128)(2,1)} %refs_3_.9, bf16[2112,128]{1,0:T(8,128)(2,1)S(1)} %collective-permute-done.refs_4_.refs_8_, ...), custom_call_target="tpu_custom_call" | custom-call | flops 1610612736 | bytes 393216 | tf_op jit(solution)/shard_map/new_rows/pallas_call | solution.py:381
  141.2 0.5 collective-permute-start.3
  141.7 0.8 collective-permute-start.10
  142.6 2.2 %collective-permute-start.11 = (bf16[2112,128]{1,0:T(8,128)(2,1)S(1)}, bf16[2112,128]{1,0:T(8,128)(2,1)S(1)}, u32[]{:S(2)}, u32[]{:S(2)}) collective-permute-start(bf16[2112,128]{1,0:T(8,128)(2,1)S(1)} %new_rows.6.refs_0_), channel_id=1, source_target_pairs={{24,0},{16,8},{8,16},{0,24},{25,1},{17,9},{9,17},{1,25},{26,2},{18... | collective-permute-start | bytes 1622024 | tf_op jit(solution)/shard_map/ppermute | solution.py:457
  144.8 1.0 copy-done.3
  145.8 1.0 copy-done.5
  146.9 1.0 copy-done.7
  147.9 1.0 copy-done.9
  149.0 12.8 %new_rows.8 = (bf16[1056,128]{1,0:T(8,128)(2,1)S(1)}, f32[32768,128]{1,0:T(8,128)}, f32[256,128]{1,0:T(8,128)}) custom-call(s32[5,4]{1,0:T(8,128)S(1)} %multiply_add_fusion.refs_0_.table_ref, bf16[8192,128]{1,0:T(8,128)(2,1)S(1)} %copy-done.1, f32[1,8192]{1,0:T(1,128)S(1)} %get-tuple-element.14.refs_2_, ...), custom_call_target="tpu_custom_call", output_to_operand_aliasing={{1}: (11, {}), {2}: (12, {})} | custom-call | flops 805306368 | bytes 327680 | tf_op jit(solution)/shard_map/new_rows/pallas_call | solution.py:381
  161.8 0.9 collective-permute-start.12
  162.7 0.7 collective-permute-start.13
  163.4 1.9 collective-permute-start.14
  165.4 13.7 %new_rows.9 = (bf16[1056,128]{1,0:T(8,128)(2,1)S(1)}, f32[32768,128]{1,0:T(8,128)}, f32[256,128]{1,0:T(8,128)}) custom-call(s32[5,4]{1,0:T(8,128)S(1)} %multiply_add_fusion.refs_0_.table_ref, bf16[8192,128]{1,0:T(8,128)(2,1)S(1)} %copy-done.1, f32[1,8192]{1,0:T(1,128)S(1)} %get-tuple-element.14.refs_2_, ...), custom_call_target="tpu_custom_call", output_to_operand_aliasing={{1}: (9, {}), {2}: (10, {})} | custom-call | flops 805306368 | bytes 327680 | tf_op jit(solution)/shard_map/new_rows/pallas_call | solution.py:381
  179.1 0.9 collective-permute-start.7
  180.0 0.7 collective-permute-start.8
  180.7 1.9 collective-permute-start.9
  182.7 4.4 %placed_rows.2 = (f32[32768,128]{1,0:T(8,128)}, f32[256,128]{1,0:T(8,128)}) custom-call(s32[5,4]{1,0:T(8,128)S(1)} %multiply_add_fusion.refs_0_.table_ref, bf16[2112,128]{1,0:T(8,128)(2,1)S(1)} %new_rows.6.refs_0_, bf16[2112,128]{1,0:T(8,128)(2,1)S(1)} %collective-permute-done.3.refs_4_.refs_1_, ...), custom_call_target="tpu_custom_call", output_to_operand_aliasing={{0}: (9, {}), {1}: (10, {})} | custom-call | tf_op jit(solution)/shard_map/placed_rows/pallas_call | solution.py:427
  187.5 3.4 %collective-permute-done.8.refs_2_ = bf16[1056,128]{1,0:T(8,128)(2,1)S(1)} collective-permute-done((bf16[1056,128]{1,0:T(8,128)(2,1)S(1)}, bf16[1056,128]{1,0:T(8,128)(2,1)S(1)}, u32[]{:S(2)}, u32[]{:S(2)}) %collective-permute-start.8) | collective-permute-done | bytes 270368 | tf_op jit(solution)/shard_map/ppermute | solution.py:457
  191.0 2.4 %placed_rows.3 = (f32[32768,128]{1,0:T(8,128)}, f32[256,128]{1,0:T(8,128)}) custom-call(s32[5,4]{1,0:T(8,128)S(1)} %multiply_add_fusion.refs_0_.table_ref, bf16[1056,128]{1,0:T(8,128)(2,1)S(1)} %get-tuple-element.18.refs_0_, bf16[1056,128]{1,0:T(8,128)(2,1)S(1)} %collective-permute-done.7.refs_1_, ...), custom_call_target="tpu_custom_call", output_to_operand_aliasing={{0}: (5, {}), {1}: (6, {})} | custom-call | tf_op jit(solution)/shard_map/placed_rows/pallas_call | solution.py:427
  (39 shorter events, 0.7 us)
Async XLA Ops:
  7.2 64.6 %all-gather.2.cloned.1.call-start = ((), (), s32[]{:S(2)}) async-start(), calls=%async_computation.1 | async-start | bytes 2621440 | tf_op jit(solution)/shard_map/all_gather | solution.py:479
  7.9 53.6 %copy-start.10 = (s32[5]{0:T(128)S(1)}, s32[5]{0:T(128)}, u32[]{:S(2)}) copy-start(s32[5]{0:T(128)} %constant.17) | copy-start | bytes 64
  7.9 53.6 %copy-start.11 = (s32[5]{0:T(128)S(1)}, s32[5]{0:T(128)}, u32[]{:S(2)}) copy-start(s32[5]{0:T(128)} %constant.18) | copy-start | bytes 64
  57.4 14.3 %all-to-all-start = ((f32[32,1,2048]{2,1,0:T(1,128)}), f32[32,1,2048]{2,1,0:T(1,128)S(1)}, u32[]{:S(2)}, u32[]{:S(2)}) async-start(f32[32,1,2048]{2,1,0:T(1,128)} %row_stats.1), calls=%async_computation | async-start | bytes 524288 | tf_op jit(solution)/shard_map/all_to_all | solution.py:481
  71.7 1.6 copy-start
  93.2 48.0 %copy-start.8 = (bf16[2112,128]{1,0:T(8,128)(2,1)}, bf16[2112,128]{1,0:T(8,128)(2,1)S(1)}, u32[]{:S(2)}) copy-start(bf16[2112,128]{1,0:T(8,128)(2,1)S(1)} %get-tuple-element.15.refs_7_) | copy-start | bytes 1622020
  93.2 25.9 %collective-permute-start = (bf16[2112,128]{1,0:T(8,128)(2,1)S(1)}, bf16[2112,128]{1,0:T(8,128)(2,1)S(1)}, u32[]{:S(2)}, u32[]{:S(2)}) collective-permute-start(bf16[2112,128]{1,0:T(8,128)(2,1)S(1)} %get-tuple-element.15.refs_7_), channel_id=1, source_target_pairs={{8,0},{0,8},{24,16},{16,24},{9,1},{1,9},{25,17},{17,25},{10,2},{2,... | collective-permute-start | bytes 1622024 | tf_op jit(solution)/shard_map/ppermute | solution.py:457
  93.7 27.5 %collective-permute-start.1 = (bf16[2112,128]{1,0:T(8,128)(2,1)S(1)}, bf16[2112,128]{1,0:T(8,128)(2,1)S(1)}, u32[]{:S(2)}, u32[]{:S(2)}) collective-permute-start(bf16[2112,128]{1,0:T(8,128)(2,1)S(1)} %get-tuple-element.15.refs_7_), channel_id=1, source_target_pairs={{16,0},{24,8},{0,16},{8,24},{17,1},{25,9},{1,17},{9,25},{18,2},{26... | collective-permute-start | bytes 1622024 | tf_op jit(solution)/shard_map/ppermute | solution.py:457
  94.6 26.7 %collective-permute-start.2 = (bf16[2112,128]{1,0:T(8,128)(2,1)S(1)}, bf16[2112,128]{1,0:T(8,128)(2,1)S(1)}, u32[]{:S(2)}, u32[]{:S(2)}) collective-permute-start(bf16[2112,128]{1,0:T(8,128)(2,1)S(1)} %get-tuple-element.15.refs_7_), channel_id=1, source_target_pairs={{24,0},{16,8},{8,16},{0,24},{25,1},{17,9},{9,17},{1,25},{26,2},{18... | collective-permute-start | bytes 1622024 | tf_op jit(solution)/shard_map/ppermute | solution.py:457
  117.7 27.0 %copy-start.1 = (bf16[8192,128]{1,0:T(8,128)(2,1)S(1)}, bf16[8192,128]{1,0:T(8,128)(2,1)}, u32[]{:S(2)}) copy-start(bf16[8192,128]{1,0:T(8,128)(2,1)} %all-gather.2.cloned.1.call-done.refs_1_) | copy-start | bytes 6291460
  117.7 24.9 %collective-permute-start.4 = (bf16[2112,128]{1,0:T(8,128)(2,1)}, bf16[2112,128]{1,0:T(8,128)(2,1)}, u32[]{:S(2)}, u32[]{:S(2)}) collective-permute-start(bf16[2112,128]{1,0:T(8,128)(2,1)} %new_rows.7.refs_5_), channel_id=1, source_target_pairs={{8,0},{0,8},{24,16},{16,24},{9,1},{1,9},{25,17},{17,25},{10,2},{2,... | collective-permute-start | bytes 1622024 | tf_op jit(solution)/shard_map/ppermute | solution.py:457
  118.2 26.6 %collective-permute-start.5 = (bf16[2112,128]{1,0:T(8,128)(2,1)}, bf16[2112,128]{1,0:T(8,128)(2,1)}, u32[]{:S(2)}, u32[]{:S(2)}) collective-permute-start(bf16[2112,128]{1,0:T(8,128)(2,1)} %new_rows.7.refs_5_), channel_id=1, source_target_pairs={{16,0},{24,8},{0,16},{8,24},{17,1},{25,9},{1,17},{9,25},{18,2},{26... | collective-permute-start | bytes 1622024 | tf_op jit(solution)/shard_map/ppermute | solution.py:457
  119.1 22.1 %copy-start.2 = (bf16[2112,128]{1,0:T(8,128)(2,1)}, bf16[2112,128]{1,0:T(8,128)(2,1)S(1)}, u32[]{:S(2)}) copy-start(bf16[2112,128]{1,0:T(8,128)(2,1)S(1)} %collective-permute-done.refs_4_.refs_8_) | copy-start | bytes 1622020
  119.1 25.7 %collective-permute-start.6 = (bf16[2112,128]{1,0:T(8,128)(2,1)}, bf16[2112,128]{1,0:T(8,128)(2,1)}, u32[]{:S(2)}, u32[]{:S(2)}) collective-permute-start(bf16[2112,128]{1,0:T(8,128)(2,1)} %new_rows.7.refs_5_), channel_id=1, source_target_pairs={{24,0},{16,8},{8,16},{0,24},{25,1},{17,9},{9,17},{1,25},{26,2},{18... | collective-permute-start | bytes 1622024 | tf_op jit(solution)/shard_map/ppermute | solution.py:457
  121.2 20.0 %copy-start.4 = (bf16[2112,128]{1,0:T(8,128)(2,1)}, bf16[2112,128]{1,0:T(8,128)(2,1)S(1)}, u32[]{:S(2)}) copy-start(bf16[2112,128]{1,0:T(8,128)(2,1)S(1)} %collective-permute-done.1.refs_5_.refs_9_) | copy-start | bytes 1622020
  121.2 20.0 %copy-start.6 = (bf16[2112,128]{1,0:T(8,128)(2,1)}, bf16[2112,128]{1,0:T(8,128)(2,1)S(1)}, u32[]{:S(2)}) copy-start(bf16[2112,128]{1,0:T(8,128)(2,1)S(1)} %collective-permute-done.2.refs_6_.refs_10_) | copy-start | bytes 1622020
  141.2 22.2 %collective-permute-start.3 = (bf16[2112,128]{1,0:T(8,128)(2,1)S(1)}, bf16[2112,128]{1,0:T(8,128)(2,1)S(1)}, u32[]{:S(2)}, u32[]{:S(2)}) collective-permute-start(bf16[2112,128]{1,0:T(8,128)(2,1)S(1)} %new_rows.6.refs_0_), channel_id=1, source_target_pairs={{8,0},{0,8},{24,16},{16,24},{9,1},{1,9},{25,17},{17,25},{10,2},{2,... | collective-permute-start | bytes 1622024 | tf_op jit(solution)/shard_map/ppermute | solution.py:457
  141.7 40.9 %collective-permute-start.10 = (bf16[2112,128]{1,0:T(8,128)(2,1)S(1)}, bf16[2112,128]{1,0:T(8,128)(2,1)S(1)}, u32[]{:S(2)}, u32[]{:S(2)}) collective-permute-start(bf16[2112,128]{1,0:T(8,128)(2,1)S(1)} %new_rows.6.refs_0_), channel_id=1, source_target_pairs={{16,0},{24,8},{0,16},{8,24},{17,1},{25,9},{1,17},{9,25},{18,2},{26... | collective-permute-start | bytes 1622024 | tf_op jit(solution)/shard_map/ppermute | solution.py:457
  142.6 40.1 %collective-permute-start.11 = (bf16[2112,128]{1,0:T(8,128)(2,1)S(1)}, bf16[2112,128]{1,0:T(8,128)(2,1)S(1)}, u32[]{:S(2)}, u32[]{:S(2)}) collective-permute-start(bf16[2112,128]{1,0:T(8,128)(2,1)S(1)} %new_rows.6.refs_0_), channel_id=1, source_target_pairs={{24,0},{16,8},{8,16},{0,24},{25,1},{17,9},{9,17},{1,25},{26,2},{18... | collective-permute-start | bytes 1622024 | tf_op jit(solution)/shard_map/ppermute | solution.py:457
  144.8 1.0 copy-start.3
  145.8 1.0 copy-start.5
  146.9 1.0 copy-start.7
  147.9 1.0 copy-start.9
  161.8 17.3 %collective-permute-start.12 = (bf16[1056,128]{1,0:T(8,128)(2,1)S(1)}, bf16[1056,128]{1,0:T(8,128)(2,1)S(1)}, u32[]{:S(2)}, u32[]{:S(2)}) collective-permute-start(bf16[1056,128]{1,0:T(8,128)(2,1)S(1)} %get-tuple-element.19.refs_4_), channel_id=1, source_target_pairs={{8,0},{0,8},{24,16},{16,24},{9,1},{1,9},{25,17},{17,25},{10,2},{2,... | collective-permute-start | bytes 811016 | tf_op jit(solution)/shard_map/ppermute | solution.py:457
  162.7 17.3 %collective-permute-start.13 = (bf16[1056,128]{1,0:T(8,128)(2,1)S(1)}, bf16[1056,128]{1,0:T(8,128)(2,1)S(1)}, u32[]{:S(2)}, u32[]{:S(2)}) collective-permute-start(bf16[1056,128]{1,0:T(8,128)(2,1)S(1)} %get-tuple-element.19.refs_4_), channel_id=1, source_target_pairs={{16,0},{24,8},{0,16},{8,24},{17,1},{25,9},{1,17},{9,25},{18,2},{26... | collective-permute-start | bytes 811016 | tf_op jit(solution)/shard_map/ppermute | solution.py:457
  163.4 17.3 %collective-permute-start.14 = (bf16[1056,128]{1,0:T(8,128)(2,1)S(1)}, bf16[1056,128]{1,0:T(8,128)(2,1)S(1)}, u32[]{:S(2)}, u32[]{:S(2)}) collective-permute-start(bf16[1056,128]{1,0:T(8,128)(2,1)S(1)} %get-tuple-element.19.refs_4_), channel_id=1, source_target_pairs={{24,0},{16,8},{8,16},{0,24},{25,1},{17,9},{9,17},{1,25},{26,2},{18... | collective-permute-start | bytes 811016 | tf_op jit(solution)/shard_map/ppermute | solution.py:457
  179.1 8.5 %collective-permute-start.7 = (bf16[1056,128]{1,0:T(8,128)(2,1)S(1)}, bf16[1056,128]{1,0:T(8,128)(2,1)S(1)}, u32[]{:S(2)}, u32[]{:S(2)}) collective-permute-start(bf16[1056,128]{1,0:T(8,128)(2,1)S(1)} %get-tuple-element.18.refs_0_), channel_id=1, source_target_pairs={{8,0},{0,8},{24,16},{16,24},{9,1},{1,9},{25,17},{17,25},{10,2},{2,... | collective-permute-start | bytes 811016 | tf_op jit(solution)/shard_map/ppermute | solution.py:457
  180.0 11.0 %collective-permute-start.8 = (bf16[1056,128]{1,0:T(8,128)(2,1)S(1)}, bf16[1056,128]{1,0:T(8,128)(2,1)S(1)}, u32[]{:S(2)}, u32[]{:S(2)}) collective-permute-start(bf16[1056,128]{1,0:T(8,128)(2,1)S(1)} %get-tuple-element.18.refs_0_), channel_id=1, source_target_pairs={{16,0},{24,8},{0,16},{8,24},{17,1},{25,9},{1,17},{9,25},{18,2},{26... | collective-permute-start | bytes 811016 | tf_op jit(solution)/shard_map/ppermute | solution.py:457
  180.7 10.3 %collective-permute-start.9 = (bf16[1056,128]{1,0:T(8,128)(2,1)S(1)}, bf16[1056,128]{1,0:T(8,128)(2,1)S(1)}, u32[]{:S(2)}, u32[]{:S(2)}) collective-permute-start(bf16[1056,128]{1,0:T(8,128)(2,1)S(1)} %get-tuple-element.18.refs_0_), channel_id=1, source_target_pairs={{24,0},{16,8},{8,16},{0,24},{25,1},{17,9},{9,17},{1,25},{26,2},{18... | collective-permute-start | bytes 811016 | tf_op jit(solution)/shard_map/ppermute | solution.py:457
Sparse Core Ops, SparseCore 0:
  9.8 38.0 all-gather.1
where the time goes:
time: 204 us; the launch traced here: 201 us
  Pallas kernels  144 us (71%)
  starting transfers between devices  21.7 us (11%)
  waiting for transfers between devices  14.8 us (7%)
  between operations  14.6 us (7%)
  local copies, waits for them, and re-layouts  5.81 us (3%)
    pallas_call x5, Pallas kernels, updated_chunk(): pl.pallas_call(functools.partial(update_kernel, joins, len(after), placed...  87.2 us
    pallas_call x1, Pallas kernels, local_lse(): pl.pallas_call(functools.partial(stats_kernel, sub_rows, tok_cols), grid=...  49.5 us
    ppermute x15, starting transfers between devices, from_others(): found.append(lax.ppermute(value, axis, pairs))  17.7 us
    all_to_all x1, waiting for transfers between devices, local(): parts = lax.all_to_all(own_lse, ('tok', 'cent'), 0, 0, tiled=True)  10.2 us
    pallas_call x2, Pallas kernels, placed(): pl.pallas_call(functools.partial(place_kernel, chunks, block_rows), grid_...  6.88 us
    unnamed x24, local copies, waits for them, and re-layouts  5.81 us
  transfers between devices with their start and end apart: 17, of which 3 were waited for; matrix products, arithmetic and copies ran while one was open for 0% of the time, Pallas kernels for 60%

commit v1 on v0

--- a/solution.py
+++ b/solution.py
@@ -154,14 +154,14 @@
             pltpu.VMEM((subs, 8, tok_count), jnp.float32),
             pltpu.SMEM((flags,), jnp.float32),
         ],
-        compiler_params=pltpu.CompilerParams(vmem_limit_bytes=vmem_bytes),
+        compiler_params=pltpu.CompilerParams(vmem_limit_bytes=vmem_bytes * 4 // 7),
         cost_estimate=pl.CostEstimate(
             flops=2 * tok_count * cent_count * width,
             bytes_accessed=(tok_count + cent_count) * width * 2,
             transcendentals=tok_count * cent_count,
         ),
         name="row_stats",
-    )(tokens, centroids)
+    )(*(pltpu.with_memory_space_constraint(x, pltpu.HBM) for x in (tokens, centroids)))
 
 
 def encoded(x):
@@ -337,6 +337,11 @@
         pl.when(step == steps - 1)(placing.finish)
 
 
+def flat(codes):
+    own, *others = codes
+    return own + [pltpu.with_memory_space_constraint(part, pltpu.VMEM) for part in sum(others, [])]
+
+
 def updated_chunk(
     table, chunk, toks, lse, centroids, blocks, block_rows, after=(), received=None, joins=0
 ):
@@ -350,8 +355,8 @@
     operands = [
         toks,
         lse,
-        pltpu.with_memory_space_constraint(centroids, pltpu.HBM),
-        *after,
+        centroids,
+        *(pltpu.with_memory_space_constraint(part, pltpu.VMEM) for part in after),
     ]
     in_specs = [
         pl.BlockSpec((all_count, width), whole),
@@ -372,7 +377,7 @@
     if received:
         placed_chunk, codes, outs = received
         pieces = [len(parts) for parts in codes]
-        operands += [*sum(codes, []), *outs]
+        operands += [*flat(codes), *outs]
         in_specs += [anywhere] * (sum(pieces) + 2)
         out_specs += [anywhere] * 2
         out_shape += [jax.ShapeDtypeStruct(out.shape, out.dtype) for out in outs]
@@ -419,7 +424,7 @@
     operands, chunks, scratch_shapes = [], [], []
     for chunk, codes in received:
         chunks.append((chunk, [len(parts) for parts in codes]))
-        operands += sum(codes, [])
+        operands += flat(codes)
         rows, width = codes[0][0].shape
         blocks = rows // coded_rows(block_rows)
         scratch_shapes += Placing.scratch(len(codes), blocks, block_rows, width)

time: 204 us -> 206 us (level)
  local copies, waits for them, and re-layouts: 5.81 us -> 9.19 us
    unnamed x24 -> x26, local copies, waits for them, and re-layouts: 5.81 us -> 9.19 us
  transfers between devices with their start and end apart: 17 -> 17, of which waited for: 3 -> 3; matrix products, arithmetic and copies ran while one was open for 0% -> 0% of each run, Pallas kernels for 60% -> 59%
where the time goes in v1:
time: 206 us; the launch traced here: 203 us
  Pallas kernels  142 us (69%)
  starting transfers between devices  21.7 us (11%)
  waiting for transfers between devices  15.4 us (7%)
  between operations  14.6 us (7%)
  local copies, waits for them, and re-layouts  9.19 us (4%)
    pallas_call x5, Pallas kernels, updated_chunk(): pl.pallas_call(functools.partial(update_kernel, joins, len(after), placed...  85.3 us
    pallas_call x1, Pallas kernels, local_lse(): pl.pallas_call(functools.partial(stats_kernel, sub_rows, tok_cols), grid=...  49.5 us
    ppermute x15, starting transfers between devices, from_others(): found.append(lax.ppermute(value, axis, pairs))  17.7 us
    all_to_all x1, waiting for transfers between devices, local(): parts = lax.all_to_all(own_lse, ('tok', 'cent'), 0, 0, tiled=True)  10.2 us
    unnamed x26, local copies, waits for them, and re-layouts  9.19 us
    pallas_call x2, Pallas kernels, placed(): pl.pallas_call(functools.partial(place_kernel, chunks, block_rows), grid_...  6.88 us
    ppermute x15, waiting for transfers between devices, from_others(): found.append(lax.ppermute(value, axis, pairs))  4.53 us
  transfers between devices with their start and end apart: 17, of which 3 were waited for; matrix products, arithmetic and copies ran while one was open for 0% of the time, Pallas kernels for 59%

profile of v1, /device:TPU:0, one launch (start us, length us, event | category | flops | bytes accessed | tf_op | source)
XLA Modules:
  0.0 202.8 jit_solution(1558997663934466560)
XLA Ops:
  7.2 0.7 all-gather.2.cloned.1.call-update
  7.9 49.5 %row_stats.1 = f32[32,1,2048]{2,1,0:T(1,128)} custom-call(bf16[2048,128]{1,0:T(8,128)(2,1)} %tok_ref.1, bf16[32768,128]{1,0:T(8,128)(2,1)} %refs_3_.9), custom_call_target="tpu_custom_call" | custom-call | flops 17179869184 | bytes 8912896 | tf_op jit(solution)/shard_map/row_stats/pallas_call | solution.py:141
  57.4 3.9 %all-to-all-start = ((f32[32,1,2048]{2,1,0:T(1,128)}), f32[32,1,2048]{2,1,0:T(1,128)S(1)}, u32[]{:S(2)}, u32[]{:S(2)}) async-start(f32[32,1,2048]{2,1,0:T(1,128)} %row_stats.1), calls=%async_computation | async-start | bytes 524288 | tf_op jit(solution)/shard_map/all_to_all | solution.py:486
  61.5 10.2 %all-to-all-done.refs_2_ = f32[32,1,2048]{2,1,0:T(1,128)S(1)} async-done(((f32[32,1,2048]{2,1,0:T(1,128)}), f32[32,1,2048]{2,1,0:T(1,128)S(1)}, u32[]{:S(2)}, u32[]{:S(2)}) %all-to-all-start) | async-done | bytes 262176 | tf_op jit(solution)/shard_map/all_to_all | solution.py:486
  71.8 3.4 %copy-done = bf16[32768,128]{1,0:T(8,128)(2,1)S(1)} copy-done((bf16[32768,128]{1,0:T(8,128)(2,1)S(1)}, bf16[32768,128]{1,0:T(8,128)(2,1)}, u32[]{:S(2)}) %copy-start) | copy-done | bytes 8388632
  75.1 1.6 copy-done.1
  76.7 18.9 %new_rows.5 = (bf16[2112,128]{1,0:T(8,128)(2,1)S(1)}, f32[1,8192]{1,0:T(1,128)S(1)}) custom-call(s32[5,4]{1,0:T(8,128)S(1)} %multiply_add_fusion.refs_0_.table_ref, bf16[8192,128]{1,0:T(8,128)(2,1)S(1)} %copy-done.1, f32[32,1,2048]{2,1,0:T(1,128)S(1)} %all-to-all-done.refs_2_, bf16[32768,128]{1,0:T(8,128)(2,1)S(1)} %copy-done), custom_call_target="tpu_custom_call" | custom-call | flops 1610612736 | bytes 393216 | tf_op jit(solution)/shard_map/new_rows/pallas_call | solution.py:386
  96.2 0.9 collective-permute-start.1
  97.0 2.2 %collective-permute-start.2 = (bf16[2112,128]{1,0:T(8,128)(2,1)S(1)}, bf16[2112,128]{1,0:T(8,128)(2,1)S(1)}, u32[]{:S(2)}, u32[]{:S(2)}) collective-permute-start(bf16[2112,128]{1,0:T(8,128)(2,1)S(1)} %get-tuple-element.15.refs_7_), channel_id=1, source_target_pairs={{24,0},{16,8},{8,16},{0,24},{25,1},{17,9},{9,17},{1,25},{26,2},{18... | collective-permute-start | bytes 1622024 | tf_op jit(solution)/shard_map/ppermute | solution.py:462
  99.2 20.0 %new_rows.7.refs_5_ = bf16[2112,128]{1,0:T(8,128)(2,1)} custom-call(s32[5,4]{1,0:T(8,128)S(1)} %multiply_add_fusion.refs_0_.table_ref, bf16[8192,128]{1,0:T(8,128)(2,1)S(1)} %copy-done.1, f32[1,8192]{1,0:T(1,128)S(1)} %get-tuple-element.14.refs_2_, bf16[32768,128]{1,0:T(8,128)(2,1)S(1)} %copy-done), custom_call_target="tpu_custom_call" | custom-call | flops 1610612736 | bytes 393216 | tf_op jit(solution)/shard_map/new_rows/pallas_call | solution.py:386
  119.7 0.9 collective-permute-start.5
  120.5 2.2 %collective-permute-start.6 = (bf16[2112,128]{1,0:T(8,128)(2,1)}, bf16[2112,128]{1,0:T(8,128)(2,1)}, u32[]{:S(2)}, u32[]{:S(2)}) collective-permute-start(bf16[2112,128]{1,0:T(8,128)(2,1)} %new_rows.7.refs_5_), channel_id=1, source_target_pairs={{24,0},{16,8},{8,16},{0,24},{25,1},{17,9},{9,17},{1,25},{26,2},{18... | collective-permute-start | bytes 1622024 | tf_op jit(solution)/shard_map/ppermute | solution.py:462
  122.7 19.9 %new_rows.6.refs_0_ = bf16[2112,128]{1,0:T(8,128)(2,1)S(1)} custom-call(s32[5,4]{1,0:T(8,128)S(1)} %multiply_add_fusion.refs_0_.table_ref, bf16[8192,128]{1,0:T(8,128)(2,1)S(1)} %copy-done.1, f32[1,8192]{1,0:T(1,128)S(1)} %get-tuple-element.14.refs_2_, bf16[32768,128]{1,0:T(8,128)(2,1)} %refs_3_.9, ...), custom_call_target="tpu_custom_call" | custom-call | flops 1610612736 | bytes 393216 | tf_op jit(solution)/shard_map/new_rows/pallas_call | solution.py:386
  142.7 1.1 collective-permute-start.3
  143.8 0.7 collective-permute-start.10
  144.5 1.7 collective-permute-start.11
  146.3 1.0 copy-done.4
  147.3 1.0 copy-done.6
  148.4 1.0 copy-done.8
  149.4 1.0 copy-done.10
  150.4 12.8 %new_rows.8 = (bf16[1056,128]{1,0:T(8,128)(2,1)S(1)}, f32[32768,128]{1,0:T(8,128)}, f32[256,128]{1,0:T(8,128)}) custom-call(s32[5,4]{1,0:T(8,128)S(1)} %multiply_add_fusion.refs_0_.table_ref, bf16[8192,128]{1,0:T(8,128)(2,1)S(1)} %copy-done.2, f32[1,8192]{1,0:T(1,128)S(1)} %get-tuple-element.14.refs_2_, ...), custom_call_target="tpu_custom_call", output_to_operand_aliasing={{1}: (11, {}), {2}: (12, {})} | custom-call | flops 805306368 | bytes 327680 | tf_op jit(solution)/shard_map/new_rows/pallas_call | solution.py:386
  163.3 1.1 collective-permute-start.12
  164.4 1.0 collective-permute-start.13
  165.4 1.4 collective-permute-start.14
  166.9 13.7 %new_rows.9 = (bf16[1056,128]{1,0:T(8,128)(2,1)S(1)}, f32[32768,128]{1,0:T(8,128)}, f32[256,128]{1,0:T(8,128)}) custom-call(s32[5,4]{1,0:T(8,128)S(1)} %multiply_add_fusion.refs_0_.table_ref, bf16[8192,128]{1,0:T(8,128)(2,1)S(1)} %copy-done.2, f32[1,8192]{1,0:T(1,128)S(1)} %get-tuple-element.14.refs_2_, ...), custom_call_target="tpu_custom_call", output_to_operand_aliasing={{1}: (9, {}), {2}: (10, {})} | custom-call | flops 805306368 | bytes 327680 | tf_op jit(solution)/shard_map/new_rows/pallas_call | solution.py:386
  180.6 1.1 collective-permute-start.7
  181.7 1.0 collective-permute-start.8
  182.7 1.4 collective-permute-start.9
  184.1 4.4 %placed_rows.2 = (f32[32768,128]{1,0:T(8,128)}, f32[256,128]{1,0:T(8,128)}) custom-call(s32[5,4]{1,0:T(8,128)S(1)} %multiply_add_fusion.refs_0_.table_ref, bf16[2112,128]{1,0:T(8,128)(2,1)S(1)} %new_rows.6.refs_0_, bf16[2112,128]{1,0:T(8,128)(2,1)S(1)} %collective-permute-done.3.refs_4_.refs_1_, ...), custom_call_target="tpu_custom_call", output_to_operand_aliasing={{0}: (9, {}), {1}: (10, {})} | custom-call | tf_op jit(solution)/shard_map/placed_rows/pallas_call | solution.py:432
  188.6 1.0 collective-permute-done.7.refs_1_
  189.6 3.5 %collective-permute-done.8.refs_2_ = bf16[1056,128]{1,0:T(8,128)(2,1)S(1)} collective-permute-done((bf16[1056,128]{1,0:T(8,128)(2,1)S(1)}, bf16[1056,128]{1,0:T(8,128)(2,1)S(1)}, u32[]{:S(2)}, u32[]{:S(2)}) %collective-permute-start.8) | collective-permute-done | bytes 270368 | tf_op jit(solution)/shard_map/ppermute | solution.py:462
  193.1 2.4 %placed_rows.3 = (f32[32768,128]{1,0:T(8,128)}, f32[256,128]{1,0:T(8,128)}) custom-call(s32[5,4]{1,0:T(8,128)S(1)} %multiply_add_fusion.refs_0_.table_ref, bf16[1056,128]{1,0:T(8,128)(2,1)S(1)} %get-tuple-element.18.refs_0_, bf16[1056,128]{1,0:T(8,128)(2,1)S(1)} %collective-permute-done.7.refs_1_, ...), custom_call_target="tpu_custom_call", output_to_operand_aliasing={{0}: (5, {}), {1}: (6, {})} | custom-call | tf_op jit(solution)/shard_map/placed_rows/pallas_call | solution.py:432
  (41 shorter events, 1.3 us)
Async XLA Ops:
  7.2 64.6 %all-gather.2.cloned.1.call-start = ((), (), s32[]{:S(2)}) async-start(), calls=%async_computation.1 | async-start | bytes 2621440 | tf_op jit(solution)/shard_map/all_gather | solution.py:484
  7.9 53.6 %copy-start.11 = (s32[5]{0:T(128)S(1)}, s32[5]{0:T(128)}, u32[]{:S(2)}) copy-start(s32[5]{0:T(128)} %constant.17) | copy-start | bytes 64
  7.9 53.6 %copy-start.12 = (s32[5]{0:T(128)S(1)}, s32[5]{0:T(128)}, u32[]{:S(2)}) copy-start(s32[5]{0:T(128)} %constant.18) | copy-start | bytes 64
  57.4 14.3 %all-to-all-start = ((f32[32,1,2048]{2,1,0:T(1,128)}), f32[32,1,2048]{2,1,0:T(1,128)S(1)}, u32[]{:S(2)}, u32[]{:S(2)}) async-start(f32[32,1,2048]{2,1,0:T(1,128)} %row_stats.1), calls=%async_computation | async-start | bytes 524288 | tf_op jit(solution)/shard_map/all_to_all | solution.py:486
  71.7 3.4 %copy-start = (bf16[32768,128]{1,0:T(8,128)(2,1)S(1)}, bf16[32768,128]{1,0:T(8,128)(2,1)}, u32[]{:S(2)}) copy-start(bf16[32768,128]{1,0:T(8,128)(2,1)} %refs_3_.9) | copy-start | bytes 25165828
  75.1 1.6 copy-start.1
  95.6 47.1 %copy-start.9 = (bf16[2112,128]{1,0:T(8,128)(2,1)}, bf16[2112,128]{1,0:T(8,128)(2,1)S(1)}, u32[]{:S(2)}) copy-start(bf16[2112,128]{1,0:T(8,128)(2,1)S(1)} %get-tuple-element.15.refs_7_) | copy-start | bytes 1622020
  95.6 24.9 %collective-permute-start = (bf16[2112,128]{1,0:T(8,128)(2,1)S(1)}, bf16[2112,128]{1,0:T(8,128)(2,1)S(1)}, u32[]{:S(2)}, u32[]{:S(2)}) collective-permute-start(bf16[2112,128]{1,0:T(8,128)(2,1)S(1)} %get-tuple-element.15.refs_7_), channel_id=1, source_target_pairs={{8,0},{0,8},{24,16},{16,24},{9,1},{1,9},{25,17},{17,25},{10,2},{2,... | collective-permute-start | bytes 1622024 | tf_op jit(solution)/shard_map/ppermute | solution.py:462
  96.2 26.5 %collective-permute-start.1 = (bf16[2112,128]{1,0:T(8,128)(2,1)S(1)}, bf16[2112,128]{1,0:T(8,128)(2,1)S(1)}, u32[]{:S(2)}, u32[]{:S(2)}) collective-permute-start(bf16[2112,128]{1,0:T(8,128)(2,1)S(1)} %get-tuple-element.15.refs_7_), channel_id=1, source_target_pairs={{16,0},{24,8},{0,16},{8,24},{17,1},{25,9},{1,17},{9,25},{18,2},{26... | collective-permute-start | bytes 1622024 | tf_op jit(solution)/shard_map/ppermute | solution.py:462
  97.0 25.7 %collective-permute-start.2 = (bf16[2112,128]{1,0:T(8,128)(2,1)S(1)}, bf16[2112,128]{1,0:T(8,128)(2,1)S(1)}, u32[]{:S(2)}, u32[]{:S(2)}) collective-permute-start(bf16[2112,128]{1,0:T(8,128)(2,1)S(1)} %get-tuple-element.15.refs_7_), channel_id=1, source_target_pairs={{24,0},{16,8},{8,16},{0,24},{25,1},{17,9},{9,17},{1,25},{26,2},{18... | collective-permute-start | bytes 1622024 | tf_op jit(solution)/shard_map/ppermute | solution.py:462
  119.2 27.0 %copy-start.2 = (bf16[8192,128]{1,0:T(8,128)(2,1)S(1)}, bf16[8192,128]{1,0:T(8,128)(2,1)}, u32[]{:S(2)}) copy-start(bf16[8192,128]{1,0:T(8,128)(2,1)} %all-gather.2.cloned.1.call-done.refs_1_) | copy-start | bytes 6291460
  119.2 25.3 %collective-permute-start.4 = (bf16[2112,128]{1,0:T(8,128)(2,1)}, bf16[2112,128]{1,0:T(8,128)(2,1)}, u32[]{:S(2)}, u32[]{:S(2)}) collective-permute-start(bf16[2112,128]{1,0:T(8,128)(2,1)} %new_rows.7.refs_5_), channel_id=1, source_target_pairs={{8,0},{0,8},{24,16},{16,24},{9,1},{1,9},{25,17},{17,25},{10,2},{2,... | collective-permute-start | bytes 1622024 | tf_op jit(solution)/shard_map/ppermute | solution.py:462
  119.7 26.6 %collective-permute-start.5 = (bf16[2112,128]{1,0:T(8,128)(2,1)}, bf16[2112,128]{1,0:T(8,128)(2,1)}, u32[]{:S(2)}, u32[]{:S(2)}) collective-permute-start(bf16[2112,128]{1,0:T(8,128)(2,1)} %new_rows.7.refs_5_), channel_id=1, source_target_pairs={{16,0},{24,8},{0,16},{8,24},{17,1},{25,9},{1,17},{9,25},{18,2},{26... | collective-permute-start | bytes 1622024 | tf_op jit(solution)/shard_map/ppermute | solution.py:462
  120.5 22.1 %copy-start.3 = (bf16[2112,128]{1,0:T(8,128)(2,1)}, bf16[2112,128]{1,0:T(8,128)(2,1)S(1)}, u32[]{:S(2)}) copy-start(bf16[2112,128]{1,0:T(8,128)(2,1)S(1)} %collective-permute-done.refs_4_.refs_8_) | copy-start | bytes 1622020
  120.5 25.7 %collective-permute-start.6 = (bf16[2112,128]{1,0:T(8,128)(2,1)}, bf16[2112,128]{1,0:T(8,128)(2,1)}, u32[]{:S(2)}, u32[]{:S(2)}) collective-permute-start(bf16[2112,128]{1,0:T(8,128)(2,1)} %new_rows.7.refs_5_), channel_id=1, source_target_pairs={{24,0},{16,8},{8,16},{0,24},{25,1},{17,9},{9,17},{1,25},{26,2},{18... | collective-permute-start | bytes 1622024 | tf_op jit(solution)/shard_map/ppermute | solution.py:462
  122.7 20.0 %copy-start.5 = (bf16[2112,128]{1,0:T(8,128)(2,1)}, bf16[2112,128]{1,0:T(8,128)(2,1)S(1)}, u32[]{:S(2)}) copy-start(bf16[2112,128]{1,0:T(8,128)(2,1)S(1)} %collective-permute-done.1.refs_5_.refs_9_) | copy-start | bytes 1622020
  122.7 20.0 %copy-start.7 = (bf16[2112,128]{1,0:T(8,128)(2,1)}, bf16[2112,128]{1,0:T(8,128)(2,1)S(1)}, u32[]{:S(2)}) copy-start(bf16[2112,128]{1,0:T(8,128)(2,1)S(1)} %collective-permute-done.2.refs_6_.refs_10_) | copy-start | bytes 1622020
  142.7 22.7 %collective-permute-start.3 = (bf16[2112,128]{1,0:T(8,128)(2,1)S(1)}, bf16[2112,128]{1,0:T(8,128)(2,1)S(1)}, u32[]{:S(2)}, u32[]{:S(2)}) collective-permute-start(bf16[2112,128]{1,0:T(8,128)(2,1)S(1)} %new_rows.6.refs_0_), channel_id=1, source_target_pairs={{8,0},{0,8},{24,16},{16,24},{9,1},{1,9},{25,17},{17,25},{10,2},{2,... | collective-permute-start | bytes 1622024 | tf_op jit(solution)/shard_map/ppermute | solution.py:462
  143.8 40.3 %collective-permute-start.10 = (bf16[2112,128]{1,0:T(8,128)(2,1)S(1)}, bf16[2112,128]{1,0:T(8,128)(2,1)S(1)}, u32[]{:S(2)}, u32[]{:S(2)}) collective-permute-start(bf16[2112,128]{1,0:T(8,128)(2,1)S(1)} %new_rows.6.refs_0_), channel_id=1, source_target_pairs={{16,0},{24,8},{0,16},{8,24},{17,1},{25,9},{1,17},{9,25},{18,2},{26... | collective-permute-start | bytes 1622024 | tf_op jit(solution)/shard_map/ppermute | solution.py:462
  144.5 39.6 %collective-permute-start.11 = (bf16[2112,128]{1,0:T(8,128)(2,1)S(1)}, bf16[2112,128]{1,0:T(8,128)(2,1)S(1)}, u32[]{:S(2)}, u32[]{:S(2)}) collective-permute-start(bf16[2112,128]{1,0:T(8,128)(2,1)S(1)} %new_rows.6.refs_0_), channel_id=1, source_target_pairs={{24,0},{16,8},{8,16},{0,24},{25,1},{17,9},{9,17},{1,25},{26,2},{18... | collective-permute-start | bytes 1622024 | tf_op jit(solution)/shard_map/ppermute | solution.py:462
  146.3 1.0 copy-start.4
  147.3 1.0 copy-start.6
  148.4 1.0 copy-start.8
  149.4 1.0 copy-start.10
  163.3 17.3 %collective-permute-start.12 = (bf16[1056,128]{1,0:T(8,128)(2,1)S(1)}, bf16[1056,128]{1,0:T(8,128)(2,1)S(1)}, u32[]{:S(2)}, u32[]{:S(2)}) collective-permute-start(bf16[1056,128]{1,0:T(8,128)(2,1)S(1)} %get-tuple-element.19.refs_4_), channel_id=1, source_target_pairs={{8,0},{0,8},{24,16},{16,24},{9,1},{1,9},{25,17},{17,25},{10,2},{2,... | collective-permute-start | bytes 811016 | tf_op jit(solution)/shard_map/ppermute | solution.py:462
  164.4 17.3 %collective-permute-start.13 = (bf16[1056,128]{1,0:T(8,128)(2,1)S(1)}, bf16[1056,128]{1,0:T(8,128)(2,1)S(1)}, u32[]{:S(2)}, u32[]{:S(2)}) collective-permute-start(bf16[1056,128]{1,0:T(8,128)(2,1)S(1)} %get-tuple-element.19.refs_4_), channel_id=1, source_target_pairs={{16,0},{24,8},{0,16},{8,24},{17,1},{25,9},{1,17},{9,25},{18,2},{26... | collective-permute-start | bytes 811016 | tf_op jit(solution)/shard_map/ppermute | solution.py:462
  165.4 17.3 %collective-permute-start.14 = (bf16[1056,128]{1,0:T(8,128)(2,1)S(1)}, bf16[1056,128]{1,0:T(8,128)(2,1)S(1)}, u32[]{:S(2)}, u32[]{:S(2)}) collective-permute-start(bf16[1056,128]{1,0:T(8,128)(2,1)S(1)} %get-tuple-element.19.refs_4_), channel_id=1, source_target_pairs={{24,0},{16,8},{8,16},{0,24},{25,1},{17,9},{9,17},{1,25},{26,2},{18... | collective-permute-start | bytes 811016 | tf_op jit(solution)/shard_map/ppermute | solution.py:462
  180.6 9.0 %collective-permute-start.7 = (bf16[1056,128]{1,0:T(8,128)(2,1)S(1)}, bf16[1056,128]{1,0:T(8,128)(2,1)S(1)}, u32[]{:S(2)}, u32[]{:S(2)}) collective-permute-start(bf16[1056,128]{1,0:T(8,128)(2,1)S(1)} %get-tuple-element.18.refs_0_), channel_id=1, source_target_pairs={{8,0},{0,8},{24,16},{16,24},{9,1},{1,9},{25,17},{17,25},{10,2},{2,... | collective-permute-start | bytes 811016 | tf_op jit(solution)/shard_map/ppermute | solution.py:462
  181.7 11.4 %collective-permute-start.8 = (bf16[1056,128]{1,0:T(8,128)(2,1)S(1)}, bf16[1056,128]{1,0:T(8,128)(2,1)S(1)}, u32[]{:S(2)}, u32[]{:S(2)}) collective-permute-start(bf16[1056,128]{1,0:T(8,128)(2,1)S(1)} %get-tuple-element.18.refs_0_), channel_id=1, source_target_pairs={{16,0},{24,8},{0,16},{8,24},{17,1},{25,9},{1,17},{9,25},{18,2},{26... | collective-permute-start | bytes 811016 | tf_op jit(solution)/shard_map/ppermute | solution.py:462
  182.7 10.4 %collective-permute-start.9 = (bf16[1056,128]{1,0:T(8,128)(2,1)S(1)}, bf16[1056,128]{1,0:T(8,128)(2,1)S(1)}, u32[]{:S(2)}, u32[]{:S(2)}) collective-permute-start(bf16[1056,128]{1,0:T(8,128)(2,1)S(1)} %get-tuple-element.18.refs_0_), channel_id=1, source_target_pairs={{24,0},{16,8},{8,16},{0,24},{25,1},{17,9},{9,17},{1,25},{26,2},{18... | collective-permute-start | bytes 811016 | tf_op jit(solution)/shard_map/ppermute | solution.py:462
Sparse Core Ops, SparseCore 0:
  9.8 38.0 all-gather.1

commit v2 on v0

--- a/solution.py
+++ b/solution.py
@@ -348,7 +348,7 @@
     anywhere = pl.BlockSpec(memory_space=pl.ANY)
     whole = lambda j, place: (0, 0)
     operands = [
-        toks,
+        pltpu.with_memory_space_constraint(toks, pltpu.HBM),
         lse,
         pltpu.with_memory_space_constraint(centroids, pltpu.HBM),
         *after,
@@ -372,7 +372,8 @@
     if received:
         placed_chunk, codes, outs = received
         pieces = [len(parts) for parts in codes]
-        operands += [*sum(codes, []), *outs]
+        operands += [pltpu.with_memory_space_constraint(part, pltpu.HBM) for part in sum(codes, [])]
+        operands += outs
         in_specs += [anywhere] * (sum(pieces) + 2)
         out_specs += [anywhere] * 2
         out_shape += [jax.ShapeDtypeStruct(out.shape, out.dtype) for out in outs]

time: 204 us -> 204 us (level)
  local copies, waits for them, and re-layouts: 5.81 us -> 0.03 us
  Pallas kernels: 144 us -> 147 us
  waiting for transfers between devices: 14.8 us -> 17.4 us
    unnamed x24 -> x14, local copies, waits for them, and re-layouts: 5.81 us -> 0.03 us
    pallas_call x5, Pallas kernels: 87.2 us -> 90.8 us  [updated_chunk(): pl.pallas_call(functools.partial(update_kernel, joins, len(after), placed...]
    ppermute x15, waiting for transfers between devices: 3.9 us -> 6.47 us  [from_others(): found.append(lax.ppermute(value, axis, pairs))]
  transfers between devices with their start and end apart: 17 -> 17, of which waited for: 3 -> 3; matrix products, arithmetic and copies ran while one was open for 0% -> 0% of each run, Pallas kernels for 60% -> 62%
where the time goes in v2:
time: 204 us; the launch traced here: 201 us
  Pallas kernels  147 us (72%)
  starting transfers between devices  21.8 us (11%)
  waiting for transfers between devices  17.4 us (9%)
  between operations  14.7 us (7%)
    pallas_call x5, Pallas kernels, updated_chunk(): pl.pallas_call(functools.partial(update_kernel, joins, len(after), placed...  90.8 us
    pallas_call x1, Pallas kernels, local_lse(): pl.pallas_call(functools.partial(stats_kernel, sub_rows, tok_cols), grid=...  49.5 us
    ppermute x15, starting transfers between devices, from_others(): found.append(lax.ppermute(value, axis, pairs))  17.8 us
    all_to_all x1, waiting for transfers between devices, local(): parts = lax.all_to_all(own_lse, ('tok', 'cent'), 0, 0, tiled=True)  10.2 us
    pallas_call x2, Pallas kernels, placed(): pl.pallas_call(functools.partial(place_kernel, chunks, block_rows), grid_...  6.88 us
    ppermute x15, waiting for transfers between devices, from_others(): found.append(lax.ppermute(value, axis, pairs))  6.47 us
  transfers between devices with their start and end apart: 17, of which 3 were waited for; matrix products, arithmetic and copies ran while one was open for 0% of the time, Pallas kernels for 62%

profile of v2, /device:TPU:0, one launch (start us, length us, event | category | flops | bytes accessed | tf_op | source)
XLA Modules:
  0.0 201.2 jit_solution(7406329933435047584)
XLA Ops:
  7.2 0.0 all-gather.2.cloned.1.call-start
  7.2 0.7 all-gather.2.cloned.1.call-update
  7.9 0.0 copy-start.5
  7.9 49.5 %row_stats.1 = f32[32,1,2048]{2,1,0:T(1,128)} custom-call(bf16[2048,128]{1,0:T(8,128)(2,1)} %tok_ref.1, bf16[32768,128]{1,0:T(8,128)(2,1)} %refs_3_.9), custom_call_target="tpu_custom_call" | custom-call | flops 17179869184 | bytes 8912896 | tf_op jit(solution)/shard_map/row_stats/pallas_call | solution.py:141
  57.4 3.9 %all-to-all-start = ((f32[32,1,2048]{2,1,0:T(1,128)}), f32[32,1,2048]{2,1,0:T(1,128)S(1)}, u32[]{:S(2)}, u32[]{:S(2)}) async-start(f32[32,1,2048]{2,1,0:T(1,128)} %row_stats.1), calls=%async_computation | async-start | bytes 524288 | tf_op jit(solution)/shard_map/all_to_all | solution.py:482
  61.4 0.1 pad_add_fusion
  61.5 0.1 multiply_add_fusion.refs_0_.table_ref
  61.5 10.2 %all-to-all-done.refs_2_ = f32[32,1,2048]{2,1,0:T(1,128)S(1)} async-done(((f32[32,1,2048]{2,1,0:T(1,128)}), f32[32,1,2048]{2,1,0:T(1,128)S(1)}, u32[]{:S(2)}, u32[]{:S(2)}) %all-to-all-start) | async-done | bytes 262176 | tf_op jit(solution)/shard_map/all_to_all | solution.py:482
  71.7 20.5 %new_rows.5 = (bf16[2112,128]{1,0:T(8,128)(2,1)S(1)}, f32[1,8192]{1,0:T(1,128)S(1)}) custom-call(s32[5,4]{1,0:T(8,128)S(1)} %multiply_add_fusion.refs_0_.table_ref, bf16[8192,128]{1,0:T(8,128)(2,1)} %all-gather.2.cloned.1.call-done.refs_1_, f32[32,1,2048]{2,1,0:T(1,128)S(1)} %all-to-all-done.refs_2_, bf16[32768,128]{1,0:T(8,128)(2,1)} %refs_3_.9), custom_call_target="tpu_custom_call" | custom-call | flops 1610612736 | bytes 393216 | tf_op jit(solution)/shard_map/new_rows/pallas_call | solution.py:382
  92.3 0.6 collective-permute-start
  92.9 0.8 collective-permute-start.1
  93.7 2.2 %collective-permute-start.2 = (bf16[2112,128]{1,0:T(8,128)(2,1)S(1)}, bf16[2112,128]{1,0:T(8,128)(2,1)S(1)}, u32[]{:S(2)}, u32[]{:S(2)}) collective-permute-start(bf16[2112,128]{1,0:T(8,128)(2,1)S(1)} %get-tuple-element.15.refs_7_), channel_id=1, source_target_pairs={{24,0},{16,8},{8,16},{0,24},{25,1},{17,9},{9,17},{1,25},{26,2},{18... | collective-permute-start | bytes 1622024 | tf_op jit(solution)/shard_map/ppermute | solution.py:458
  95.9 21.0 %new_rows.7.refs_5_ = bf16[2112,128]{1,0:T(8,128)(2,1)S(1)} custom-call(s32[5,4]{1,0:T(8,128)S(1)} %multiply_add_fusion.refs_0_.table_ref, bf16[8192,128]{1,0:T(8,128)(2,1)} %all-gather.2.cloned.1.call-done.refs_1_, f32[1,8192]{1,0:T(1,128)S(1)} %get-tuple-element.14.refs_2_, bf16[32768,128]{1,0:T(8,128)(2,1)} %refs_3_.9), custom_call_target="tpu_custom_call" | custom-call | flops 1610612736 | bytes 393216 | tf_op jit(solution)/shard_map/new_rows/pallas_call | solution.py:382
  116.9 0.5 collective-permute-start.4
  117.5 0.8 collective-permute-start.5
  118.3 2.2 %collective-permute-start.6 = (bf16[2112,128]{1,0:T(8,128)(2,1)S(1)}, bf16[2112,128]{1,0:T(8,128)(2,1)}, u32[]{:S(2)}, u32[]{:S(2)}) collective-permute-start(bf16[2112,128]{1,0:T(8,128)(2,1)S(1)} %new_rows.7.refs_5_), channel_id=1, source_target_pairs={{24,0},{16,8},{8,16},{0,24},{25,1},{17,9},{9,17},{1,25},{26,2},{18... | collective-permute-start | bytes 1622024 | tf_op jit(solution)/shard_map/ppermute | solution.py:458
  120.5 20.6 %new_rows.6.refs_0_ = bf16[2112,128]{1,0:T(8,128)(2,1)S(1)} custom-call(s32[5,4]{1,0:T(8,128)S(1)} %multiply_add_fusion.refs_0_.table_ref, bf16[8192,128]{1,0:T(8,128)(2,1)} %all-gather.2.cloned.1.call-done.refs_1_, f32[1,8192]{1,0:T(1,128)S(1)} %get-tuple-element.14.refs_2_, bf16[32768,128]{1,0:T(8,128)(2,1)} %refs_3_.9, ...), custom_call_target="tpu_custom_call" | custom-call | flops 1610612736 | bytes 393216 | tf_op jit(solution)/shard_map/new_rows/pallas_call | solution.py:382
  141.2 0.5 collective-permute-start.3
  141.7 0.8 collective-permute-start.10
  142.6 2.2 %collective-permute-start.11 = (bf16[2112,128]{1,0:T(8,128)(2,1)S(1)}, bf16[2112,128]{1,0:T(8,128)(2,1)S(1)}, u32[]{:S(2)}, u32[]{:S(2)}) collective-permute-start(bf16[2112,128]{1,0:T(8,128)(2,1)S(1)} %new_rows.6.refs_0_), channel_id=1, source_target_pairs={{24,0},{16,8},{8,16},{0,24},{25,1},{17,9},{9,17},{1,25},{26,2},{18... | collective-permute-start | bytes 1622024 | tf_op jit(solution)/shard_map/ppermute | solution.py:458
  144.8 14.3 %new_rows.8 = (bf16[1056,128]{1,0:T(8,128)(2,1)S(1)}, f32[32768,128]{1,0:T(8,128)}, f32[256,128]{1,0:T(8,128)}) custom-call(s32[5,4]{1,0:T(8,128)S(1)} %multiply_add_fusion.refs_0_.table_ref, bf16[8192,128]{1,0:T(8,128)(2,1)} %all-gather.2.cloned.1.call-done.refs_1_, ...), custom_call_target="tpu_custom_call", output_to_operand_aliasing={{1}: (11, {}), {2}: (12, {})} | custom-call | flops 805306368 | bytes 327680 | tf_op jit(solution)/shard_map/new_rows/pallas_call | solution.py:382
  159.1 0.5 collective-permute-start.12
  159.6 0.8 collective-permute-start.13
  160.5 2.2 %collective-permute-start.14 = (bf16[1056,128]{1,0:T(8,128)(2,1)S(1)}, bf16[1056,128]{1,0:T(8,128)(2,1)S(1)}, u32[]{:S(2)}, u32[]{:S(2)}) collective-permute-start(bf16[1056,128]{1,0:T(8,128)(2,1)S(1)} %get-tuple-element.19.refs_4_), channel_id=1, source_target_pairs={{24,0},{16,8},{8,16},{0,24},{25,1},{17,9},{9,17},{1,25},{26,2},{18... | collective-permute-start | bytes 811016 | tf_op jit(solution)/shard_map/ppermute | solution.py:458
  162.6 14.3 %new_rows.9 = (bf16[1056,128]{1,0:T(8,128)(2,1)S(1)}, f32[32768,128]{1,0:T(8,128)}, f32[256,128]{1,0:T(8,128)}) custom-call(s32[5,4]{1,0:T(8,128)S(1)} %multiply_add_fusion.refs_0_.table_ref, bf16[8192,128]{1,0:T(8,128)(2,1)} %all-gather.2.cloned.1.call-done.refs_1_, ...), custom_call_target="tpu_custom_call", output_to_operand_aliasing={{1}: (9, {}), {2}: (10, {})} | custom-call | flops 805306368 | bytes 327680 | tf_op jit(solution)/shard_map/new_rows/pallas_call | solution.py:382
  177.0 0.5 collective-permute-start.7
  177.5 0.8 collective-permute-start.8
  178.4 2.2 %collective-permute-start.9 = (bf16[1056,128]{1,0:T(8,128)(2,1)S(1)}, bf16[1056,128]{1,0:T(8,128)(2,1)S(1)}, u32[]{:S(2)}, u32[]{:S(2)}) collective-permute-start(bf16[1056,128]{1,0:T(8,128)(2,1)S(1)} %get-tuple-element.18.refs_0_), channel_id=1, source_target_pairs={{24,0},{16,8},{8,16},{0,24},{25,1},{17,9},{9,17},{1,25},{26,2},{18... | collective-permute-start | bytes 811016 | tf_op jit(solution)/shard_map/ppermute | solution.py:458
  180.6 4.4 %placed_rows.2 = (f32[32768,128]{1,0:T(8,128)}, f32[256,128]{1,0:T(8,128)}) custom-call(s32[5,4]{1,0:T(8,128)S(1)} %multiply_add_fusion.refs_0_.table_ref, bf16[2112,128]{1,0:T(8,128)(2,1)S(1)} %new_rows.6.refs_0_, bf16[2112,128]{1,0:T(8,128)(2,1)S(1)} %collective-permute-done.3.refs_4_.refs_1_, ...), custom_call_target="tpu_custom_call", output_to_operand_aliasing={{0}: (9, {}), {1}: (10, {})} | custom-call | tf_op jit(solution)/shard_map/placed_rows/pallas_call | solution.py:428
  185.0 1.1 collective-permute-done.7.refs_1_
  186.1 5.4 %collective-permute-done.8.refs_2_ = bf16[1056,128]{1,0:T(8,128)(2,1)S(1)} collective-permute-done((bf16[1056,128]{1,0:T(8,128)(2,1)S(1)}, bf16[1056,128]{1,0:T(8,128)(2,1)S(1)}, u32[]{:S(2)}, u32[]{:S(2)}) %collective-permute-start.8) | collective-permute-done | bytes 270368 | tf_op jit(solution)/shard_map/ppermute | solution.py:458
  191.4 2.4 %placed_rows.3 = (f32[32768,128]{1,0:T(8,128)}, f32[256,128]{1,0:T(8,128)}) custom-call(s32[5,4]{1,0:T(8,128)S(1)} %multiply_add_fusion.refs_0_.table_ref, bf16[1056,128]{1,0:T(8,128)(2,1)S(1)} %get-tuple-element.18.refs_0_, bf16[1056,128]{1,0:T(8,128)(2,1)S(1)} %collective-permute-done.7.refs_1_, ...), custom_call_target="tpu_custom_call", output_to_operand_aliasing={{0}: (5, {}), {1}: (6, {})} | custom-call | tf_op jit(solution)/shard_map/placed_rows/pallas_call | solution.py:428
  (29 shorter events, 0.1 us)
Async XLA Ops:
  7.2 64.6 %all-gather.2.cloned.1.call-start = ((), (), s32[]{:S(2)}) async-start(), calls=%async_computation.1 | async-start | bytes 2621440 | tf_op jit(solution)/shard_map/all_gather | solution.py:480
  7.9 53.6 %copy-start.5 = (s32[5]{0:T(128)S(1)}, s32[5]{0:T(128)}, u32[]{:S(2)}) copy-start(s32[5]{0:T(128)} %constant.17) | copy-start | bytes 64
  7.9 53.6 %copy-start.6 = (s32[5]{0:T(128)S(1)}, s32[5]{0:T(128)}, u32[]{:S(2)}) copy-start(s32[5]{0:T(128)} %constant.18) | copy-start | bytes 64
  57.4 14.3 %all-to-all-start = ((f32[32,1,2048]{2,1,0:T(1,128)}), f32[32,1,2048]{2,1,0:T(1,128)S(1)}, u32[]{:S(2)}, u32[]{:S(2)}) async-start(f32[32,1,2048]{2,1,0:T(1,128)} %row_stats.1), calls=%async_computation | async-start | bytes 524288 | tf_op jit(solution)/shard_map/all_to_all | solution.py:482
  92.3 28.2 %copy-start.4 = (bf16[2112,128]{1,0:T(8,128)(2,1)}, bf16[2112,128]{1,0:T(8,128)(2,1)S(1)}, u32[]{:S(2)}) copy-start(bf16[2112,128]{1,0:T(8,128)(2,1)S(1)} %get-tuple-element.15.refs_7_) | copy-start | bytes 1622020
  92.3 26.0 %collective-permute-start = (bf16[2112,128]{1,0:T(8,128)(2,1)S(1)}, bf16[2112,128]{1,0:T(8,128)(2,1)S(1)}, u32[]{:S(2)}, u32[]{:S(2)}) collective-permute-start(bf16[2112,128]{1,0:T(8,128)(2,1)S(1)} %get-tuple-element.15.refs_7_), channel_id=1, source_target_pairs={{8,0},{0,8},{24,16},{16,24},{9,1},{1,9},{25,17},{17,25},{10,2},{2,... | collective-permute-start | bytes 1622024 | tf_op jit(solution)/shard_map/ppermute | solution.py:458
  92.9 27.6 %collective-permute-start.1 = (bf16[2112,128]{1,0:T(8,128)(2,1)S(1)}, bf16[2112,128]{1,0:T(8,128)(2,1)S(1)}, u32[]{:S(2)}, u32[]{:S(2)}) collective-permute-start(bf16[2112,128]{1,0:T(8,128)(2,1)S(1)} %get-tuple-element.15.refs_7_), channel_id=1, source_target_pairs={{16,0},{24,8},{0,16},{8,24},{17,1},{25,9},{1,17},{9,25},{18,2},{26... | collective-permute-start | bytes 1622024 | tf_op jit(solution)/shard_map/ppermute | solution.py:458
  93.7 26.8 %collective-permute-start.2 = (bf16[2112,128]{1,0:T(8,128)(2,1)S(1)}, bf16[2112,128]{1,0:T(8,128)(2,1)S(1)}, u32[]{:S(2)}, u32[]{:S(2)}) collective-permute-start(bf16[2112,128]{1,0:T(8,128)(2,1)S(1)} %get-tuple-element.15.refs_7_), channel_id=1, source_target_pairs={{24,0},{16,8},{8,16},{0,24},{25,1},{17,9},{9,17},{1,25},{26,2},{18... | collective-permute-start | bytes 1622024 | tf_op jit(solution)/shard_map/ppermute | solution.py:458
  116.9 42.2 %copy-start = (bf16[2112,128]{1,0:T(8,128)(2,1)}, bf16[2112,128]{1,0:T(8,128)(2,1)S(1)}, u32[]{:S(2)}) copy-start(bf16[2112,128]{1,0:T(8,128)(2,1)S(1)} %new_rows.7.refs_5_) | copy-start | bytes 1622020
  116.9 25.6 %collective-permute-start.4 = (bf16[2112,128]{1,0:T(8,128)(2,1)S(1)}, bf16[2112,128]{1,0:T(8,128)(2,1)}, u32[]{:S(2)}, u32[]{:S(2)}) collective-permute-start(bf16[2112,128]{1,0:T(8,128)(2,1)S(1)} %new_rows.7.refs_5_), channel_id=1, source_target_pairs={{8,0},{0,8},{24,16},{16,24},{9,1},{1,9},{25,17},{17,25},{10,2},{2,... | collective-permute-start | bytes 1622024 | tf_op jit(solution)/shard_map/ppermute | solution.py:458
  117.5 27.3 %collective-permute-start.5 = (bf16[2112,128]{1,0:T(8,128)(2,1)S(1)}, bf16[2112,128]{1,0:T(8,128)(2,1)}, u32[]{:S(2)}, u32[]{:S(2)}) collective-permute-start(bf16[2112,128]{1,0:T(8,128)(2,1)S(1)} %new_rows.7.refs_5_), channel_id=1, source_target_pairs={{16,0},{24,8},{0,16},{8,24},{17,1},{25,9},{1,17},{9,25},{18,2},{26... | collective-permute-start | bytes 1622024 | tf_op jit(solution)/shard_map/ppermute | solution.py:458
  118.3 26.4 %copy-start.1 = (bf16[2112,128]{1,0:T(8,128)(2,1)}, bf16[2112,128]{1,0:T(8,128)(2,1)S(1)}, u32[]{:S(2)}) copy-start(bf16[2112,128]{1,0:T(8,128)(2,1)S(1)} %collective-permute-done.refs_4_.refs_8_) | copy-start | bytes 1622020
  118.3 26.4 %collective-permute-start.6 = (bf16[2112,128]{1,0:T(8,128)(2,1)S(1)}, bf16[2112,128]{1,0:T(8,128)(2,1)}, u32[]{:S(2)}, u32[]{:S(2)}) collective-permute-start(bf16[2112,128]{1,0:T(8,128)(2,1)S(1)} %new_rows.7.refs_5_), channel_id=1, source_target_pairs={{24,0},{16,8},{8,16},{0,24},{25,1},{17,9},{9,17},{1,25},{26,2},{18... | collective-permute-start | bytes 1622024 | tf_op jit(solution)/shard_map/ppermute | solution.py:458
  120.5 24.3 %copy-start.2 = (bf16[2112,128]{1,0:T(8,128)(2,1)}, bf16[2112,128]{1,0:T(8,128)(2,1)S(1)}, u32[]{:S(2)}) copy-start(bf16[2112,128]{1,0:T(8,128)(2,1)S(1)} %collective-permute-done.1.refs_5_.refs_9_) | copy-start | bytes 1622020
  120.5 24.3 %copy-start.3 = (bf16[2112,128]{1,0:T(8,128)(2,1)}, bf16[2112,128]{1,0:T(8,128)(2,1)S(1)}, u32[]{:S(2)}) copy-start(bf16[2112,128]{1,0:T(8,128)(2,1)S(1)} %collective-permute-done.2.refs_6_.refs_10_) | copy-start | bytes 1622020
  141.2 19.3 %collective-permute-start.3 = (bf16[2112,128]{1,0:T(8,128)(2,1)S(1)}, bf16[2112,128]{1,0:T(8,128)(2,1)S(1)}, u32[]{:S(2)}, u32[]{:S(2)}) collective-permute-start(bf16[2112,128]{1,0:T(8,128)(2,1)S(1)} %new_rows.6.refs_0_), channel_id=1, source_target_pairs={{8,0},{0,8},{24,16},{16,24},{9,1},{1,9},{25,17},{17,25},{10,2},{2,... | collective-permute-start | bytes 1622024 | tf_op jit(solution)/shard_map/ppermute | solution.py:458
  141.7 38.8 %collective-permute-start.10 = (bf16[2112,128]{1,0:T(8,128)(2,1)S(1)}, bf16[2112,128]{1,0:T(8,128)(2,1)S(1)}, u32[]{:S(2)}, u32[]{:S(2)}) collective-permute-start(bf16[2112,128]{1,0:T(8,128)(2,1)S(1)} %new_rows.6.refs_0_), channel_id=1, source_target_pairs={{16,0},{24,8},{0,16},{8,24},{17,1},{25,9},{1,17},{9,25},{18,2},{26... | collective-permute-start | bytes 1622024 | tf_op jit(solution)/shard_map/ppermute | solution.py:458
  142.6 38.0 %collective-permute-start.11 = (bf16[2112,128]{1,0:T(8,128)(2,1)S(1)}, bf16[2112,128]{1,0:T(8,128)(2,1)S(1)}, u32[]{:S(2)}, u32[]{:S(2)}) collective-permute-start(bf16[2112,128]{1,0:T(8,128)(2,1)S(1)} %new_rows.6.refs_0_), channel_id=1, source_target_pairs={{24,0},{16,8},{8,16},{0,24},{25,1},{17,9},{9,17},{1,25},{26,2},{18... | collective-permute-start | bytes 1622024 | tf_op jit(solution)/shard_map/ppermute | solution.py:458
  159.1 17.9 %collective-permute-start.12 = (bf16[1056,128]{1,0:T(8,128)(2,1)S(1)}, bf16[1056,128]{1,0:T(8,128)(2,1)S(1)}, u32[]{:S(2)}, u32[]{:S(2)}) collective-permute-start(bf16[1056,128]{1,0:T(8,128)(2,1)S(1)} %get-tuple-element.19.refs_4_), channel_id=1, source_target_pairs={{8,0},{0,8},{24,16},{16,24},{9,1},{1,9},{25,17},{17,25},{10,2},{2,... | collective-permute-start | bytes 811016 | tf_op jit(solution)/shard_map/ppermute | solution.py:458
  159.6 17.9 %collective-permute-start.13 = (bf16[1056,128]{1,0:T(8,128)(2,1)S(1)}, bf16[1056,128]{1,0:T(8,128)(2,1)S(1)}, u32[]{:S(2)}, u32[]{:S(2)}) collective-permute-start(bf16[1056,128]{1,0:T(8,128)(2,1)S(1)} %get-tuple-element.19.refs_4_), channel_id=1, source_target_pairs={{16,0},{24,8},{0,16},{8,24},{17,1},{25,9},{1,17},{9,25},{18,2},{26... | collective-permute-start | bytes 811016 | tf_op jit(solution)/shard_map/ppermute | solution.py:458
  160.5 17.9 %collective-permute-start.14 = (bf16[1056,128]{1,0:T(8,128)(2,1)S(1)}, bf16[1056,128]{1,0:T(8,128)(2,1)S(1)}, u32[]{:S(2)}, u32[]{:S(2)}) collective-permute-start(bf16[1056,128]{1,0:T(8,128)(2,1)S(1)} %get-tuple-element.19.refs_4_), channel_id=1, source_target_pairs={{24,0},{16,8},{8,16},{0,24},{25,1},{17,9},{9,17},{1,25},{26,2},{18... | collective-permute-start | bytes 811016 | tf_op jit(solution)/shard_map/ppermute | solution.py:458
  177.0 9.1 %collective-permute-start.7 = (bf16[1056,128]{1,0:T(8,128)(2,1)S(1)}, bf16[1056,128]{1,0:T(8,128)(2,1)S(1)}, u32[]{:S(2)}, u32[]{:S(2)}) collective-permute-start(bf16[1056,128]{1,0:T(8,128)(2,1)S(1)} %get-tuple-element.18.refs_0_), channel_id=1, source_target_pairs={{8,0},{0,8},{24,16},{16,24},{9,1},{1,9},{25,17},{17,25},{10,2},{2,... | collective-permute-start | bytes 811016 | tf_op jit(solution)/shard_map/ppermute | solution.py:458
  177.5 13.9 %collective-permute-start.8 = (bf16[1056,128]{1,0:T(8,128)(2,1)S(1)}, bf16[1056,128]{1,0:T(8,128)(2,1)S(1)}, u32[]{:S(2)}, u32[]{:S(2)}) collective-permute-start(bf16[1056,128]{1,0:T(8,128)(2,1)S(1)} %get-tuple-element.18.refs_0_), channel_id=1, source_target_pairs={{16,0},{24,8},{0,16},{8,24},{17,1},{25,9},{1,17},{9,25},{18,2},{26... | collective-permute-start | bytes 811016 | tf_op jit(solution)/shard_map/ppermute | solution.py:458
  178.4 13.1 %collective-permute-start.9 = (bf16[1056,128]{1,0:T(8,128)(2,1)S(1)}, bf16[1056,128]{1,0:T(8,128)(2,1)S(1)}, u32[]{:S(2)}, u32[]{:S(2)}) collective-permute-start(bf16[1056,128]{1,0:T(8,128)(2,1)S(1)} %get-tuple-element.18.refs_0_), channel_id=1, source_target_pairs={{24,0},{16,8},{8,16},{0,24},{25,1},{17,9},{9,17},{1,25},{26,2},{18... | collective-permute-start | bytes 811016 | tf_op jit(solution)/shard_map/ppermute | solution.py:458
Sparse Core Ops, SparseCore 0:
  9.8 38.0 all-gather.1

commit v3 on v2

--- a/solution.py
+++ b/solution.py
@@ -262,7 +262,7 @@
         out_ref[:, t * count : (t + 1) * count] = top + jnp.log(total)
 
 
-def update_kernel(joins, unread, placed_chunk, pieces, block_rows, *refs):
+def update_kernel(chunk, joins, unread, placed_chunk, pieces, block_rows, *refs):
     table_ref, tok_ref, lse_ref, cent_ref = refs[:4]
     refs = refs[4 + unread :]
     code_refs, refs = refs[: sum(pieces)], refs[sum(pieces) :]
@@ -270,35 +270,42 @@
         code_ref, updated_ref, masses_ref = refs[2:5]
         scratch = refs[5:]
         outs = updated_ref, masses_ref
-        placing = Placing(block_rows, table_ref, placed_chunk, pieces, code_refs, outs, scratch[3:])
+        placing = Placing(block_rows, table_ref, placed_chunk, pieces, code_refs, outs, scratch[6:])
     else:
         code_ref, scratch, placing = refs[0], refs[1:], None
     if joins:
         parts_ref, lse_ref, scratch = lse_ref, scratch[0], scratch[1:]
-        pl.when(pl.program_id(0) == 0)(lambda: combine(joins, parts_ref, lse_ref))
-    weights_ref, total_ref, mass_ref = scratch[:3]
-    step, steps = pl.program_id(0), pl.num_programs(0)
-    width = tok_ref.shape[1]
+    weights_ref, total_ref, mass_ref, toks_ref, cents_ref, sems = scratch[:6]
+    rows, width = cents_ref.shape
     _, tile, depth = weights_ref.shape
     piece = divisor(depth, 512)
-    stages = tok_ref.shape[0] // depth
-    tiles = block_rows // tile
-
+    stages = toks_ref.shape[0] // depth
+    full = coded_rows(block_rows)
+
+    first_row = pl.multiple_of(table_ref[chunk, 0] * block_rows, block_rows)
+    loads = [pltpu.make_async_copy(cent_ref.at[pl.ds(first_row, rows), :], cents_ref, sems.at[0])]
+    for stage in range(stages):
+        span = pl.ds(stage * depth, depth)
+        loads.append(pltpu.make_async_copy(tok_ref.at[span, :], toks_ref.at[span, :], sems.at[1 + stage]))
+    for load in loads:
+        load.start()
     if placing:
-        pl.when(step == 0)(placing.fetch)
+        placing.fetch()
+    if joins:
+        combine(joins, parts_ref, lse_ref)
 
     def weigh(first, stage):
-        cents = cent_ref[pl.ds(first, tile), :] * jnp.bfloat16(inverse_temp)
+        cents = cents_ref[pl.ds(first, tile), :] * jnp.bfloat16(inverse_temp)
         for k in range(depth // piece):
             span = pl.ds(stage * depth + k * piece, piece)
-            logits = dot_nt(cents, tok_ref[span, :])
+            logits = dot_nt(cents, toks_ref[span, :])
             lse = lse_ref[:, span]
             for r in range(0, tile, slice_rows):
                 weights = jnp.exp(logits[r : r + slice_rows] - lse).astype(jnp.bfloat16)
                 weights_ref[stage % 2, r : r + slice_rows, pl.ds(k * piece, piece)] = weights
 
     def gather_up(stage):
-        toks = tok_ref[pl.ds(stage * depth, depth), :]
+        toks = toks_ref[pl.ds(stage * depth, depth), :]
         rhs = jnp.concatenate([toks, jnp.ones_like(toks)], axis=1)
         part = jnp.dot(weights_ref[stage % 2], rhs, preferred_element_type=jnp.float32)
         if stage == 0:
@@ -310,31 +317,37 @@
         jnp.int32, (128, 128), 1
     )
 
-    def run(r):
-        first = pl.multiple_of(r * tile, tile)
-        weigh(first, 0)
-        for stage in range(1, stages):
+    def run(r, waits):
+        first = r * tile
+        for stage in range(stages):
+            if waits:
+                waits[stage].wait()
             weigh(first, stage)
-            gather_up(stage - 1)
+            if stage:
+                gather_up(stage - 1)
         gather_up(stages - 1)
         mass = total_ref[:, width : 2 * width]
-        prior = prior_weight * cent_ref[pl.ds(first, tile), :].astype(jnp.float32)
+        prior = prior_weight * cents_ref[pl.ds(first, tile), :].astype(jnp.float32)
         new = (total_ref[:, 0:width] + prior) / (mass + prior_weight)
-        code_ref[pl.ds(first, tile), :] = encoded(new)
+        code_ref[pl.ds(first + first // block_rows * (full - block_rows), tile), :] = encoded(new)
         for k in range(tile // 128):
             square = jnp.where(diagonal, mass[k * 128 : (k + 1) * 128, :], 0.0)
-            mass_ref[pl.ds(r * (tile // 128) + k, 1), :] = jnp.sum(square, axis=0, keepdims=True)
-
-    pl.loop(0, tiles // 2)(run)
+            mass_ref[pl.ds(first // 128 + k, 1), :] = jnp.sum(square, axis=0, keepdims=True)
+
+    loads[0].wait()
+    for r in range(rows // tile):
+        run(r, () if r else loads[1:])
+        if placing and not r:
+            placing.place()
+
+    per_block = block_rows // 128
+    for block in range(rows // block_rows):
+        terms = split_exactly(mass_ref[block * per_block : (block + 1) * per_block, :])
+        terms = jnp.concatenate([*terms, jnp.zeros_like(terms[0])], axis=0)
+        last = block * full + block_rows
+        code_ref[last : last + terms.shape[0], :] = terms.astype(jnp.bfloat16)
     if placing:
-        pl.when(step == 0)(placing.place)
-    pl.loop(tiles // 2, tiles)(run)
-
-    terms = split_exactly(mass_ref[...])
-    terms = jnp.concatenate([*terms, jnp.zeros_like(terms[0])], axis=0)
-    code_ref[block_rows : block_rows + terms.shape[0], :] = terms.astype(jnp.bfloat16)
-    if placing:
-        pl.when(step == steps - 1)(placing.finish)
+        placing.finish()
 
 
 def updated_chunk(
@@ -354,16 +367,19 @@
         *after,
     ]
     in_specs = [
-        pl.BlockSpec((all_count, width), whole),
-        pl.BlockSpec(lse.shape, (lambda j, place: (0, 0, 0)) if joins else whole),
-        pl.BlockSpec((block_rows, width), lambda j, table: (table[chunk, 0] + j, 0)),
+        anywhere,
+        pl.BlockSpec(lse.shape, (lambda j, table: (0, 0, 0)) if joins else whole),
+        anywhere,
     ] + [anywhere] * len(after)
-    out_specs = [pl.BlockSpec((full, width), lambda j, place: (j, 0))]
+    out_specs = [pl.BlockSpec((blocks * full, width), whole)]
     out_shape = [jax.ShapeDtypeStruct((blocks * full, width), jnp.bfloat16)]
     scratch_shapes = [
         pltpu.VMEM((2, tile, depth), jnp.bfloat16),
         pltpu.VMEM((tile, 2 * width), jnp.float32),
-        pltpu.VMEM((block_rows // 128, 128), jnp.float32),
+        pltpu.VMEM((rows // 128, 128), jnp.float32),
+        pltpu.VMEM((all_count, width), jnp.bfloat16),
+        pltpu.VMEM((rows, width), jnp.bfloat16),
+        pltpu.SemaphoreType.DMA((1 + all_count // depth,)),
     ]
     aliases, pieces, placed_chunk = {}, [], None
     if joins:
@@ -380,10 +396,12 @@
         aliases = {len(operands) - 1: 1, len(operands): 2}
         scratch_shapes += Placing.scratch(len(codes), codes[0][0].shape[0] // full, block_rows, width)
     return pl.pallas_call(
-        functools.partial(update_kernel, joins, len(after), placed_chunk, pieces, block_rows),
+        functools.partial(
+            update_kernel, chunk, joins, len(after), placed_chunk, pieces, block_rows
+        ),
         grid_spec=pltpu.PrefetchScalarGridSpec(
             num_scalar_prefetch=1,
-            grid=(blocks,),
+            grid=(1,),
             in_specs=in_specs,
             out_specs=out_specs,
             scratch_shapes=scratch_shapes,

time: 204 us -> 210 us (1.029)
  Pallas kernels: 147 us -> 157 us
  waiting for transfers between devices: 17.4 us -> 14 us
    pallas_call x5, Pallas kernels: 90.8 us -> 100 us  [updated_chunk(): pl.pallas_call(functools.partial(update_kernel, chunk, joins, len(after),...]
    ppermute x15, waiting for transfers between devices: 6.47 us -> 3.65 us  [from_others(): found.append(lax.ppermute(value, axis, pairs))]
  transfers between devices with their start and end apart: 17 -> 17, of which waited for: 3 -> 3; matrix products, arithmetic and copies ran while one was open for 0% -> 0% of each run, Pallas kernels for 62% -> 64%
where the time goes in v3:
time: 210 us; the launch traced here: 208 us
  Pallas kernels  157 us (75%)
  starting transfers between devices  22 us (10%)
  between operations  14.4 us (7%)
  waiting for transfers between devices  14 us (7%)
    pallas_call x5, Pallas kernels, updated_chunk(): pl.pallas_call(functools.partial(update_kernel, chunk, joins, len(after),...  100 us
    pallas_call x1, Pallas kernels, local_lse(): pl.pallas_call(functools.partial(stats_kernel, sub_rows, tok_cols), grid=...  49.5 us
    ppermute x15, starting transfers between devices, from_others(): found.append(lax.ppermute(value, axis, pairs))  17.8 us
    all_to_all x1, waiting for transfers between devices, local(): parts = lax.all_to_all(own_lse, ('tok', 'cent'), 0, 0, tiled=True)  9.7 us
    pallas_call x2, Pallas kernels, placed(): pl.pallas_call(functools.partial(place_kernel, chunks, block_rows), grid_...  7.05 us
  transfers between devices with their start and end apart: 17, of which 3 were waited for; matrix products, arithmetic and copies ran while one was open for 0% of the time, Pallas kernels for 64%

profile of v3, /device:TPU:0, one launch (start us, length us, event | category | flops | bytes accessed | tf_op | source)
XLA Modules:
  0.0 207.5 jit_solution(8632323310521447502)
XLA Ops:
  7.2 0.0 all-gather.2.cloned.1.call-start
  7.2 0.7 all-gather.2.cloned.1.call-update
  7.9 0.0 copy-start.5
  7.9 49.5 %row_stats.1 = f32[32,1,2048]{2,1,0:T(1,128)} custom-call(bf16[2048,128]{1,0:T(8,128)(2,1)} %tok_ref.1, bf16[32768,128]{1,0:T(8,128)(2,1)} %refs_3_.9), custom_call_target="tpu_custom_call" | custom-call | flops 17179869184 | bytes 8912896 | tf_op jit(solution)/shard_map/row_stats/pallas_call | solution.py:141
  57.5 4.2 %all-to-all-start = ((f32[32,1,2048]{2,1,0:T(1,128)}), f32[32,1,2048]{2,1,0:T(1,128)S(1)}, u32[]{:S(2)}, u32[]{:S(2)}) async-start(f32[32,1,2048]{2,1,0:T(1,128)} %row_stats.1), calls=%async_computation | async-start | bytes 524288 | tf_op jit(solution)/shard_map/all_to_all | solution.py:500
  61.6 0.1 pad_add_fusion
  61.7 0.1 multiply_add_fusion.refs_0_.table_ref
  61.8 9.7 %all-to-all-done.refs_2_ = f32[32,1,2048]{2,1,0:T(1,128)S(1)} async-done(((f32[32,1,2048]{2,1,0:T(1,128)}), f32[32,1,2048]{2,1,0:T(1,128)S(1)}, u32[]{:S(2)}, u32[]{:S(2)}) %all-to-all-start) | async-done | bytes 262176 | tf_op jit(solution)/shard_map/all_to_all | solution.py:500
  71.5 22.4 %new_rows.5 = (bf16[2112,128]{1,0:T(8,128)(2,1)S(1)}, f32[1,8192]{1,0:T(1,128)S(1)}) custom-call(s32[5,4]{1,0:T(8,128)S(1)} %multiply_add_fusion.refs_0_.table_ref, bf16[8192,128]{1,0:T(8,128)(2,1)} %all-gather.2.cloned.1.call-done.refs_1_, f32[32,1,2048]{2,1,0:T(1,128)S(1)} %all-to-all-done.refs_2_, bf16[32768,128]{1,0:T(8,128)(2,1)} %refs_3_.9), custom_call_target="tpu_custom_call" | custom-call | flops 1610612736 | bytes 393216 | tf_op jit(solution)/shard_map/new_rows/pallas_call | solution.py:398
  93.9 0.6 collective-permute-start
  94.5 0.8 collective-permute-start.1
  95.3 2.2 %collective-permute-start.2 = (bf16[2112,128]{1,0:T(8,128)(2,1)S(1)}, bf16[2112,128]{1,0:T(8,128)(2,1)S(1)}, u32[]{:S(2)}, u32[]{:S(2)}) collective-permute-start(bf16[2112,128]{1,0:T(8,128)(2,1)S(1)} %get-tuple-element.15.refs_7_), channel_id=1, source_target_pairs={{24,0},{16,8},{8,16},{0,24},{25,1},{17,9},{9,17},{1,25},{26,2},{18... | collective-permute-start | bytes 1622024 | tf_op jit(solution)/shard_map/ppermute | solution.py:476
  97.5 22.9 %new_rows.7.refs_5_ = bf16[2112,128]{1,0:T(8,128)(2,1)S(1)} custom-call(s32[5,4]{1,0:T(8,128)S(1)} %multiply_add_fusion.refs_0_.table_ref, bf16[8192,128]{1,0:T(8,128)(2,1)} %all-gather.2.cloned.1.call-done.refs_1_, f32[1,8192]{1,0:T(1,128)S(1)} %get-tuple-element.14.refs_2_, bf16[32768,128]{1,0:T(8,128)(2,1)} %refs_3_.9), custom_call_target="tpu_custom_call" | custom-call | flops 1610612736 | bytes 393216 | tf_op jit(solution)/shard_map/new_rows/pallas_call | solution.py:398
  120.4 0.5 collective-permute-start.4
  120.9 0.8 collective-permute-start.5
  121.8 2.2 %collective-permute-start.6 = (bf16[2112,128]{1,0:T(8,128)(2,1)S(1)}, bf16[2112,128]{1,0:T(8,128)(2,1)}, u32[]{:S(2)}, u32[]{:S(2)}) collective-permute-start(bf16[2112,128]{1,0:T(8,128)(2,1)S(1)} %new_rows.7.refs_5_), channel_id=1, source_target_pairs={{24,0},{16,8},{8,16},{0,24},{25,1},{17,9},{9,17},{1,25},{26,2},{18... | collective-permute-start | bytes 1622024 | tf_op jit(solution)/shard_map/ppermute | solution.py:476
  124.0 22.4 %new_rows.6.refs_0_ = bf16[2112,128]{1,0:T(8,128)(2,1)S(1)} custom-call(s32[5,4]{1,0:T(8,128)S(1)} %multiply_add_fusion.refs_0_.table_ref, bf16[8192,128]{1,0:T(8,128)(2,1)} %all-gather.2.cloned.1.call-done.refs_1_, f32[1,8192]{1,0:T(1,128)S(1)} %get-tuple-element.14.refs_2_, bf16[32768,128]{1,0:T(8,128)(2,1)} %refs_3_.9, ...), custom_call_target="tpu_custom_call" | custom-call | flops 1610612736 | bytes 393216 | tf_op jit(solution)/shard_map/new_rows/pallas_call | solution.py:398
  146.4 0.5 collective-permute-start.3
  146.9 0.8 collective-permute-start.10
  147.8 2.2 %collective-permute-start.11 = (bf16[2112,128]{1,0:T(8,128)(2,1)S(1)}, bf16[2112,128]{1,0:T(8,128)(2,1)S(1)}, u32[]{:S(2)}, u32[]{:S(2)}) collective-permute-start(bf16[2112,128]{1,0:T(8,128)(2,1)S(1)} %new_rows.6.refs_0_), channel_id=1, source_target_pairs={{24,0},{16,8},{8,16},{0,24},{25,1},{17,9},{9,17},{1,25},{26,2},{18... | collective-permute-start | bytes 1622024 | tf_op jit(solution)/shard_map/ppermute | solution.py:476
  150.0 16.6 %new_rows.8 = (bf16[1056,128]{1,0:T(8,128)(2,1)S(1)}, f32[32768,128]{1,0:T(8,128)}, f32[256,128]{1,0:T(8,128)}) custom-call(s32[5,4]{1,0:T(8,128)S(1)} %multiply_add_fusion.refs_0_.table_ref, bf16[8192,128]{1,0:T(8,128)(2,1)} %all-gather.2.cloned.1.call-done.refs_1_, ...), custom_call_target="tpu_custom_call", output_to_operand_aliasing={{1}: (11, {}), {2}: (12, {})} | custom-call | flops 805306368 | bytes 327680 | tf_op jit(solution)/shard_map/new_rows/pallas_call | solution.py:398
  166.6 0.5 collective-permute-start.12
  167.2 0.8 collective-permute-start.13
  168.0 2.2 %collective-permute-start.14 = (bf16[1056,128]{1,0:T(8,128)(2,1)S(1)}, bf16[1056,128]{1,0:T(8,128)(2,1)S(1)}, u32[]{:S(2)}, u32[]{:S(2)}) collective-permute-start(bf16[1056,128]{1,0:T(8,128)(2,1)S(1)} %get-tuple-element.19.refs_4_), channel_id=1, source_target_pairs={{24,0},{16,8},{8,16},{0,24},{25,1},{17,9},{9,17},{1,25},{26,2},{18... | collective-permute-start | bytes 811016 | tf_op jit(solution)/shard_map/ppermute | solution.py:476
  170.2 16.0 %new_rows.9 = (bf16[1056,128]{1,0:T(8,128)(2,1)S(1)}, f32[32768,128]{1,0:T(8,128)}, f32[256,128]{1,0:T(8,128)}) custom-call(s32[5,4]{1,0:T(8,128)S(1)} %multiply_add_fusion.refs_0_.table_ref, bf16[8192,128]{1,0:T(8,128)(2,1)} %all-gather.2.cloned.1.call-done.refs_1_, ...), custom_call_target="tpu_custom_call", output_to_operand_aliasing={{1}: (9, {}), {2}: (10, {})} | custom-call | flops 805306368 | bytes 327680 | tf_op jit(solution)/shard_map/new_rows/pallas_call | solution.py:398
  186.2 0.5 collective-permute-start.7
  186.8 0.8 collective-permute-start.8
  187.6 2.2 %collective-permute-start.9 = (bf16[1056,128]{1,0:T(8,128)(2,1)S(1)}, bf16[1056,128]{1,0:T(8,128)(2,1)S(1)}, u32[]{:S(2)}, u32[]{:S(2)}) collective-permute-start(bf16[1056,128]{1,0:T(8,128)(2,1)S(1)} %get-tuple-element.18.refs_0_), channel_id=1, source_target_pairs={{24,0},{16,8},{8,16},{0,24},{25,1},{17,9},{9,17},{1,25},{26,2},{18... | collective-permute-start | bytes 811016 | tf_op jit(solution)/shard_map/ppermute | solution.py:476
  189.8 4.6 %placed_rows.2 = (f32[32768,128]{1,0:T(8,128)}, f32[256,128]{1,0:T(8,128)}) custom-call(s32[5,4]{1,0:T(8,128)S(1)} %multiply_add_fusion.refs_0_.table_ref, bf16[2112,128]{1,0:T(8,128)(2,1)S(1)} %new_rows.6.refs_0_, bf16[2112,128]{1,0:T(8,128)(2,1)S(1)} %collective-permute-done.3.refs_4_.refs_1_, ...), custom_call_target="tpu_custom_call", output_to_operand_aliasing={{0}: (9, {}), {1}: (10, {})} | custom-call | tf_op jit(solution)/shard_map/placed_rows/pallas_call | solution.py:446
  194.4 0.2 collective-permute-done.7.refs_1_
  194.6 3.5 %collective-permute-done.8.refs_2_ = bf16[1056,128]{1,0:T(8,128)(2,1)S(1)} collective-permute-done((bf16[1056,128]{1,0:T(8,128)(2,1)S(1)}, bf16[1056,128]{1,0:T(8,128)(2,1)S(1)}, u32[]{:S(2)}, u32[]{:S(2)}) %collective-permute-start.8) | collective-permute-done | bytes 270368 | tf_op jit(solution)/shard_map/ppermute | solution.py:476
  198.1 2.4 %placed_rows.3 = (f32[32768,128]{1,0:T(8,128)}, f32[256,128]{1,0:T(8,128)}) custom-call(s32[5,4]{1,0:T(8,128)S(1)} %multiply_add_fusion.refs_0_.table_ref, bf16[1056,128]{1,0:T(8,128)(2,1)S(1)} %get-tuple-element.18.refs_0_, bf16[1056,128]{1,0:T(8,128)(2,1)S(1)} %collective-permute-done.7.refs_1_, ...), custom_call_target="tpu_custom_call", output_to_operand_aliasing={{0}: (5, {}), {1}: (6, {})} | custom-call | tf_op jit(solution)/shard_map/placed_rows/pallas_call | solution.py:446
  (29 shorter events, 0.1 us)
Async XLA Ops:
  7.2 64.3 %all-gather.2.cloned.1.call-start = ((), (), s32[]{:S(2)}) async-start(), calls=%async_computation.1 | async-start | bytes 2621440 | tf_op jit(solution)/shard_map/all_gather | solution.py:498
  7.9 53.8 %copy-start.5 = (s32[5]{0:T(128)S(1)}, s32[5]{0:T(128)}, u32[]{:S(2)}) copy-start(s32[5]{0:T(128)} %constant.17) | copy-start | bytes 64
  7.9 53.8 %copy-start.6 = (s32[5]{0:T(128)S(1)}, s32[5]{0:T(128)}, u32[]{:S(2)}) copy-start(s32[5]{0:T(128)} %constant.18) | copy-start | bytes 64
  57.5 14.0 %all-to-all-start = ((f32[32,1,2048]{2,1,0:T(1,128)}), f32[32,1,2048]{2,1,0:T(1,128)S(1)}, u32[]{:S(2)}, u32[]{:S(2)}) async-start(f32[32,1,2048]{2,1,0:T(1,128)} %row_stats.1), calls=%async_computation | async-start | bytes 524288 | tf_op jit(solution)/shard_map/all_to_all | solution.py:500
  93.9 30.1 %copy-start.4 = (bf16[2112,128]{1,0:T(8,128)(2,1)}, bf16[2112,128]{1,0:T(8,128)(2,1)S(1)}, u32[]{:S(2)}) copy-start(bf16[2112,128]{1,0:T(8,128)(2,1)S(1)} %get-tuple-element.15.refs_7_) | copy-start | bytes 1622020
  93.9 27.9 %collective-permute-start = (bf16[2112,128]{1,0:T(8,128)(2,1)S(1)}, bf16[2112,128]{1,0:T(8,128)(2,1)S(1)}, u32[]{:S(2)}, u32[]{:S(2)}) collective-permute-start(bf16[2112,128]{1,0:T(8,128)(2,1)S(1)} %get-tuple-element.15.refs_7_), channel_id=1, source_target_pairs={{8,0},{0,8},{24,16},{16,24},{9,1},{1,9},{25,17},{17,25},{10,2},{2,... | collective-permute-start | bytes 1622024 | tf_op jit(solution)/shard_map/ppermute | solution.py:476
  94.5 29.5 %collective-permute-start.1 = (bf16[2112,128]{1,0:T(8,128)(2,1)S(1)}, bf16[2112,128]{1,0:T(8,128)(2,1)S(1)}, u32[]{:S(2)}, u32[]{:S(2)}) collective-permute-start(bf16[2112,128]{1,0:T(8,128)(2,1)S(1)} %get-tuple-element.15.refs_7_), channel_id=1, source_target_pairs={{16,0},{24,8},{0,16},{8,24},{17,1},{25,9},{1,17},{9,25},{18,2},{26... | collective-permute-start | bytes 1622024 | tf_op jit(solution)/shard_map/ppermute | solution.py:476
  95.3 28.6 %collective-permute-start.2 = (bf16[2112,128]{1,0:T(8,128)(2,1)S(1)}, bf16[2112,128]{1,0:T(8,128)(2,1)S(1)}, u32[]{:S(2)}, u32[]{:S(2)}) collective-permute-start(bf16[2112,128]{1,0:T(8,128)(2,1)S(1)} %get-tuple-element.15.refs_7_), channel_id=1, source_target_pairs={{24,0},{16,8},{8,16},{0,24},{25,1},{17,9},{9,17},{1,25},{26,2},{18... | collective-permute-start | bytes 1622024 | tf_op jit(solution)/shard_map/ppermute | solution.py:476
  120.4 46.3 %copy-start = (bf16[2112,128]{1,0:T(8,128)(2,1)}, bf16[2112,128]{1,0:T(8,128)(2,1)S(1)}, u32[]{:S(2)}) copy-start(bf16[2112,128]{1,0:T(8,128)(2,1)S(1)} %new_rows.7.refs_5_) | copy-start | bytes 1622020
  120.4 27.4 %collective-permute-start.4 = (bf16[2112,128]{1,0:T(8,128)(2,1)S(1)}, bf16[2112,128]{1,0:T(8,128)(2,1)}, u32[]{:S(2)}, u32[]{:S(2)}) collective-permute-start(bf16[2112,128]{1,0:T(8,128)(2,1)S(1)} %new_rows.7.refs_5_), channel_id=1, source_target_pairs={{8,0},{0,8},{24,16},{16,24},{9,1},{1,9},{25,17},{17,25},{10,2},{2,... | collective-permute-start | bytes 1622024 | tf_op jit(solution)/shard_map/ppermute | solution.py:476
  120.9 29.0 %collective-permute-start.5 = (bf16[2112,128]{1,0:T(8,128)(2,1)S(1)}, bf16[2112,128]{1,0:T(8,128)(2,1)}, u32[]{:S(2)}, u32[]{:S(2)}) collective-permute-start(bf16[2112,128]{1,0:T(8,128)(2,1)S(1)} %new_rows.7.refs_5_), channel_id=1, source_target_pairs={{16,0},{24,8},{0,16},{8,24},{17,1},{25,9},{1,17},{9,25},{18,2},{26... | collective-permute-start | bytes 1622024 | tf_op jit(solution)/shard_map/ppermute | solution.py:476
  121.8 28.2 %copy-start.1 = (bf16[2112,128]{1,0:T(8,128)(2,1)}, bf16[2112,128]{1,0:T(8,128)(2,1)S(1)}, u32[]{:S(2)}) copy-start(bf16[2112,128]{1,0:T(8,128)(2,1)S(1)} %collective-permute-done.refs_4_.refs_8_) | copy-start | bytes 1622020
  121.8 28.2 %collective-permute-start.6 = (bf16[2112,128]{1,0:T(8,128)(2,1)S(1)}, bf16[2112,128]{1,0:T(8,128)(2,1)}, u32[]{:S(2)}, u32[]{:S(2)}) collective-permute-start(bf16[2112,128]{1,0:T(8,128)(2,1)S(1)} %new_rows.7.refs_5_), channel_id=1, source_target_pairs={{24,0},{16,8},{8,16},{0,24},{25,1},{17,9},{9,17},{1,25},{26,2},{18... | collective-permute-start | bytes 1622024 | tf_op jit(solution)/shard_map/ppermute | solution.py:476
  123.9 26.0 %copy-start.2 = (bf16[2112,128]{1,0:T(8,128)(2,1)}, bf16[2112,128]{1,0:T(8,128)(2,1)S(1)}, u32[]{:S(2)}) copy-start(bf16[2112,128]{1,0:T(8,128)(2,1)S(1)} %collective-permute-done.1.refs_5_.refs_9_) | copy-start | bytes 1622020
  124.0 26.0 %copy-start.3 = (bf16[2112,128]{1,0:T(8,128)(2,1)}, bf16[2112,128]{1,0:T(8,128)(2,1)S(1)}, u32[]{:S(2)}) copy-start(bf16[2112,128]{1,0:T(8,128)(2,1)S(1)} %collective-permute-done.2.refs_6_.refs_10_) | copy-start | bytes 1622020
  146.4 21.6 %collective-permute-start.3 = (bf16[2112,128]{1,0:T(8,128)(2,1)S(1)}, bf16[2112,128]{1,0:T(8,128)(2,1)S(1)}, u32[]{:S(2)}, u32[]{:S(2)}) collective-permute-start(bf16[2112,128]{1,0:T(8,128)(2,1)S(1)} %new_rows.6.refs_0_), channel_id=1, source_target_pairs={{8,0},{0,8},{24,16},{16,24},{9,1},{1,9},{25,17},{17,25},{10,2},{2,... | collective-permute-start | bytes 1622024 | tf_op jit(solution)/shard_map/ppermute | solution.py:476
  146.9 42.9 %collective-permute-start.10 = (bf16[2112,128]{1,0:T(8,128)(2,1)S(1)}, bf16[2112,128]{1,0:T(8,128)(2,1)S(1)}, u32[]{:S(2)}, u32[]{:S(2)}) collective-permute-start(bf16[2112,128]{1,0:T(8,128)(2,1)S(1)} %new_rows.6.refs_0_), channel_id=1, source_target_pairs={{16,0},{24,8},{0,16},{8,24},{17,1},{25,9},{1,17},{9,25},{18,2},{26... | collective-permute-start | bytes 1622024 | tf_op jit(solution)/shard_map/ppermute | solution.py:476
  147.8 42.0 %collective-permute-start.11 = (bf16[2112,128]{1,0:T(8,128)(2,1)S(1)}, bf16[2112,128]{1,0:T(8,128)(2,1)S(1)}, u32[]{:S(2)}, u32[]{:S(2)}) collective-permute-start(bf16[2112,128]{1,0:T(8,128)(2,1)S(1)} %new_rows.6.refs_0_), channel_id=1, source_target_pairs={{24,0},{16,8},{8,16},{0,24},{25,1},{17,9},{9,17},{1,25},{26,2},{18... | collective-permute-start | bytes 1622024 | tf_op jit(solution)/shard_map/ppermute | solution.py:476
  166.6 19.6 %collective-permute-start.12 = (bf16[1056,128]{1,0:T(8,128)(2,1)S(1)}, bf16[1056,128]{1,0:T(8,128)(2,1)S(1)}, u32[]{:S(2)}, u32[]{:S(2)}) collective-permute-start(bf16[1056,128]{1,0:T(8,128)(2,1)S(1)} %get-tuple-element.19.refs_4_), channel_id=1, source_target_pairs={{8,0},{0,8},{24,16},{16,24},{9,1},{1,9},{25,17},{17,25},{10,2},{2,... | collective-permute-start | bytes 811016 | tf_op jit(solution)/shard_map/ppermute | solution.py:476
  167.2 19.6 %collective-permute-start.13 = (bf16[1056,128]{1,0:T(8,128)(2,1)S(1)}, bf16[1056,128]{1,0:T(8,128)(2,1)S(1)}, u32[]{:S(2)}, u32[]{:S(2)}) collective-permute-start(bf16[1056,128]{1,0:T(8,128)(2,1)S(1)} %get-tuple-element.19.refs_4_), channel_id=1, source_target_pairs={{16,0},{24,8},{0,16},{8,24},{17,1},{25,9},{1,17},{9,25},{18,2},{26... | collective-permute-start | bytes 811016 | tf_op jit(solution)/shard_map/ppermute | solution.py:476
  168.0 19.6 %collective-permute-start.14 = (bf16[1056,128]{1,0:T(8,128)(2,1)S(1)}, bf16[1056,128]{1,0:T(8,128)(2,1)S(1)}, u32[]{:S(2)}, u32[]{:S(2)}) collective-permute-start(bf16[1056,128]{1,0:T(8,128)(2,1)S(1)} %get-tuple-element.19.refs_4_), channel_id=1, source_target_pairs={{24,0},{16,8},{8,16},{0,24},{25,1},{17,9},{9,17},{1,25},{26,2},{18... | collective-permute-start | bytes 811016 | tf_op jit(solution)/shard_map/ppermute | solution.py:476
  186.2 8.4 %collective-permute-start.7 = (bf16[1056,128]{1,0:T(8,128)(2,1)S(1)}, bf16[1056,128]{1,0:T(8,128)(2,1)S(1)}, u32[]{:S(2)}, u32[]{:S(2)}) collective-permute-start(bf16[1056,128]{1,0:T(8,128)(2,1)S(1)} %get-tuple-element.18.refs_0_), channel_id=1, source_target_pairs={{8,0},{0,8},{24,16},{16,24},{9,1},{1,9},{25,17},{17,25},{10,2},{2,... | collective-permute-start | bytes 811016 | tf_op jit(solution)/shard_map/ppermute | solution.py:476
  186.8 11.3 %collective-permute-start.8 = (bf16[1056,128]{1,0:T(8,128)(2,1)S(1)}, bf16[1056,128]{1,0:T(8,128)(2,1)S(1)}, u32[]{:S(2)}, u32[]{:S(2)}) collective-permute-start(bf16[1056,128]{1,0:T(8,128)(2,1)S(1)} %get-tuple-element.18.refs_0_), channel_id=1, source_target_pairs={{16,0},{24,8},{0,16},{8,24},{17,1},{25,9},{1,17},{9,25},{18,2},{26... | collective-permute-start | bytes 811016 | tf_op jit(solution)/shard_map/ppermute | solution.py:476
  187.6 10.4 %collective-permute-start.9 = (bf16[1056,128]{1,0:T(8,128)(2,1)S(1)}, bf16[1056,128]{1,0:T(8,128)(2,1)S(1)}, u32[]{:S(2)}, u32[]{:S(2)}) collective-permute-start(bf16[1056,128]{1,0:T(8,128)(2,1)S(1)} %get-tuple-element.18.refs_0_), channel_id=1, source_target_pairs={{24,0},{16,8},{8,16},{0,24},{25,1},{17,9},{9,17},{1,25},{26,2},{18... | collective-permute-start | bytes 811016 | tf_op jit(solution)/shard_map/ppermute | solution.py:476
Sparse Core Ops, SparseCore 0:
  9.8 38.0 all-gather.1

commit v4 on v2

--- a/solution.py
+++ b/solution.py
@@ -464,11 +464,12 @@
 
 
 def chunk_plan(blocks):
-    plan = []
-    while blocks > 2:
-        plan.append(2)
-        blocks -= 2
-    return plan + [1] * blocks
+    plan = [1] if blocks > 1 else []
+    blocks -= len(plan)
+    while blocks:
+        plan.insert(0, min(blocks, 2 if blocks > 3 else 3))
+        blocks -= plan[0]
+    return plan
 
 
 def local(tokens, centroids):
@@ -491,10 +492,9 @@
     for k, blocks in enumerate(plan):
         arrived, received = [], None
         if len(waiting) > 1:
-            arrived = sum(waiting[-2][1][1:], [])
+            arrived = sum(waiting[-2][1][1:2], [])
             if blocks == 1:
                 received = (*waiting.pop(0), outs)
-                arrived = arrived[:1] if k + 1 == len(plan) else arrived
         operands = toks, lse if k else parts, centroids, blocks, block_rows, arrived, received
         codes, *rest = updated_chunk(table, k, *operands, joins=0 if k else tok_size)
         if not k:

time: 204 us -> 210 us (1.029)
  waiting for transfers between devices: 17.4 us -> 30.3 us
  Pallas kernels: 147 us -> 143 us
  starting transfers between devices: 21.8 us -> 18.3 us
    ppermute x15 -> x12, waiting for transfers between devices: 6.47 us -> 19.4 us  [from_others(): found.append(lax.ppermute(value, axis, pairs))]
    pallas_call x5 -> x4, Pallas kernels: 90.8 us -> 86.1 us  [updated_chunk(): pl.pallas_call(functools.partial(update_kernel, joins, len(after), placed...]
    ppermute x15 -> x12, starting transfers between devices: 17.8 us -> 14.1 us  [from_others(): found.append(lax.ppermute(value, axis, pairs))]
  transfers between devices with their start and end apart: 17 -> 14, of which waited for: 3 -> 5; matrix products, arithmetic and copies ran while one was open for 0% -> 0% of each run, Pallas kernels for 62% -> 54%
where the time goes in v4:
time: 210 us; the launch traced here: 207 us
  Pallas kernels  143 us (68%)
  waiting for transfers between devices  30.3 us (14%)
  starting transfers between devices  18.3 us (9%)
  between operations  14.4 us (7%)
    pallas_call x4, Pallas kernels, updated_chunk(): pl.pallas_call(functools.partial(update_kernel, joins, len(after), placed...  86.1 us
    pallas_call x1, Pallas kernels, local_lse(): pl.pallas_call(functools.partial(stats_kernel, sub_rows, tok_cols), grid=...  49.5 us
    ppermute x12, waiting for transfers between devices, from_others(): found.append(lax.ppermute(value, axis, pairs))  19.4 us
    ppermute x12, starting transfers between devices, from_others(): found.append(lax.ppermute(value, axis, pairs))  14.1 us
    all_to_all x1, waiting for transfers between devices, local(): parts = lax.all_to_all(own_lse, ('tok', 'cent'), 0, 0, tiled=True)  10.2 us
    pallas_call x2, Pallas kernels, placed(): pl.pallas_call(functools.partial(place_kernel, chunks, block_rows), grid_...  7.76 us
  transfers between devices with their start and end apart: 14, of which 5 were waited for; matrix products, arithmetic and copies ran while one was open for 0% of the time, Pallas kernels for 54%

profile of v4, /device:TPU:0, one launch (start us, length us, event | category | flops | bytes accessed | tf_op | source)
XLA Modules:
  0.0 207.4 jit_solution(9212355369419312502)
XLA Ops:
  7.2 0.0 all-gather.2.cloned.1.call-start
  7.2 0.7 all-gather.2.cloned.1.call-update
  7.9 0.0 copy-start.4
  7.9 0.0 copy-start.5
  7.9 49.5 %row_stats.1 = f32[32,1,2048]{2,1,0:T(1,128)} custom-call(bf16[2048,128]{1,0:T(8,128)(2,1)} %tok_ref.1, bf16[32768,128]{1,0:T(8,128)(2,1)} %refs_3_.7), custom_call_target="tpu_custom_call" | custom-call | flops 17179869184 | bytes 8912896 | tf_op jit(solution)/shard_map/row_stats/pallas_call | solution.py:141
  57.4 4.2 %all-to-all-start = ((f32[32,1,2048]{2,1,0:T(1,128)}), f32[32,1,2048]{2,1,0:T(1,128)S(1)}, u32[]{:S(2)}, u32[]{:S(2)}) async-start(f32[32,1,2048]{2,1,0:T(1,128)} %row_stats.1), calls=%async_computation | async-start | bytes 524288 | tf_op jit(solution)/shard_map/all_to_all | solution.py:483
  61.6 0.1 pad_add_fusion
  61.7 0.1 multiply_add_fusion.refs_0_.table_ref
  61.8 10.2 %all-to-all-done.refs_2_ = f32[32,1,2048]{2,1,0:T(1,128)S(1)} async-done(((f32[32,1,2048]{2,1,0:T(1,128)}), f32[32,1,2048]{2,1,0:T(1,128)S(1)}, u32[]{:S(2)}, u32[]{:S(2)}) %all-to-all-start) | async-done | bytes 262176 | tf_op jit(solution)/shard_map/all_to_all | solution.py:483
  72.0 29.6 %new_rows.4 = (bf16[3168,128]{1,0:T(8,128)(2,1)S(1)}, f32[1,8192]{1,0:T(1,128)S(1)}) custom-call(s32[4,4]{1,0:T(4,128)S(1)} %multiply_add_fusion.refs_0_.table_ref, bf16[8192,128]{1,0:T(8,128)(2,1)} %all-gather.2.cloned.1.call-done.refs_1_, f32[32,1,2048]{2,1,0:T(1,128)S(1)} %all-to-all-done.refs_2_, bf16[32768,128]{1,0:T(8,128)(2,1)} %refs_3_.7), custom_call_target="tpu_custom_call" | custom-call | flops 2415919104 | bytes 458752 | tf_op jit(solution)/shard_map/new_rows/pallas_call | solution.py:382
  101.6 0.6 collective-permute-start.1
  102.2 0.9 collective-permute-start.2
  103.0 2.2 %collective-permute-start.3 = (bf16[3168,128]{1,0:T(8,128)(2,1)S(1)}, bf16[3168,128]{1,0:T(8,128)(2,1)S(1)}, u32[]{:S(2)}, u32[]{:S(2)}) collective-permute-start(bf16[3168,128]{1,0:T(8,128)(2,1)S(1)} %get-tuple-element.12.refs_5_), channel_id=1, source_target_pairs={{24,0},{16,8},{8,16},{0,24},{25,1},{17,9},{9,17},{1,25},{26,2},{18... | collective-permute-start | bytes 2433032 | tf_op jit(solution)/shard_map/ppermute | solution.py:458
  105.2 20.6 %new_rows.5.refs_0_ = bf16[2112,128]{1,0:T(8,128)(2,1)S(1)} custom-call(s32[4,4]{1,0:T(4,128)S(1)} %multiply_add_fusion.refs_0_.table_ref, bf16[8192,128]{1,0:T(8,128)(2,1)} %all-gather.2.cloned.1.call-done.refs_1_, f32[1,8192]{1,0:T(1,128)S(1)} %get-tuple-element.11.refs_2_, bf16[32768,128]{1,0:T(8,128)(2,1)} %refs_3_.7), custom_call_target="tpu_custom_call" | custom-call | flops 1610612736 | bytes 393216 | tf_op jit(solution)/shard_map/new_rows/pallas_call | solution.py:382
  125.8 0.5 collective-permute-start
  126.3 0.9 collective-permute-start.7
  127.2 2.2 %collective-permute-start.8 = (bf16[2112,128]{1,0:T(8,128)(2,1)S(1)}, bf16[2112,128]{1,0:T(8,128)(2,1)}, u32[]{:S(2)}, u32[]{:S(2)}) collective-permute-start(bf16[2112,128]{1,0:T(8,128)(2,1)S(1)} %new_rows.5.refs_0_), channel_id=1, source_target_pairs={{24,0},{16,8},{8,16},{0,24},{25,1},{17,9},{9,17},{1,25},{26,2},{18... | collective-permute-start | bytes 1622024 | tf_op jit(solution)/shard_map/ppermute | solution.py:458
  129.4 20.7 %new_rows.7.refs_4_ = bf16[2112,128]{1,0:T(8,128)(2,1)S(1)} custom-call(s32[4,4]{1,0:T(4,128)S(1)} %multiply_add_fusion.refs_0_.table_ref, bf16[8192,128]{1,0:T(8,128)(2,1)} %all-gather.2.cloned.1.call-done.refs_1_, f32[1,8192]{1,0:T(1,128)S(1)} %get-tuple-element.11.refs_2_, bf16[32768,128]{1,0:T(8,128)(2,1)} %refs_3_.7, ...), custom_call_target="tpu_custom_call" | custom-call | flops 1610612736 | bytes 393216 | tf_op jit(solution)/shard_map/new_rows/pallas_call | solution.py:382
  150.0 1.6 collective-permute-done.refs_4_.refs_1_
  151.6 0.6 collective-permute-start.10
  152.2 1.4 collective-permute-start.11
  153.6 0.9 copy-done.3
  154.5 1.5 collective-permute-start.9
  156.0 15.2 %new_rows.6 = (bf16[1056,128]{1,0:T(8,128)(2,1)S(1)}, f32[32768,128]{1,0:T(8,128)}, f32[256,128]{1,0:T(8,128)}) custom-call(s32[4,4]{1,0:T(4,128)S(1)} %multiply_add_fusion.refs_0_.table_ref, bf16[8192,128]{1,0:T(8,128)(2,1)} %all-gather.2.cloned.1.call-done.refs_1_, ...), custom_call_target="tpu_custom_call", output_to_operand_aliasing={{1}: (9, {}), {2}: (10, {})} | custom-call | flops 805306368 | bytes 327680 | tf_op jit(solution)/shard_map/new_rows/pallas_call | solution.py:382
  171.2 3.7 %collective-permute-done.7.refs_2_ = bf16[2112,128]{1,0:T(8,128)(2,1)} collective-permute-done((bf16[2112,128]{1,0:T(8,128)(2,1)S(1)}, bf16[2112,128]{1,0:T(8,128)(2,1)}, u32[]{:S(2)}, u32[]{:S(2)}) %collective-permute-start.7) | collective-permute-done | bytes 540704 | tf_op jit(solution)/shard_map/ppermute | solution.py:458
  174.9 1.8 collective-permute-start.4
  176.8 0.2 collective-permute-start.5
  177.0 9.6 %collective-permute-done.10.refs_6_ = bf16[2112,128]{1,0:T(8,128)(2,1)} collective-permute-done((bf16[2112,128]{1,0:T(8,128)(2,1)S(1)}, bf16[2112,128]{1,0:T(8,128)(2,1)}, u32[]{:S(2)}, u32[]{:S(2)}) %collective-permute-start.10) | collective-permute-done | bytes 540704 | tf_op jit(solution)/shard_map/ppermute | solution.py:458
  186.5 1.4 collective-permute-start.6
  188.0 5.4 %placed_rows.2 = (f32[32768,128]{1,0:T(8,128)}, f32[256,128]{1,0:T(8,128)}) custom-call(s32[4,4]{1,0:T(4,128)S(1)} %multiply_add_fusion.refs_0_.table_ref, bf16[2112,128]{1,0:T(8,128)(2,1)S(1)} %new_rows.5.refs_0_, bf16[2112,128]{1,0:T(8,128)(2,1)S(1)} %collective-permute-done.refs_4_.refs_1_, ...), custom_call_target="tpu_custom_call", output_to_operand_aliasing={{0}: (9, {}), {1}: (10, {})} | custom-call | tf_op jit(solution)/shard_map/placed_rows/pallas_call | solution.py:428
  193.4 4.5 %collective-permute-done.5.refs_2_ = bf16[1056,128]{1,0:T(8,128)(2,1)S(1)} collective-permute-done((bf16[1056,128]{1,0:T(8,128)(2,1)S(1)}, bf16[1056,128]{1,0:T(8,128)(2,1)S(1)}, u32[]{:S(2)}, u32[]{:S(2)}) %collective-permute-start.5) | collective-permute-done | bytes 270368 | tf_op jit(solution)/shard_map/ppermute | solution.py:458
  197.9 2.4 %placed_rows.3 = (f32[32768,128]{1,0:T(8,128)}, f32[256,128]{1,0:T(8,128)}) custom-call(s32[4,4]{1,0:T(4,128)S(1)} %multiply_add_fusion.refs_0_.table_ref, bf16[1056,128]{1,0:T(8,128)(2,1)S(1)} %get-tuple-element.13.refs_0_, bf16[1056,128]{1,0:T(8,128)(2,1)S(1)} %collective-permute-done.4.refs_1_, ...), custom_call_target="tpu_custom_call", output_to_operand_aliasing={{0}: (5, {}), {1}: (6, {})} | custom-call | tf_op jit(solution)/shard_map/placed_rows/pallas_call | solution.py:428
  (20 shorter events, 0.0 us)
Async XLA Ops:
  7.2 64.8 %all-gather.2.cloned.1.call-start = ((), (), s32[]{:S(2)}) async-start(), calls=%async_computation.1 | async-start | bytes 2621440 | tf_op jit(solution)/shard_map/all_gather | solution.py:481
  7.9 53.8 %copy-start.4 = (s32[4]{0:T(128)S(1)}, s32[4]{0:T(128)}, u32[]{:S(2)}) copy-start(s32[4]{0:T(128)} %constant.17) | copy-start | bytes 52
  7.9 53.8 %copy-start.5 = (s32[4]{0:T(128)S(1)}, s32[4]{0:T(128)}, u32[]{:S(2)}) copy-start(s32[4]{0:T(128)} %constant.18) | copy-start | bytes 52
  57.4 14.5 %all-to-all-start = ((f32[32,1,2048]{2,1,0:T(1,128)}), f32[32,1,2048]{2,1,0:T(1,128)S(1)}, u32[]{:S(2)}, u32[]{:S(2)}) async-start(f32[32,1,2048]{2,1,0:T(1,128)} %row_stats.1), calls=%async_computation | async-start | bytes 524288 | tf_op jit(solution)/shard_map/all_to_all | solution.py:483
  101.6 54.4 %copy-start.1 = (bf16[3168,128]{1,0:T(8,128)(2,1)}, bf16[3168,128]{1,0:T(8,128)(2,1)S(1)}, u32[]{:S(2)}) copy-start(bf16[3168,128]{1,0:T(8,128)(2,1)S(1)} %get-tuple-element.12.refs_5_) | copy-start | bytes 2433028
  101.6 25.6 %collective-permute-start.1 = (bf16[3168,128]{1,0:T(8,128)(2,1)S(1)}, bf16[3168,128]{1,0:T(8,128)(2,1)S(1)}, u32[]{:S(2)}, u32[]{:S(2)}) collective-permute-start(bf16[3168,128]{1,0:T(8,128)(2,1)S(1)} %get-tuple-element.12.refs_5_), channel_id=1, source_target_pairs={{8,0},{0,8},{24,16},{16,24},{9,1},{1,9},{25,17},{17,25},{10,2},{2,... | collective-permute-start | bytes 2433032 | tf_op jit(solution)/shard_map/ppermute | solution.py:458
  102.2 50.0 %collective-permute-start.2 = (bf16[3168,128]{1,0:T(8,128)(2,1)S(1)}, bf16[3168,128]{1,0:T(8,128)(2,1)S(1)}, u32[]{:S(2)}, u32[]{:S(2)}) collective-permute-start(bf16[3168,128]{1,0:T(8,128)(2,1)S(1)} %get-tuple-element.12.refs_5_), channel_id=1, source_target_pairs={{16,0},{24,8},{0,16},{8,24},{17,1},{25,9},{1,17},{9,25},{18,2},{26... | collective-permute-start | bytes 2433032 | tf_op jit(solution)/shard_map/ppermute | solution.py:458
  103.0 50.6 %collective-permute-start.3 = (bf16[3168,128]{1,0:T(8,128)(2,1)S(1)}, bf16[3168,128]{1,0:T(8,128)(2,1)S(1)}, u32[]{:S(2)}, u32[]{:S(2)}) collective-permute-start(bf16[3168,128]{1,0:T(8,128)(2,1)S(1)} %get-tuple-element.12.refs_5_), channel_id=1, source_target_pairs={{24,0},{16,8},{8,16},{0,24},{25,1},{17,9},{9,17},{1,25},{26,2},{18... | collective-permute-start | bytes 2433032 | tf_op jit(solution)/shard_map/ppermute | solution.py:458
  125.8 25.8 %collective-permute-start = (bf16[2112,128]{1,0:T(8,128)(2,1)S(1)}, bf16[2112,128]{1,0:T(8,128)(2,1)S(1)}, u32[]{:S(2)}, u32[]{:S(2)}) collective-permute-start(bf16[2112,128]{1,0:T(8,128)(2,1)S(1)} %new_rows.5.refs_0_), channel_id=1, source_target_pairs={{8,0},{0,8},{24,16},{16,24},{9,1},{1,9},{25,17},{17,25},{10,2},{2,... | collective-permute-start | bytes 1622024 | tf_op jit(solution)/shard_map/ppermute | solution.py:458
  126.3 48.6 %collective-permute-start.7 = (bf16[2112,128]{1,0:T(8,128)(2,1)S(1)}, bf16[2112,128]{1,0:T(8,128)(2,1)}, u32[]{:S(2)}, u32[]{:S(2)}) collective-permute-start(bf16[2112,128]{1,0:T(8,128)(2,1)S(1)} %new_rows.5.refs_0_), channel_id=1, source_target_pairs={{16,0},{24,8},{0,16},{8,24},{17,1},{25,9},{1,17},{9,25},{18,2},{26... | collective-permute-start | bytes 1622024 | tf_op jit(solution)/shard_map/ppermute | solution.py:458
  127.2 28.8 %copy-start = (bf16[3168,128]{1,0:T(8,128)(2,1)}, bf16[3168,128]{1,0:T(8,128)(2,1)S(1)}, u32[]{:S(2)}) copy-start(bf16[3168,128]{1,0:T(8,128)(2,1)S(1)} %collective-permute-done.1.refs_6_.refs_4_) | copy-start | bytes 2433028
  127.2 49.6 %collective-permute-start.8 = (bf16[2112,128]{1,0:T(8,128)(2,1)S(1)}, bf16[2112,128]{1,0:T(8,128)(2,1)}, u32[]{:S(2)}, u32[]{:S(2)}) collective-permute-start(bf16[2112,128]{1,0:T(8,128)(2,1)S(1)} %new_rows.5.refs_0_), channel_id=1, source_target_pairs={{24,0},{16,8},{8,16},{0,24},{25,1},{17,9},{9,17},{1,25},{26,2},{18... | collective-permute-start | bytes 1622024 | tf_op jit(solution)/shard_map/ppermute | solution.py:458
  151.6 34.9 %collective-permute-start.10 = (bf16[2112,128]{1,0:T(8,128)(2,1)S(1)}, bf16[2112,128]{1,0:T(8,128)(2,1)}, u32[]{:S(2)}, u32[]{:S(2)}) collective-permute-start(bf16[2112,128]{1,0:T(8,128)(2,1)S(1)} %new_rows.7.refs_4_), channel_id=1, source_target_pairs={{16,0},{24,8},{0,16},{8,24},{17,1},{25,9},{1,17},{9,25},{18,2},{26... | collective-permute-start | bytes 1622024 | tf_op jit(solution)/shard_map/ppermute | solution.py:458
  152.2 1.4 copy-start.2
  152.2 35.8 %collective-permute-start.11 = (bf16[2112,128]{1,0:T(8,128)(2,1)S(1)}, bf16[2112,128]{1,0:T(8,128)(2,1)}, u32[]{:S(2)}, u32[]{:S(2)}) collective-permute-start(bf16[2112,128]{1,0:T(8,128)(2,1)S(1)} %new_rows.7.refs_4_), channel_id=1, source_target_pairs={{24,0},{16,8},{8,16},{0,24},{25,1},{17,9},{9,17},{1,25},{26,2},{18... | collective-permute-start | bytes 1622024 | tf_op jit(solution)/shard_map/ppermute | solution.py:458
  153.6 0.9 copy-start.3
  154.5 33.5 %collective-permute-start.9 = (bf16[2112,128]{1,0:T(8,128)(2,1)S(1)}, bf16[2112,128]{1,0:T(8,128)(2,1)}, u32[]{:S(2)}, u32[]{:S(2)}) collective-permute-start(bf16[2112,128]{1,0:T(8,128)(2,1)S(1)} %new_rows.7.refs_4_), channel_id=1, source_target_pairs={{8,0},{0,8},{24,16},{16,24},{9,1},{1,9},{25,17},{17,25},{10,2},{2,... | collective-permute-start | bytes 1622024 | tf_op jit(solution)/shard_map/ppermute | solution.py:458
  174.9 18.4 %collective-permute-start.4 = (bf16[1056,128]{1,0:T(8,128)(2,1)S(1)}, bf16[1056,128]{1,0:T(8,128)(2,1)S(1)}, u32[]{:S(2)}, u32[]{:S(2)}) collective-permute-start(bf16[1056,128]{1,0:T(8,128)(2,1)S(1)} %get-tuple-element.13.refs_0_), channel_id=1, source_target_pairs={{8,0},{0,8},{24,16},{16,24},{9,1},{1,9},{25,17},{17,25},{10,2},{2,... | collective-permute-start | bytes 811016 | tf_op jit(solution)/shard_map/ppermute | solution.py:458
  176.8 21.1 %collective-permute-start.5 = (bf16[1056,128]{1,0:T(8,128)(2,1)S(1)}, bf16[1056,128]{1,0:T(8,128)(2,1)S(1)}, u32[]{:S(2)}, u32[]{:S(2)}) collective-permute-start(bf16[1056,128]{1,0:T(8,128)(2,1)S(1)} %get-tuple-element.13.refs_0_), channel_id=1, source_target_pairs={{16,0},{24,8},{0,16},{8,24},{17,1},{25,9},{1,17},{9,25},{18,2},{26... | collective-permute-start | bytes 811016 | tf_op jit(solution)/shard_map/ppermute | solution.py:458
  186.5 11.4 %collective-permute-start.6 = (bf16[1056,128]{1,0:T(8,128)(2,1)S(1)}, bf16[1056,128]{1,0:T(8,128)(2,1)S(1)}, u32[]{:S(2)}, u32[]{:S(2)}) collective-permute-start(bf16[1056,128]{1,0:T(8,128)(2,1)S(1)} %get-tuple-element.13.refs_0_), channel_id=1, source_target_pairs={{24,0},{16,8},{8,16},{0,24},{25,1},{17,9},{9,17},{1,25},{26,2},{18... | collective-permute-start | bytes 811016 | tf_op jit(solution)/shard_map/ppermute | solution.py:458
Sparse Core Ops, SparseCore 0:
  9.8 38.0 all-gather.1

commit v5 on v2

--- a/solution.py
+++ b/solution.py
@@ -290,21 +290,19 @@
     def weigh(first, stage):
         cents = cent_ref[pl.ds(first, tile), :] * jnp.bfloat16(inverse_temp)
         for k in range(depth // piece):
-            span = pl.ds(stage * depth + k * piece, piece)
+            span = pl.ds(pl.multiple_of(stage * depth + k * piece, piece), piece)
             logits = dot_nt(cents, tok_ref[span, :])
             lse = lse_ref[:, span]
             for r in range(0, tile, slice_rows):
                 weights = jnp.exp(logits[r : r + slice_rows] - lse).astype(jnp.bfloat16)
-                weights_ref[stage % 2, r : r + slice_rows, pl.ds(k * piece, piece)] = weights
+                weights_ref[lax.rem(stage, 2), r : r + slice_rows, pl.ds(k * piece, piece)] = weights
 
     def gather_up(stage):
-        toks = tok_ref[pl.ds(stage * depth, depth), :]
+        toks = tok_ref[pl.ds(pl.multiple_of(stage * depth, depth), depth), :]
         rhs = jnp.concatenate([toks, jnp.ones_like(toks)], axis=1)
-        part = jnp.dot(weights_ref[stage % 2], rhs, preferred_element_type=jnp.float32)
-        if stage == 0:
-            total_ref[...] = part
-        else:
-            total_ref[...] += part
+        total_ref[...] += jnp.dot(
+            weights_ref[lax.rem(stage, 2)], rhs, preferred_element_type=jnp.float32
+        )
 
     diagonal = lax.broadcasted_iota(jnp.int32, (128, 128), 0) == lax.broadcasted_iota(
         jnp.int32, (128, 128), 1
@@ -312,11 +310,15 @@
 
     def run(r):
         first = pl.multiple_of(r * tile, tile)
-        weigh(first, 0)
-        for stage in range(1, stages):
+        weigh(first, jnp.int32(0))
+        total_ref[...] = jnp.zeros_like(total_ref)
+
+        @pl.loop(1, stages)
+        def _(stage):
             weigh(first, stage)
             gather_up(stage - 1)
-        gather_up(stages - 1)
+
+        gather_up(jnp.int32(stages - 1))
         mass = total_ref[:, width : 2 * width]
         prior = prior_weight * cent_ref[pl.ds(first, tile), :].astype(jnp.float32)
         new = (total_ref[:, 0:width] + prior) / (mass + prior_weight)

time: 204 us -> 213 us (1.044); the launches traced: 201 us -> 213 us
  Pallas kernels: 147 us -> 162 us
  waiting for transfers between devices: 17.4 us -> 14.5 us
    pallas_call x5, Pallas kernels: 90.8 us -> 106 us  [updated_chunk(): pl.pallas_call(functools.partial(update_kernel, joins, len(after), placed...]
    ppermute x15, waiting for transfers between devices: 6.47 us -> 3.8 us  [from_others(): found.append(lax.ppermute(value, axis, pairs))]
  transfers between devices with their start and end apart: 17 -> 17, of which waited for: 3 -> 3; matrix products, arithmetic and copies ran while one was open for 0% -> 0% of each run, Pallas kernels for 62% -> 63%
where the time goes in v5:
time: 213 us
  Pallas kernels  162 us (76%)
  starting transfers between devices  22.1 us (10%)
  waiting for transfers between devices  14.5 us (7%)
  between operations  14.2 us (7%)
    pallas_call x5, Pallas kernels, updated_chunk(): pl.pallas_call(functools.partial(update_kernel, joins, len(after), placed...  106 us
    pallas_call x1, Pallas kernels, local_lse(): pl.pallas_call(functools.partial(stats_kernel, sub_rows, tok_cols), grid=...  49 us
    ppermute x15, starting transfers between devices, from_others(): found.append(lax.ppermute(value, axis, pairs))  17.8 us
    all_to_all x1, waiting for transfers between devices, local(): parts = lax.all_to_all(own_lse, ('tok', 'cent'), 0, 0, tiled=True)  10 us
    pallas_call x2, Pallas kernels, placed(): pl.pallas_call(functools.partial(place_kernel, chunks, block_rows), grid_...  6.88 us
    all_to_all x1, starting transfers between devices, local(): parts = lax.all_to_all(own_lse, ('tok', 'cent'), 0, 0, tiled=True)  4.31 us
  transfers between devices with their start and end apart: 17, of which 3 were waited for; matrix products, arithmetic and copies ran while one was open for 0% of the time, Pallas kernels for 63%

profile of v5, /device:TPU:0, one launch (start us, length us, event | category | flops | bytes accessed | tf_op | source)
XLA Modules:
  0.0 212.8 jit_solution(5436763492772397385)
XLA Ops:
  7.2 0.0 all-gather.2.cloned.1.call-start
  7.2 0.7 all-gather.2.cloned.1.call-update
  7.9 0.0 copy-start.5
  7.9 49.0 %row_stats.1 = f32[32,1,2048]{2,1,0:T(1,128)} custom-call(bf16[2048,128]{1,0:T(8,128)(2,1)} %tok_ref.1, bf16[32768,128]{1,0:T(8,128)(2,1)} %refs_3_.9), custom_call_target="tpu_custom_call" | custom-call | flops 17179869184 | bytes 8912896 | tf_op jit(solution)/shard_map/row_stats/pallas_call | solution.py:141
  57.0 4.3 %all-to-all-start = ((f32[32,1,2048]{2,1,0:T(1,128)}), f32[32,1,2048]{2,1,0:T(1,128)S(1)}, u32[]{:S(2)}, u32[]{:S(2)}) async-start(f32[32,1,2048]{2,1,0:T(1,128)} %row_stats.1), calls=%async_computation | async-start | bytes 524288 | tf_op jit(solution)/shard_map/all_to_all | solution.py:484
  61.3 0.1 pad_add_fusion
  61.4 0.1 multiply_add_fusion.refs_0_.table_ref
  61.4 10.0 %all-to-all-done.refs_2_ = f32[32,1,2048]{2,1,0:T(1,128)S(1)} async-done(((f32[32,1,2048]{2,1,0:T(1,128)}), f32[32,1,2048]{2,1,0:T(1,128)S(1)}, u32[]{:S(2)}, u32[]{:S(2)}) %all-to-all-start) | async-done | bytes 262176 | tf_op jit(solution)/shard_map/all_to_all | solution.py:484
  71.5 24.5 %new_rows.5 = (bf16[2112,128]{1,0:T(8,128)(2,1)S(1)}, f32[1,8192]{1,0:T(1,128)S(1)}) custom-call(s32[5,4]{1,0:T(8,128)S(1)} %multiply_add_fusion.refs_0_.table_ref, bf16[8192,128]{1,0:T(8,128)(2,1)} %all-gather.2.cloned.1.call-done.refs_1_, f32[32,1,2048]{2,1,0:T(1,128)S(1)} %all-to-all-done.refs_2_, bf16[32768,128]{1,0:T(8,128)(2,1)} %refs_3_.9), custom_call_target="tpu_custom_call" | custom-call | flops 1610612736 | bytes 393216 | tf_op jit(solution)/shard_map/new_rows/pallas_call | solution.py:384
  96.0 0.6 collective-permute-start
  96.6 0.8 collective-permute-start.1
  97.4 2.2 %collective-permute-start.2 = (bf16[2112,128]{1,0:T(8,128)(2,1)S(1)}, bf16[2112,128]{1,0:T(8,128)(2,1)S(1)}, u32[]{:S(2)}, u32[]{:S(2)}) collective-permute-start(bf16[2112,128]{1,0:T(8,128)(2,1)S(1)} %get-tuple-element.15.refs_7_), channel_id=1, source_target_pairs={{24,0},{16,8},{8,16},{0,24},{25,1},{17,9},{9,17},{1,25},{26,2},{18... | collective-permute-start | bytes 1622024 | tf_op jit(solution)/shard_map/ppermute | solution.py:460
  99.6 24.4 %new_rows.7.refs_5_ = bf16[2112,128]{1,0:T(8,128)(2,1)S(1)} custom-call(s32[5,4]{1,0:T(8,128)S(1)} %multiply_add_fusion.refs_0_.table_ref, bf16[8192,128]{1,0:T(8,128)(2,1)} %all-gather.2.cloned.1.call-done.refs_1_, f32[1,8192]{1,0:T(1,128)S(1)} %get-tuple-element.14.refs_2_, bf16[32768,128]{1,0:T(8,128)(2,1)} %refs_3_.9), custom_call_target="tpu_custom_call" | custom-call | flops 1610612736 | bytes 393216 | tf_op jit(solution)/shard_map/new_rows/pallas_call | solution.py:384
  124.0 0.5 collective-permute-start.4
  124.5 0.8 collective-permute-start.5
  125.3 2.2 %collective-permute-start.6 = (bf16[2112,128]{1,0:T(8,128)(2,1)S(1)}, bf16[2112,128]{1,0:T(8,128)(2,1)}, u32[]{:S(2)}, u32[]{:S(2)}) collective-permute-start(bf16[2112,128]{1,0:T(8,128)(2,1)S(1)} %new_rows.7.refs_5_), channel_id=1, source_target_pairs={{24,0},{16,8},{8,16},{0,24},{25,1},{17,9},{9,17},{1,25},{26,2},{18... | collective-permute-start | bytes 1622024 | tf_op jit(solution)/shard_map/ppermute | solution.py:460
  127.6 24.6 %new_rows.6.refs_0_ = bf16[2112,128]{1,0:T(8,128)(2,1)S(1)} custom-call(s32[5,4]{1,0:T(8,128)S(1)} %multiply_add_fusion.refs_0_.table_ref, bf16[8192,128]{1,0:T(8,128)(2,1)} %all-gather.2.cloned.1.call-done.refs_1_, f32[1,8192]{1,0:T(1,128)S(1)} %get-tuple-element.14.refs_2_, bf16[32768,128]{1,0:T(8,128)(2,1)} %refs_3_.9, ...), custom_call_target="tpu_custom_call" | custom-call | flops 1610612736 | bytes 393216 | tf_op jit(solution)/shard_map/new_rows/pallas_call | solution.py:384
  152.1 0.6 collective-permute-start.3
  152.7 0.8 collective-permute-start.10
  153.5 2.2 %collective-permute-start.11 = (bf16[2112,128]{1,0:T(8,128)(2,1)S(1)}, bf16[2112,128]{1,0:T(8,128)(2,1)S(1)}, u32[]{:S(2)}, u32[]{:S(2)}) collective-permute-start(bf16[2112,128]{1,0:T(8,128)(2,1)S(1)} %new_rows.6.refs_0_), channel_id=1, source_target_pairs={{24,0},{16,8},{8,16},{0,24},{25,1},{17,9},{9,17},{1,25},{26,2},{18... | collective-permute-start | bytes 1622024 | tf_op jit(solution)/shard_map/ppermute | solution.py:460
  155.7 16.1 %new_rows.8 = (bf16[1056,128]{1,0:T(8,128)(2,1)S(1)}, f32[32768,128]{1,0:T(8,128)}, f32[256,128]{1,0:T(8,128)}) custom-call(s32[5,4]{1,0:T(8,128)S(1)} %multiply_add_fusion.refs_0_.table_ref, bf16[8192,128]{1,0:T(8,128)(2,1)} %all-gather.2.cloned.1.call-done.refs_1_, ...), custom_call_target="tpu_custom_call", output_to_operand_aliasing={{1}: (11, {}), {2}: (12, {})} | custom-call | flops 805306368 | bytes 327680 | tf_op jit(solution)/shard_map/new_rows/pallas_call | solution.py:384
  171.8 0.6 collective-permute-start.12
  172.4 0.8 collective-permute-start.13
  173.2 2.2 %collective-permute-start.14 = (bf16[1056,128]{1,0:T(8,128)(2,1)S(1)}, bf16[1056,128]{1,0:T(8,128)(2,1)S(1)}, u32[]{:S(2)}, u32[]{:S(2)}) collective-permute-start(bf16[1056,128]{1,0:T(8,128)(2,1)S(1)} %get-tuple-element.19.refs_4_), channel_id=1, source_target_pairs={{24,0},{16,8},{8,16},{0,24},{25,1},{17,9},{9,17},{1,25},{26,2},{18... | collective-permute-start | bytes 811016 | tf_op jit(solution)/shard_map/ppermute | solution.py:460
  175.4 16.3 %new_rows.9 = (bf16[1056,128]{1,0:T(8,128)(2,1)S(1)}, f32[32768,128]{1,0:T(8,128)}, f32[256,128]{1,0:T(8,128)}) custom-call(s32[5,4]{1,0:T(8,128)S(1)} %multiply_add_fusion.refs_0_.table_ref, bf16[8192,128]{1,0:T(8,128)(2,1)} %all-gather.2.cloned.1.call-done.refs_1_, ...), custom_call_target="tpu_custom_call", output_to_operand_aliasing={{1}: (9, {}), {2}: (10, {})} | custom-call | flops 805306368 | bytes 327680 | tf_op jit(solution)/shard_map/new_rows/pallas_call | solution.py:384
  191.7 0.6 collective-permute-start.7
  192.3 0.8 collective-permute-start.8
  193.1 2.2 %collective-permute-start.9 = (bf16[1056,128]{1,0:T(8,128)(2,1)S(1)}, bf16[1056,128]{1,0:T(8,128)(2,1)S(1)}, u32[]{:S(2)}, u32[]{:S(2)}) collective-permute-start(bf16[1056,128]{1,0:T(8,128)(2,1)S(1)} %get-tuple-element.18.refs_0_), channel_id=1, source_target_pairs={{24,0},{16,8},{8,16},{0,24},{25,1},{17,9},{9,17},{1,25},{26,2},{18... | collective-permute-start | bytes 811016 | tf_op jit(solution)/shard_map/ppermute | solution.py:460
  195.3 4.4 %placed_rows.2 = (f32[32768,128]{1,0:T(8,128)}, f32[256,128]{1,0:T(8,128)}) custom-call(s32[5,4]{1,0:T(8,128)S(1)} %multiply_add_fusion.refs_0_.table_ref, bf16[2112,128]{1,0:T(8,128)(2,1)S(1)} %new_rows.6.refs_0_, bf16[2112,128]{1,0:T(8,128)(2,1)S(1)} %collective-permute-done.3.refs_4_.refs_1_, ...), custom_call_target="tpu_custom_call", output_to_operand_aliasing={{0}: (9, {}), {1}: (10, {})} | custom-call | tf_op jit(solution)/shard_map/placed_rows/pallas_call | solution.py:430
  199.8 0.3 collective-permute-done.7.refs_1_
  200.1 3.5 %collective-permute-done.8.refs_2_ = bf16[1056,128]{1,0:T(8,128)(2,1)S(1)} collective-permute-done((bf16[1056,128]{1,0:T(8,128)(2,1)S(1)}, bf16[1056,128]{1,0:T(8,128)(2,1)S(1)}, u32[]{:S(2)}, u32[]{:S(2)}) %collective-permute-start.8) | collective-permute-done | bytes 270368 | tf_op jit(solution)/shard_map/ppermute | solution.py:460
  203.5 2.4 %placed_rows.3 = (f32[32768,128]{1,0:T(8,128)}, f32[256,128]{1,0:T(8,128)}) custom-call(s32[5,4]{1,0:T(8,128)S(1)} %multiply_add_fusion.refs_0_.table_ref, bf16[1056,128]{1,0:T(8,128)(2,1)S(1)} %get-tuple-element.18.refs_0_, bf16[1056,128]{1,0:T(8,128)(2,1)S(1)} %collective-permute-done.7.refs_1_, ...), custom_call_target="tpu_custom_call", output_to_operand_aliasing={{0}: (5, {}), {1}: (6, {})} | custom-call | tf_op jit(solution)/shard_map/placed_rows/pallas_call | solution.py:430
  (29 shorter events, 0.1 us)
Async XLA Ops:
  7.2 64.3 %all-gather.2.cloned.1.call-start = ((), (), s32[]{:S(2)}) async-start(), calls=%async_computation.1 | async-start | bytes 2621440 | tf_op jit(solution)/shard_map/all_gather | solution.py:482
  7.9 53.5 %copy-start.5 = (s32[5]{0:T(128)S(1)}, s32[5]{0:T(128)}, u32[]{:S(2)}) copy-start(s32[5]{0:T(128)} %constant.17) | copy-start | bytes 64
  7.9 53.4 %copy-start.6 = (s32[5]{0:T(128)S(1)}, s32[5]{0:T(128)}, u32[]{:S(2)}) copy-start(s32[5]{0:T(128)} %constant.18) | copy-start | bytes 64
  57.0 14.5 %all-to-all-start = ((f32[32,1,2048]{2,1,0:T(1,128)}), f32[32,1,2048]{2,1,0:T(1,128)S(1)}, u32[]{:S(2)}, u32[]{:S(2)}) async-start(f32[32,1,2048]{2,1,0:T(1,128)} %row_stats.1), calls=%async_computation | async-start | bytes 524288 | tf_op jit(solution)/shard_map/all_to_all | solution.py:484
  96.0 31.6 %copy-start.4 = (bf16[2112,128]{1,0:T(8,128)(2,1)}, bf16[2112,128]{1,0:T(8,128)(2,1)S(1)}, u32[]{:S(2)}) copy-start(bf16[2112,128]{1,0:T(8,128)(2,1)S(1)} %get-tuple-element.15.refs_7_) | copy-start | bytes 1622020
  96.0 29.3 %collective-permute-start = (bf16[2112,128]{1,0:T(8,128)(2,1)S(1)}, bf16[2112,128]{1,0:T(8,128)(2,1)S(1)}, u32[]{:S(2)}, u32[]{:S(2)}) collective-permute-start(bf16[2112,128]{1,0:T(8,128)(2,1)S(1)} %get-tuple-element.15.refs_7_), channel_id=1, source_target_pairs={{8,0},{0,8},{24,16},{16,24},{9,1},{1,9},{25,17},{17,25},{10,2},{2,... | collective-permute-start | bytes 1622024 | tf_op jit(solution)/shard_map/ppermute | solution.py:460
  96.6 31.0 %collective-permute-start.1 = (bf16[2112,128]{1,0:T(8,128)(2,1)S(1)}, bf16[2112,128]{1,0:T(8,128)(2,1)S(1)}, u32[]{:S(2)}, u32[]{:S(2)}) collective-permute-start(bf16[2112,128]{1,0:T(8,128)(2,1)S(1)} %get-tuple-element.15.refs_7_), channel_id=1, source_target_pairs={{16,0},{24,8},{0,16},{8,24},{17,1},{25,9},{1,17},{9,25},{18,2},{26... | collective-permute-start | bytes 1622024 | tf_op jit(solution)/shard_map/ppermute | solution.py:460
  97.4 30.1 %collective-permute-start.2 = (bf16[2112,128]{1,0:T(8,128)(2,1)S(1)}, bf16[2112,128]{1,0:T(8,128)(2,1)S(1)}, u32[]{:S(2)}, u32[]{:S(2)}) collective-permute-start(bf16[2112,128]{1,0:T(8,128)(2,1)S(1)} %get-tuple-element.15.refs_7_), channel_id=1, source_target_pairs={{24,0},{16,8},{8,16},{0,24},{25,1},{17,9},{9,17},{1,25},{26,2},{18... | collective-permute-start | bytes 1622024 | tf_op jit(solution)/shard_map/ppermute | solution.py:460
  124.0 47.9 %copy-start = (bf16[2112,128]{1,0:T(8,128)(2,1)}, bf16[2112,128]{1,0:T(8,128)(2,1)S(1)}, u32[]{:S(2)}) copy-start(bf16[2112,128]{1,0:T(8,128)(2,1)S(1)} %new_rows.7.refs_5_) | copy-start | bytes 1622020
  124.0 29.6 %collective-permute-start.4 = (bf16[2112,128]{1,0:T(8,128)(2,1)S(1)}, bf16[2112,128]{1,0:T(8,128)(2,1)}, u32[]{:S(2)}, u32[]{:S(2)}) collective-permute-start(bf16[2112,128]{1,0:T(8,128)(2,1)S(1)} %new_rows.7.refs_5_), channel_id=1, source_target_pairs={{8,0},{0,8},{24,16},{16,24},{9,1},{1,9},{25,17},{17,25},{10,2},{2,... | collective-permute-start | bytes 1622024 | tf_op jit(solution)/shard_map/ppermute | solution.py:460
  124.5 31.2 %collective-permute-start.5 = (bf16[2112,128]{1,0:T(8,128)(2,1)S(1)}, bf16[2112,128]{1,0:T(8,128)(2,1)}, u32[]{:S(2)}, u32[]{:S(2)}) collective-permute-start(bf16[2112,128]{1,0:T(8,128)(2,1)S(1)} %new_rows.7.refs_5_), channel_id=1, source_target_pairs={{16,0},{24,8},{0,16},{8,24},{17,1},{25,9},{1,17},{9,25},{18,2},{26... | collective-permute-start | bytes 1622024 | tf_op jit(solution)/shard_map/ppermute | solution.py:460
  125.3 30.4 %copy-start.1 = (bf16[2112,128]{1,0:T(8,128)(2,1)}, bf16[2112,128]{1,0:T(8,128)(2,1)S(1)}, u32[]{:S(2)}) copy-start(bf16[2112,128]{1,0:T(8,128)(2,1)S(1)} %collective-permute-done.refs_4_.refs_8_) | copy-start | bytes 1622020
  125.3 30.4 %collective-permute-start.6 = (bf16[2112,128]{1,0:T(8,128)(2,1)S(1)}, bf16[2112,128]{1,0:T(8,128)(2,1)}, u32[]{:S(2)}, u32[]{:S(2)}) collective-permute-start(bf16[2112,128]{1,0:T(8,128)(2,1)S(1)} %new_rows.7.refs_5_), channel_id=1, source_target_pairs={{24,0},{16,8},{8,16},{0,24},{25,1},{17,9},{9,17},{1,25},{26,2},{18... | collective-permute-start | bytes 1622024 | tf_op jit(solution)/shard_map/ppermute | solution.py:460
  127.5 28.2 %copy-start.2 = (bf16[2112,128]{1,0:T(8,128)(2,1)}, bf16[2112,128]{1,0:T(8,128)(2,1)S(1)}, u32[]{:S(2)}) copy-start(bf16[2112,128]{1,0:T(8,128)(2,1)S(1)} %collective-permute-done.1.refs_5_.refs_9_) | copy-start | bytes 1622020
  127.6 28.2 %copy-start.3 = (bf16[2112,128]{1,0:T(8,128)(2,1)}, bf16[2112,128]{1,0:T(8,128)(2,1)S(1)}, u32[]{:S(2)}) copy-start(bf16[2112,128]{1,0:T(8,128)(2,1)S(1)} %collective-permute-done.2.refs_6_.refs_10_) | copy-start | bytes 1622020
  152.1 21.1 %collective-permute-start.3 = (bf16[2112,128]{1,0:T(8,128)(2,1)S(1)}, bf16[2112,128]{1,0:T(8,128)(2,1)S(1)}, u32[]{:S(2)}, u32[]{:S(2)}) collective-permute-start(bf16[2112,128]{1,0:T(8,128)(2,1)S(1)} %new_rows.6.refs_0_), channel_id=1, source_target_pairs={{8,0},{0,8},{24,16},{16,24},{9,1},{1,9},{25,17},{17,25},{10,2},{2,... | collective-permute-start | bytes 1622024 | tf_op jit(solution)/shard_map/ppermute | solution.py:460
  152.7 42.6 %collective-permute-start.10 = (bf16[2112,128]{1,0:T(8,128)(2,1)S(1)}, bf16[2112,128]{1,0:T(8,128)(2,1)S(1)}, u32[]{:S(2)}, u32[]{:S(2)}) collective-permute-start(bf16[2112,128]{1,0:T(8,128)(2,1)S(1)} %new_rows.6.refs_0_), channel_id=1, source_target_pairs={{16,0},{24,8},{0,16},{8,24},{17,1},{25,9},{1,17},{9,25},{18,2},{26... | collective-permute-start | bytes 1622024 | tf_op jit(solution)/shard_map/ppermute | solution.py:460
  153.5 41.8 %collective-permute-start.11 = (bf16[2112,128]{1,0:T(8,128)(2,1)S(1)}, bf16[2112,128]{1,0:T(8,128)(2,1)S(1)}, u32[]{:S(2)}, u32[]{:S(2)}) collective-permute-start(bf16[2112,128]{1,0:T(8,128)(2,1)S(1)} %new_rows.6.refs_0_), channel_id=1, source_target_pairs={{24,0},{16,8},{8,16},{0,24},{25,1},{17,9},{9,17},{1,25},{26,2},{18... | collective-permute-start | bytes 1622024 | tf_op jit(solution)/shard_map/ppermute | solution.py:460
  171.8 19.9 %collective-permute-start.12 = (bf16[1056,128]{1,0:T(8,128)(2,1)S(1)}, bf16[1056,128]{1,0:T(8,128)(2,1)S(1)}, u32[]{:S(2)}, u32[]{:S(2)}) collective-permute-start(bf16[1056,128]{1,0:T(8,128)(2,1)S(1)} %get-tuple-element.19.refs_4_), channel_id=1, source_target_pairs={{8,0},{0,8},{24,16},{16,24},{9,1},{1,9},{25,17},{17,25},{10,2},{2,... | collective-permute-start | bytes 811016 | tf_op jit(solution)/shard_map/ppermute | solution.py:460
  172.4 19.9 %collective-permute-start.13 = (bf16[1056,128]{1,0:T(8,128)(2,1)S(1)}, bf16[1056,128]{1,0:T(8,128)(2,1)S(1)}, u32[]{:S(2)}, u32[]{:S(2)}) collective-permute-start(bf16[1056,128]{1,0:T(8,128)(2,1)S(1)} %get-tuple-element.19.refs_4_), channel_id=1, source_target_pairs={{16,0},{24,8},{0,16},{8,24},{17,1},{25,9},{1,17},{9,25},{18,2},{26... | collective-permute-start | bytes 811016 | tf_op jit(solution)/shard_map/ppermute | solution.py:460
  173.2 19.9 %collective-permute-start.14 = (bf16[1056,128]{1,0:T(8,128)(2,1)S(1)}, bf16[1056,128]{1,0:T(8,128)(2,1)S(1)}, u32[]{:S(2)}, u32[]{:S(2)}) collective-permute-start(bf16[1056,128]{1,0:T(8,128)(2,1)S(1)} %get-tuple-element.19.refs_4_), channel_id=1, source_target_pairs={{24,0},{16,8},{8,16},{0,24},{25,1},{17,9},{9,17},{1,25},{26,2},{18... | collective-permute-start | bytes 811016 | tf_op jit(solution)/shard_map/ppermute | solution.py:460
  191.7 8.3 %collective-permute-start.7 = (bf16[1056,128]{1,0:T(8,128)(2,1)S(1)}, bf16[1056,128]{1,0:T(8,128)(2,1)S(1)}, u32[]{:S(2)}, u32[]{:S(2)}) collective-permute-start(bf16[1056,128]{1,0:T(8,128)(2,1)S(1)} %get-tuple-element.18.refs_0_), channel_id=1, source_target_pairs={{8,0},{0,8},{24,16},{16,24},{9,1},{1,9},{25,17},{17,25},{10,2},{2,... | collective-permute-start | bytes 811016 | tf_op jit(solution)/shard_map/ppermute | solution.py:460
  192.3 11.2 %collective-permute-start.8 = (bf16[1056,128]{1,0:T(8,128)(2,1)S(1)}, bf16[1056,128]{1,0:T(8,128)(2,1)S(1)}, u32[]{:S(2)}, u32[]{:S(2)}) collective-permute-start(bf16[1056,128]{1,0:T(8,128)(2,1)S(1)} %get-tuple-element.18.refs_0_), channel_id=1, source_target_pairs={{16,0},{24,8},{0,16},{8,24},{17,1},{25,9},{1,17},{9,25},{18,2},{26... | collective-permute-start | bytes 811016 | tf_op jit(solution)/shard_map/ppermute | solution.py:460
  193.1 10.4 %collective-permute-start.9 = (bf16[1056,128]{1,0:T(8,128)(2,1)S(1)}, bf16[1056,128]{1,0:T(8,128)(2,1)S(1)}, u32[]{:S(2)}, u32[]{:S(2)}) collective-permute-start(bf16[1056,128]{1,0:T(8,128)(2,1)S(1)} %get-tuple-element.18.refs_0_), channel_id=1, source_target_pairs={{24,0},{16,8},{8,16},{0,24},{25,1},{17,9},{9,17},{1,25},{26,2},{18... | collective-permute-start | bytes 811016 | tf_op jit(solution)/shard_map/ppermute | solution.py:460
Sparse Core Ops, SparseCore 0:
  9.8 38.0 all-gather.1

commit v6 on v2

--- a/solution.py
+++ b/solution.py
@@ -341,7 +341,7 @@
     table, chunk, toks, lse, centroids, blocks, block_rows, after=(), received=None, joins=0
 ):
     all_count, width = toks.shape
-    depth = divisor(all_count, 2048)
+    depth = divisor(all_count, 1024)
     tile = divisor(block_rows, 1024)
     rows = blocks * block_rows
     full = coded_rows(block_rows)

time: 204 us -> 204 us (level)
  no operation moved by 1% of the time
where the time goes in v6:
time: 204 us; the launch traced here: 201 us
  Pallas kernels  147 us (72%)
  starting transfers between devices  21.8 us (11%)
  waiting for transfers between devices  17.4 us (9%)
  between operations  14.7 us (7%)
    pallas_call x5, Pallas kernels, updated_chunk(): pl.pallas_call(functools.partial(update_kernel, joins, len(after), placed...  90.8 us
    pallas_call x1, Pallas kernels, local_lse(): pl.pallas_call(functools.partial(stats_kernel, sub_rows, tok_cols), grid=...  49.5 us
    ppermute x15, starting transfers between devices, from_others(): found.append(lax.ppermute(value, axis, pairs))  17.8 us
    all_to_all x1, waiting for transfers between devices, local(): parts = lax.all_to_all(own_lse, ('tok', 'cent'), 0, 0, tiled=True)  10.2 us
    pallas_call x2, Pallas kernels, placed(): pl.pallas_call(functools.partial(place_kernel, chunks, block_rows), grid_...  6.88 us
    ppermute x15, waiting for transfers between devices, from_others(): found.append(lax.ppermute(value, axis, pairs))  6.46 us
  transfers between devices with their start and end apart: 17, of which 3 were waited for; matrix products, arithmetic and copies ran while one was open for 0% of the time, Pallas kernels for 62%

profile of v6, /device:TPU:0, one launch (start us, length us, event | category | flops | bytes accessed | tf_op | source)
XLA Modules:
  0.0 201.2 jit_solution(17165735035212895671)
XLA Ops:
  7.2 0.0 all-gather.2.cloned.1.call-start
  7.2 0.7 all-gather.2.cloned.1.call-update
  7.9 0.0 copy-start.6
  7.9 49.5 %row_stats.1 = f32[32,1,2048]{2,1,0:T(1,128)} custom-call(bf16[2048,128]{1,0:T(8,128)(2,1)} %tok_ref.1, bf16[32768,128]{1,0:T(8,128)(2,1)} %refs_3_.9), custom_call_target="tpu_custom_call" | custom-call | flops 17179869184 | bytes 8912896 | tf_op jit(solution)/shard_map/row_stats/pallas_call | solution.py:141
  57.4 3.9 %all-to-all-start = ((f32[32,1,2048]{2,1,0:T(1,128)}), f32[32,1,2048]{2,1,0:T(1,128)S(1)}, u32[]{:S(2)}, u32[]{:S(2)}) async-start(f32[32,1,2048]{2,1,0:T(1,128)} %row_stats.1), calls=%async_computation | async-start | bytes 524288 | tf_op jit(solution)/shard_map/all_to_all | solution.py:482
  61.4 0.1 pad_add_fusion
  61.5 0.1 multiply_add_fusion.refs_0_.table_ref
  61.5 10.2 %all-to-all-done.refs_2_ = f32[32,1,2048]{2,1,0:T(1,128)S(1)} async-done(((f32[32,1,2048]{2,1,0:T(1,128)}), f32[32,1,2048]{2,1,0:T(1,128)S(1)}, u32[]{:S(2)}, u32[]{:S(2)}) %all-to-all-start) | async-done | bytes 262176 | tf_op jit(solution)/shard_map/all_to_all | solution.py:482
  71.7 20.5 %new_rows.5 = (bf16[2112,128]{1,0:T(8,128)(2,1)S(1)}, f32[1,8192]{1,0:T(1,128)S(1)}) custom-call(s32[5,4]{1,0:T(8,128)S(1)} %multiply_add_fusion.refs_0_.table_ref, bf16[8192,128]{1,0:T(8,128)(2,1)} %all-gather.2.cloned.1.call-done.refs_1_, f32[32,1,2048]{2,1,0:T(1,128)S(1)} %all-to-all-done.refs_2_, bf16[32768,128]{1,0:T(8,128)(2,1)} %refs_3_.9), custom_call_target="tpu_custom_call" | custom-call | flops 1610612736 | bytes 393216 | tf_op jit(solution)/shard_map/new_rows/pallas_call | solution.py:382
  92.3 0.6 collective-permute-start
  92.9 0.8 collective-permute-start.1
  93.7 2.2 %collective-permute-start.2 = (bf16[2112,128]{1,0:T(8,128)(2,1)S(1)}, bf16[2112,128]{1,0:T(8,128)(2,1)S(1)}, u32[]{:S(2)}, u32[]{:S(2)}) collective-permute-start(bf16[2112,128]{1,0:T(8,128)(2,1)S(1)} %get-tuple-element.15.refs_7_), channel_id=1, source_target_pairs={{24,0},{16,8},{8,16},{0,24},{25,1},{17,9},{9,17},{1,25},{26,2},{18... | collective-permute-start | bytes 1622024 | tf_op jit(solution)/shard_map/ppermute | solution.py:458
  95.9 21.0 %new_rows.7.refs_5_ = bf16[2112,128]{1,0:T(8,128)(2,1)S(1)} custom-call(s32[5,4]{1,0:T(8,128)S(1)} %multiply_add_fusion.refs_0_.table_ref, bf16[8192,128]{1,0:T(8,128)(2,1)} %all-gather.2.cloned.1.call-done.refs_1_, f32[1,8192]{1,0:T(1,128)S(1)} %get-tuple-element.14.refs_2_, bf16[32768,128]{1,0:T(8,128)(2,1)} %refs_3_.9), custom_call_target="tpu_custom_call" | custom-call | flops 1610612736 | bytes 393216 | tf_op jit(solution)/shard_map/new_rows/pallas_call | solution.py:382
  116.9 0.6 collective-permute-start.4
  117.5 0.8 collective-permute-start.5
  118.3 2.2 %collective-permute-start.6 = (bf16[2112,128]{1,0:T(8,128)(2,1)S(1)}, bf16[2112,128]{1,0:T(8,128)(2,1)}, u32[]{:S(2)}, u32[]{:S(2)}) collective-permute-start(bf16[2112,128]{1,0:T(8,128)(2,1)S(1)} %new_rows.7.refs_5_), channel_id=1, source_target_pairs={{24,0},{16,8},{8,16},{0,24},{25,1},{17,9},{9,17},{1,25},{26,2},{18... | collective-permute-start | bytes 1622024 | tf_op jit(solution)/shard_map/ppermute | solution.py:458
  120.5 20.7 %new_rows.6.refs_0_ = bf16[2112,128]{1,0:T(8,128)(2,1)S(1)} custom-call(s32[5,4]{1,0:T(8,128)S(1)} %multiply_add_fusion.refs_0_.table_ref, bf16[8192,128]{1,0:T(8,128)(2,1)} %all-gather.2.cloned.1.call-done.refs_1_, f32[1,8192]{1,0:T(1,128)S(1)} %get-tuple-element.14.refs_2_, bf16[32768,128]{1,0:T(8,128)(2,1)} %refs_3_.9, ...), custom_call_target="tpu_custom_call" | custom-call | flops 1610612736 | bytes 393216 | tf_op jit(solution)/shard_map/new_rows/pallas_call | solution.py:382
  141.2 0.6 collective-permute-start.3
  141.7 0.8 collective-permute-start.10
  142.6 2.2 %collective-permute-start.11 = (bf16[2112,128]{1,0:T(8,128)(2,1)S(1)}, bf16[2112,128]{1,0:T(8,128)(2,1)S(1)}, u32[]{:S(2)}, u32[]{:S(2)}) collective-permute-start(bf16[2112,128]{1,0:T(8,128)(2,1)S(1)} %new_rows.6.refs_0_), channel_id=1, source_target_pairs={{24,0},{16,8},{8,16},{0,24},{25,1},{17,9},{9,17},{1,25},{26,2},{18... | collective-permute-start | bytes 1622024 | tf_op jit(solution)/shard_map/ppermute | solution.py:458
  144.8 14.3 %new_rows.8 = (bf16[1056,128]{1,0:T(8,128)(2,1)S(1)}, f32[32768,128]{1,0:T(8,128)}, f32[256,128]{1,0:T(8,128)}) custom-call(s32[5,4]{1,0:T(8,128)S(1)} %multiply_add_fusion.refs_0_.table_ref, bf16[8192,128]{1,0:T(8,128)(2,1)} %all-gather.2.cloned.1.call-done.refs_1_, ...), custom_call_target="tpu_custom_call", output_to_operand_aliasing={{1}: (11, {}), {2}: (12, {})} | custom-call | flops 805306368 | bytes 327680 | tf_op jit(solution)/shard_map/new_rows/pallas_call | solution.py:382
  159.1 0.6 collective-permute-start.12
  159.6 0.8 collective-permute-start.13
  160.5 2.2 %collective-permute-start.14 = (bf16[1056,128]{1,0:T(8,128)(2,1)S(1)}, bf16[1056,128]{1,0:T(8,128)(2,1)S(1)}, u32[]{:S(2)}, u32[]{:S(2)}) collective-permute-start(bf16[1056,128]{1,0:T(8,128)(2,1)S(1)} %get-tuple-element.19.refs_4_), channel_id=1, source_target_pairs={{24,0},{16,8},{8,16},{0,24},{25,1},{17,9},{9,17},{1,25},{26,2},{18... | collective-permute-start | bytes 811016 | tf_op jit(solution)/shard_map/ppermute | solution.py:458
  162.6 14.3 %new_rows.9 = (bf16[1056,128]{1,0:T(8,128)(2,1)S(1)}, f32[32768,128]{1,0:T(8,128)}, f32[256,128]{1,0:T(8,128)}) custom-call(s32[5,4]{1,0:T(8,128)S(1)} %multiply_add_fusion.refs_0_.table_ref, bf16[8192,128]{1,0:T(8,128)(2,1)} %all-gather.2.cloned.1.call-done.refs_1_, ...), custom_call_target="tpu_custom_call", output_to_operand_aliasing={{1}: (9, {}), {2}: (10, {})} | custom-call | flops 805306368 | bytes 327680 | tf_op jit(solution)/shard_map/new_rows/pallas_call | solution.py:382
  177.0 0.5 collective-permute-start.7
  177.5 0.8 collective-permute-start.8
  178.4 2.2 %collective-permute-start.9 = (bf16[1056,128]{1,0:T(8,128)(2,1)S(1)}, bf16[1056,128]{1,0:T(8,128)(2,1)S(1)}, u32[]{:S(2)}, u32[]{:S(2)}) collective-permute-start(bf16[1056,128]{1,0:T(8,128)(2,1)S(1)} %get-tuple-element.18.refs_0_), channel_id=1, source_target_pairs={{24,0},{16,8},{8,16},{0,24},{25,1},{17,9},{9,17},{1,25},{26,2},{18... | collective-permute-start | bytes 811016 | tf_op jit(solution)/shard_map/ppermute | solution.py:458
  180.6 4.4 %placed_rows.2 = (f32[32768,128]{1,0:T(8,128)}, f32[256,128]{1,0:T(8,128)}) custom-call(s32[5,4]{1,0:T(8,128)S(1)} %multiply_add_fusion.refs_0_.table_ref, bf16[2112,128]{1,0:T(8,128)(2,1)S(1)} %new_rows.6.refs_0_, bf16[2112,128]{1,0:T(8,128)(2,1)S(1)} %collective-permute-done.3.refs_4_.refs_1_, ...), custom_call_target="tpu_custom_call", output_to_operand_aliasing={{0}: (9, {}), {1}: (10, {})} | custom-call | tf_op jit(solution)/shard_map/placed_rows/pallas_call | solution.py:428
  185.0 1.1 collective-permute-done.7.refs_1_
  186.1 5.4 %collective-permute-done.8.refs_2_ = bf16[1056,128]{1,0:T(8,128)(2,1)S(1)} collective-permute-done((bf16[1056,128]{1,0:T(8,128)(2,1)S(1)}, bf16[1056,128]{1,0:T(8,128)(2,1)S(1)}, u32[]{:S(2)}, u32[]{:S(2)}) %collective-permute-start.8) | collective-permute-done | bytes 270368 | tf_op jit(solution)/shard_map/ppermute | solution.py:458
  191.4 2.4 %placed_rows.3 = (f32[32768,128]{1,0:T(8,128)}, f32[256,128]{1,0:T(8,128)}) custom-call(s32[5,4]{1,0:T(8,128)S(1)} %multiply_add_fusion.refs_0_.table_ref, bf16[1056,128]{1,0:T(8,128)(2,1)S(1)} %get-tuple-element.18.refs_0_, bf16[1056,128]{1,0:T(8,128)(2,1)S(1)} %collective-permute-done.7.refs_1_, ...), custom_call_target="tpu_custom_call", output_to_operand_aliasing={{0}: (5, {}), {1}: (6, {})} | custom-call | tf_op jit(solution)/shard_map/placed_rows/pallas_call | solution.py:428
  (29 shorter events, 0.1 us)
Async XLA Ops:
  7.2 64.6 %all-gather.2.cloned.1.call-start = ((), (), s32[]{:S(2)}) async-start(), calls=%async_computation.1 | async-start | bytes 2621440 | tf_op jit(solution)/shard_map/all_gather | solution.py:480
  7.9 53.6 %copy-start.5 = (s32[5]{0:T(128)S(1)}, s32[5]{0:T(128)}, u32[]{:S(2)}) copy-start(s32[5]{0:T(128)} %constant.17) | copy-start | bytes 64
  7.9 53.6 %copy-start.6 = (s32[5]{0:T(128)S(1)}, s32[5]{0:T(128)}, u32[]{:S(2)}) copy-start(s32[5]{0:T(128)} %constant.18) | copy-start | bytes 64
  57.4 14.3 %all-to-all-start = ((f32[32,1,2048]{2,1,0:T(1,128)}), f32[32,1,2048]{2,1,0:T(1,128)S(1)}, u32[]{:S(2)}, u32[]{:S(2)}) async-start(f32[32,1,2048]{2,1,0:T(1,128)} %row_stats.1), calls=%async_computation | async-start | bytes 524288 | tf_op jit(solution)/shard_map/all_to_all | solution.py:482
  92.3 28.2 %copy-start.4 = (bf16[2112,128]{1,0:T(8,128)(2,1)}, bf16[2112,128]{1,0:T(8,128)(2,1)S(1)}, u32[]{:S(2)}) copy-start(bf16[2112,128]{1,0:T(8,128)(2,1)S(1)} %get-tuple-element.15.refs_7_) | copy-start | bytes 1622020
  92.3 26.0 %collective-permute-start = (bf16[2112,128]{1,0:T(8,128)(2,1)S(1)}, bf16[2112,128]{1,0:T(8,128)(2,1)S(1)}, u32[]{:S(2)}, u32[]{:S(2)}) collective-permute-start(bf16[2112,128]{1,0:T(8,128)(2,1)S(1)} %get-tuple-element.15.refs_7_), channel_id=1, source_target_pairs={{8,0},{0,8},{24,16},{16,24},{9,1},{1,9},{25,17},{17,25},{10,2},{2,... | collective-permute-start | bytes 1622024 | tf_op jit(solution)/shard_map/ppermute | solution.py:458
  92.9 27.6 %collective-permute-start.1 = (bf16[2112,128]{1,0:T(8,128)(2,1)S(1)}, bf16[2112,128]{1,0:T(8,128)(2,1)S(1)}, u32[]{:S(2)}, u32[]{:S(2)}) collective-permute-start(bf16[2112,128]{1,0:T(8,128)(2,1)S(1)} %get-tuple-element.15.refs_7_), channel_id=1, source_target_pairs={{16,0},{24,8},{0,16},{8,24},{17,1},{25,9},{1,17},{9,25},{18,2},{26... | collective-permute-start | bytes 1622024 | tf_op jit(solution)/shard_map/ppermute | solution.py:458
  93.7 26.8 %collective-permute-start.2 = (bf16[2112,128]{1,0:T(8,128)(2,1)S(1)}, bf16[2112,128]{1,0:T(8,128)(2,1)S(1)}, u32[]{:S(2)}, u32[]{:S(2)}) collective-permute-start(bf16[2112,128]{1,0:T(8,128)(2,1)S(1)} %get-tuple-element.15.refs_7_), channel_id=1, source_target_pairs={{24,0},{16,8},{8,16},{0,24},{25,1},{17,9},{9,17},{1,25},{26,2},{18... | collective-permute-start | bytes 1622024 | tf_op jit(solution)/shard_map/ppermute | solution.py:458
  116.9 42.2 %copy-start = (bf16[2112,128]{1,0:T(8,128)(2,1)}, bf16[2112,128]{1,0:T(8,128)(2,1)S(1)}, u32[]{:S(2)}) copy-start(bf16[2112,128]{1,0:T(8,128)(2,1)S(1)} %new_rows.7.refs_5_) | copy-start | bytes 1622020
  116.9 25.6 %collective-permute-start.4 = (bf16[2112,128]{1,0:T(8,128)(2,1)S(1)}, bf16[2112,128]{1,0:T(8,128)(2,1)}, u32[]{:S(2)}, u32[]{:S(2)}) collective-permute-start(bf16[2112,128]{1,0:T(8,128)(2,1)S(1)} %new_rows.7.refs_5_), channel_id=1, source_target_pairs={{8,0},{0,8},{24,16},{16,24},{9,1},{1,9},{25,17},{17,25},{10,2},{2,... | collective-permute-start | bytes 1622024 | tf_op jit(solution)/shard_map/ppermute | solution.py:458
  117.5 27.3 %collective-permute-start.5 = (bf16[2112,128]{1,0:T(8,128)(2,1)S(1)}, bf16[2112,128]{1,0:T(8,128)(2,1)}, u32[]{:S(2)}, u32[]{:S(2)}) collective-permute-start(bf16[2112,128]{1,0:T(8,128)(2,1)S(1)} %new_rows.7.refs_5_), channel_id=1, source_target_pairs={{16,0},{24,8},{0,16},{8,24},{17,1},{25,9},{1,17},{9,25},{18,2},{26... | collective-permute-start | bytes 1622024 | tf_op jit(solution)/shard_map/ppermute | solution.py:458
  118.3 26.4 %copy-start.1 = (bf16[2112,128]{1,0:T(8,128)(2,1)}, bf16[2112,128]{1,0:T(8,128)(2,1)S(1)}, u32[]{:S(2)}) copy-start(bf16[2112,128]{1,0:T(8,128)(2,1)S(1)} %collective-permute-done.refs_4_.refs_8_) | copy-start | bytes 1622020
  118.3 26.4 %collective-permute-start.6 = (bf16[2112,128]{1,0:T(8,128)(2,1)S(1)}, bf16[2112,128]{1,0:T(8,128)(2,1)}, u32[]{:S(2)}, u32[]{:S(2)}) collective-permute-start(bf16[2112,128]{1,0:T(8,128)(2,1)S(1)} %new_rows.7.refs_5_), channel_id=1, source_target_pairs={{24,0},{16,8},{8,16},{0,24},{25,1},{17,9},{9,17},{1,25},{26,2},{18... | collective-permute-start | bytes 1622024 | tf_op jit(solution)/shard_map/ppermute | solution.py:458
  120.5 24.3 %copy-start.2 = (bf16[2112,128]{1,0:T(8,128)(2,1)}, bf16[2112,128]{1,0:T(8,128)(2,1)S(1)}, u32[]{:S(2)}) copy-start(bf16[2112,128]{1,0:T(8,128)(2,1)S(1)} %collective-permute-done.1.refs_5_.refs_9_) | copy-start | bytes 1622020
  120.5 24.3 %copy-start.3 = (bf16[2112,128]{1,0:T(8,128)(2,1)}, bf16[2112,128]{1,0:T(8,128)(2,1)S(1)}, u32[]{:S(2)}) copy-start(bf16[2112,128]{1,0:T(8,128)(2,1)S(1)} %collective-permute-done.2.refs_6_.refs_10_) | copy-start | bytes 1622020
  141.2 19.3 %collective-permute-start.3 = (bf16[2112,128]{1,0:T(8,128)(2,1)S(1)}, bf16[2112,128]{1,0:T(8,128)(2,1)S(1)}, u32[]{:S(2)}, u32[]{:S(2)}) collective-permute-start(bf16[2112,128]{1,0:T(8,128)(2,1)S(1)} %new_rows.6.refs_0_), channel_id=1, source_target_pairs={{8,0},{0,8},{24,16},{16,24},{9,1},{1,9},{25,17},{17,25},{10,2},{2,... | collective-permute-start | bytes 1622024 | tf_op jit(solution)/shard_map/ppermute | solution.py:458
  141.7 38.8 %collective-permute-start.10 = (bf16[2112,128]{1,0:T(8,128)(2,1)S(1)}, bf16[2112,128]{1,0:T(8,128)(2,1)S(1)}, u32[]{:S(2)}, u32[]{:S(2)}) collective-permute-start(bf16[2112,128]{1,0:T(8,128)(2,1)S(1)} %new_rows.6.refs_0_), channel_id=1, source_target_pairs={{16,0},{24,8},{0,16},{8,24},{17,1},{25,9},{1,17},{9,25},{18,2},{26... | collective-permute-start | bytes 1622024 | tf_op jit(solution)/shard_map/ppermute | solution.py:458
  142.6 38.0 %collective-permute-start.11 = (bf16[2112,128]{1,0:T(8,128)(2,1)S(1)}, bf16[2112,128]{1,0:T(8,128)(2,1)S(1)}, u32[]{:S(2)}, u32[]{:S(2)}) collective-permute-start(bf16[2112,128]{1,0:T(8,128)(2,1)S(1)} %new_rows.6.refs_0_), channel_id=1, source_target_pairs={{24,0},{16,8},{8,16},{0,24},{25,1},{17,9},{9,17},{1,25},{26,2},{18... | collective-permute-start | bytes 1622024 | tf_op jit(solution)/shard_map/ppermute | solution.py:458
  159.1 17.9 %collective-permute-start.12 = (bf16[1056,128]{1,0:T(8,128)(2,1)S(1)}, bf16[1056,128]{1,0:T(8,128)(2,1)S(1)}, u32[]{:S(2)}, u32[]{:S(2)}) collective-permute-start(bf16[1056,128]{1,0:T(8,128)(2,1)S(1)} %get-tuple-element.19.refs_4_), channel_id=1, source_target_pairs={{8,0},{0,8},{24,16},{16,24},{9,1},{1,9},{25,17},{17,25},{10,2},{2,... | collective-permute-start | bytes 811016 | tf_op jit(solution)/shard_map/ppermute | solution.py:458
  159.6 17.9 %collective-permute-start.13 = (bf16[1056,128]{1,0:T(8,128)(2,1)S(1)}, bf16[1056,128]{1,0:T(8,128)(2,1)S(1)}, u32[]{:S(2)}, u32[]{:S(2)}) collective-permute-start(bf16[1056,128]{1,0:T(8,128)(2,1)S(1)} %get-tuple-element.19.refs_4_), channel_id=1, source_target_pairs={{16,0},{24,8},{0,16},{8,24},{17,1},{25,9},{1,17},{9,25},{18,2},{26... | collective-permute-start | bytes 811016 | tf_op jit(solution)/shard_map/ppermute | solution.py:458
  160.5 17.9 %collective-permute-start.14 = (bf16[1056,128]{1,0:T(8,128)(2,1)S(1)}, bf16[1056,128]{1,0:T(8,128)(2,1)S(1)}, u32[]{:S(2)}, u32[]{:S(2)}) collective-permute-start(bf16[1056,128]{1,0:T(8,128)(2,1)S(1)} %get-tuple-element.19.refs_4_), channel_id=1, source_target_pairs={{24,0},{16,8},{8,16},{0,24},{25,1},{17,9},{9,17},{1,25},{26,2},{18... | collective-permute-start | bytes 811016 | tf_op jit(solution)/shard_map/ppermute | solution.py:458
  177.0 9.1 %collective-permute-start.7 = (bf16[1056,128]{1,0:T(8,128)(2,1)S(1)}, bf16[1056,128]{1,0:T(8,128)(2,1)S(1)}, u32[]{:S(2)}, u32[]{:S(2)}) collective-permute-start(bf16[1056,128]{1,0:T(8,128)(2,1)S(1)} %get-tuple-element.18.refs_0_), channel_id=1, source_target_pairs={{8,0},{0,8},{24,16},{16,24},{9,1},{1,9},{25,17},{17,25},{10,2},{2,... | collective-permute-start | bytes 811016 | tf_op jit(solution)/shard_map/ppermute | solution.py:458
  177.5 13.9 %collective-permute-start.8 = (bf16[1056,128]{1,0:T(8,128)(2,1)S(1)}, bf16[1056,128]{1,0:T(8,128)(2,1)S(1)}, u32[]{:S(2)}, u32[]{:S(2)}) collective-permute-start(bf16[1056,128]{1,0:T(8,128)(2,1)S(1)} %get-tuple-element.18.refs_0_), channel_id=1, source_target_pairs={{16,0},{24,8},{0,16},{8,24},{17,1},{25,9},{1,17},{9,25},{18,2},{26... | collective-permute-start | bytes 811016 | tf_op jit(solution)/shard_map/ppermute | solution.py:458
  178.4 13.1 %collective-permute-start.9 = (bf16[1056,128]{1,0:T(8,128)(2,1)S(1)}, bf16[1056,128]{1,0:T(8,128)(2,1)S(1)}, u32[]{:S(2)}, u32[]{:S(2)}) collective-permute-start(bf16[1056,128]{1,0:T(8,128)(2,1)S(1)} %get-tuple-element.18.refs_0_), channel_id=1, source_target_pairs={{24,0},{16,8},{8,16},{0,24},{25,1},{17,9},{9,17},{1,25},{26,2},{18... | collective-permute-start | bytes 811016 | tf_op jit(solution)/shard_map/ppermute | solution.py:458
Sparse Core Ops, SparseCore 0:
  9.8 38.0 all-gather.1
